TPU v7x, 32 devices: a whole 2x2x4 slice. The times are simulated.
32 devices in a mesh: rep: 4 (over y, x), shard: 8 (over z, core).
Axes of the slice: x: 2, y: 2, z: 4, core: 2. Of those that a mesh axis runs over, the one named last changes fastest.
Arguments:
- inputs: bfloat16 [32, 256, 1024], P(('rep', 'shard')), may hold values from -6 to 6
- cotangent: bfloat16 [32, 256, 1024], P(('rep', 'shard')), may hold values from -6 to 6
- seq_lengths: int32 [32], replicated, may hold values from 1 to 256, 5120 in all
- dealing: int32 [32], replicated, may hold values from 0 to 31, as said below
- rel_buckets: int32 [511], replicated, may hold values from 0 to 31
- w_query: bfloat16 [1024, 1024], P('shard'), may hold values from -0.09375 to 0.09375
- w_key: bfloat16 [1024, 1024], P('shard'), may hold values from -0.09375 to 0.09375
- w_value: bfloat16 [1024, 1024], P('shard'), may hold values from -0.1875 to 0.1875
- w_mixer: bfloat16 [1024, 1024], P('shard'), may hold values from -1 to 1
- w_inner: bfloat16 [1024, 4096], P('shard'), may hold values from -0.1875 to 0.1875
- w_outer: bfloat16 [4096, 1024], P('shard'), may hold values from -0.09375 to 0.09375
- gain_attn: bfloat16 [1024], P('shard'), may hold values from 0.5 to 1.5
- gain_mlp: bfloat16 [1024], P('shard'), may hold values from 0.5 to 1.5
- bias_table: bfloat16 [32, 16], P('shard'), may hold values from -6 to 6
Outputs:
- layer_out: bfloat16 [32, 256, 1024], P(('rep', 'shard'))
- input_grad: bfloat16 [32, 256, 1024], P(('rep', 'shard'))
- grad_query: float32 [1024, 1024], P('shard')
- grad_key: float32 [1024, 1024], P('shard')
- grad_value: float32 [1024, 1024], P('shard')
- grad_mixer: float32 [1024, 1024], P('shard')
- grad_inner: float32 [1024, 4096], P('shard')
- grad_outer: float32 [4096, 1024], P('shard')
- grad_gain_attn: float32 [1024], P('shard')
- grad_gain_mlp: float32 [1024], P('shard')
- grad_table: float32 [32, 16], P('shard')
Inputs may be any that keep to these rules, and one draw needn't show every extreme that they name: A permutation: slot s processes sequence dealing[s]; at least one slot s processes sequence (s + 16) % 32, which slot drawn from the seed. `seq_lengths`: valid tokens stand at the start of each sequence; all lengths sum to 5120 and the longest is exactly 256. `rel_buckets`: entry j - i + 255 is the bucket of key position j seen from query position i.
All inputs are finite; a program needn't handle non-finite values.
Results may differ from a plain program's by a relative error of at most 0.015.
Values may be sent and summed in bfloat16 or wider, within the bound.
No kernel may reach another device: no remote copies, remote signals or barrier semaphores. Data moves between devices by JAX's collectives and lax.ppermute only.
A program may use at most 320 MiB of HBM per device.

v0:
```python
import jax
import jax.numpy as jnp
from jax import lax
from jax.sharding import PartitionSpec as P

EPSILON = 1e-06
MASKED = -1000000000.0
HIGHEST = lax.Precision.HIGHEST


def norm_apply(hidden, gain):
    return hidden * lax.rsqrt(jnp.mean(hidden * hidden, axis=-1, keepdims=True) + EPSILON) * gain


def pick_piece(running, portion, offset, wanted):
    portion_rows = portion.shape[0]
    local_row = jnp.clip(wanted, 0, portion_rows - 1)
    chosen = lax.dynamic_slice_in_dim(portion, local_row, 1, 0)
    inside = (wanted >= offset) & (wanted < offset + portion_rows)
    return jnp.where(inside, chosen, running)


def toeplitz_bias(offset_vals, seq_len):
    span = 2 * seq_len - 1
    rolled = jnp.roll(offset_vals, -(seq_len - 1), axis=0).T
    tiled = jnp.tile(rolled, (1, seq_len))
    skewed = tiled[:, : seq_len * (span - 1)].reshape(rolled.shape[0], seq_len, span - 1)
    return skewed[:, :, :seq_len]


def diagonal_sums(grad_block, row_start, seq_len):
    span = 2 * seq_len - 1
    heads, rows = (grad_block.shape[0], grad_block.shape[1])
    widened = jnp.pad(grad_block.astype(jnp.float32), ((0, 0), (0, 0), (0, seq_len - 2)))
    flat = widened.reshape(heads, rows * (span - 1))
    flat = jnp.pad(flat, ((0, 0), (0, rows)))
    sums = jnp.sum(flat.reshape(heads, rows, span), axis=1)
    return jnp.roll(sums, seq_len - 1 - row_start, axis=1).T


def block_scores(query_block, keys_all, bias, valid_keys):
    scores = (
        jnp.einsum("ihd,jhd->hij", query_block, keys_all, preferred_element_type=jnp.float32) + bias
    )
    return jnp.where(valid_keys[None, None, :], scores, MASKED)


def local(
    inputs,
    cotangent,
    seq_lengths,
    dealing,
    rel_buckets,
    w_query,
    w_key,
    w_value,
    w_mixer,
    w_inner,
    w_outer,
    gain_attn,
    gain_mlp,
    bias_table,
):
    device = lax.axis_index(("rep", "shard"))
    inverse = jnp.argsort(dealing)
    source = dealing[device]
    length = seq_lengths[source]
    local_in = pick_piece(
        jnp.zeros_like(inputs),
        lax.all_gather(inputs, ("rep", "shard"), axis=0, tiled=True),
        jnp.int32(0),
        source,
    )
    seq_len = local_in.shape[1]
    width = local_in.shape[2]
    heads = bias_table.shape[1]
    head_size = width // heads
    block_rows = min(512, seq_len)
    hidden = local_in[0].astype(jnp.float32)
    valid_keys = jnp.arange(seq_len, dtype=jnp.int32) < length
    row_mask = valid_keys[:, None].astype(jnp.float32)
    wq_full, wk_full, wv_full, wo_full, gain_a, table = (
        lax.all_gather(w_query, "shard", axis=0, tiled=True),
        lax.all_gather(w_key, "shard", axis=0, tiled=True),
        lax.all_gather(w_value, "shard", axis=0, tiled=True),
        lax.all_gather(w_mixer, "shard", axis=0, tiled=True),
        lax.all_gather(gain_attn, "shard", axis=0, tiled=True),
        lax.all_gather(bias_table, "shard", axis=0, tiled=True),
    )
    bucket_onehot = (
        rel_buckets[:, None] == jnp.arange(table.shape[0], dtype=jnp.int32)[None, :]
    ).astype(jnp.float32)
    offset_vals = jnp.dot(bucket_onehot, table.astype(jnp.float32), precision=HIGHEST)
    bias_full = toeplitz_bias(offset_vals, seq_len)
    gain_first = gain_a.astype(jnp.float32)
    normed = norm_apply(hidden, gain_first).astype(jnp.bfloat16)
    queries = (
        jnp.dot(normed, wq_full, preferred_element_type=jnp.float32)
        .astype(jnp.bfloat16)
        .reshape(seq_len, heads, head_size)
    )
    keys_all = (
        jnp.dot(normed, wk_full, preferred_element_type=jnp.float32)
        .astype(jnp.bfloat16)
        .reshape(seq_len, heads, head_size)
    )
    values_all = (
        jnp.dot(normed, wv_full, preferred_element_type=jnp.float32)
        .astype(jnp.bfloat16)
        .reshape(seq_len, heads, head_size)
    )
    row_start = 0
    bias = bias_full
    scores = block_scores(queries, keys_all, bias, valid_keys)
    row_peak = jnp.max(scores, axis=-1, keepdims=True)
    exponent = jnp.exp(scores - row_peak)
    row_total = jnp.sum(exponent, axis=-1, keepdims=True)
    attn_probs = exponent / row_total
    lse_blocks = [row_peak + jnp.log(row_total)]
    mixed_blocks = jnp.einsum(
        "hij,jhd->ihd",
        attn_probs.astype(jnp.bfloat16),
        values_all,
        preferred_element_type=jnp.float32,
    ).astype(jnp.bfloat16)
    mixed = mixed_blocks.reshape(seq_len, width)
    middle = hidden + jnp.dot(mixed, wo_full, preferred_element_type=jnp.float32)
    wi_full, wu_full, gain_m = (
        lax.all_gather(w_inner, "shard", axis=0, tiled=True),
        lax.all_gather(w_outer, "shard", axis=0, tiled=True),
        lax.all_gather(gain_mlp, "shard", axis=0, tiled=True),
    )
    gain_second = gain_m.astype(jnp.float32)
    normed2 = norm_apply(middle, gain_second).astype(jnp.bfloat16)
    inner = jnp.dot(normed2, wi_full, preferred_element_type=jnp.float32)
    gelu_exact = lambda value: jax.nn.gelu(value, approximate=False)
    active_f, gelu_back = jax.vjp(gelu_exact, inner)
    active = active_f.astype(jnp.bfloat16)
    outer = jnp.dot(active, wu_full, preferred_element_type=jnp.float32)
    layer_out = ((middle + outer) * row_mask).astype(jnp.bfloat16)[None]
    grad_final = cotangent[0].astype(jnp.float32) * row_mask
    grad_low = grad_final.astype(jnp.bfloat16)
    grad_active = jnp.einsum("id,fd->if", grad_low, wu_full, preferred_element_type=jnp.float32)
    grad_wout = jnp.einsum("if,id->fd", active, grad_low, preferred_element_type=jnp.float32)
    grad_act_in = gelu_back(grad_active)[0].astype(jnp.bfloat16)
    grad_win = jnp.einsum("id,if->df", normed2, grad_act_in, preferred_element_type=jnp.float32)
    grad_normed2 = jnp.einsum("if,df->id", grad_act_in, wi_full, preferred_element_type=jnp.float32)
    second_norm, second_back = jax.vjp(norm_apply, middle, gain_second)
    grad_mid_part, grad_gm = second_back(grad_normed2)
    grad_middle = grad_final + grad_mid_part
    grad_att = grad_middle.astype(jnp.bfloat16)
    grad_wo = jnp.einsum("id,ie->de", mixed, grad_att, preferred_element_type=jnp.float32)
    grad_mixed = (
        jnp.einsum("ie,de->id", grad_att, wo_full, preferred_element_type=jnp.float32)
        .astype(jnp.bfloat16)
        .reshape(seq_len, heads, head_size)
    )
    grad_keys_acc = jnp.zeros((seq_len, heads, head_size), jnp.float32)
    grad_values_acc = jnp.zeros((seq_len, heads, head_size), jnp.float32)
    grad_offsets = jnp.zeros(offset_vals.shape, jnp.float32)
    query_grad_blocks = []
    for block_number, row_start in enumerate(range(0, seq_len, block_rows)):
        bias = bias_full
        scores = block_scores(queries, keys_all, bias, valid_keys)
        attn_probs = jnp.exp(scores - lse_blocks[block_number])
        grad_probs = jnp.einsum(
            "ihd,jhd->hij", grad_mixed, values_all, preferred_element_type=jnp.float32
        )
        row_delta = jnp.sum(attn_probs * grad_probs, axis=-1, keepdims=True)
        grad_scores = (attn_probs * (grad_probs - row_delta)).astype(jnp.bfloat16)
        query_grad_blocks.append(
            jnp.einsum("hij,jhd->ihd", grad_scores, keys_all, preferred_element_type=jnp.float32)
        )
        grad_keys_acc = jnp.einsum(
            "hij,ihd->jhd", grad_scores, queries, preferred_element_type=jnp.float32
        )
        grad_values_acc = jnp.einsum(
            "hij,ihd->jhd",
            attn_probs.astype(jnp.bfloat16),
            grad_mixed,
            preferred_element_type=jnp.float32,
        )
        grad_offsets = diagonal_sums(grad_scores, row_start, seq_len)
    grad_tab = jnp.dot(bucket_onehot.T, grad_offsets, precision=HIGHEST)
    grad_queries = query_grad_blocks[0].astype(jnp.bfloat16).reshape(seq_len, width)
    grad_keys = grad_keys_acc.astype(jnp.bfloat16).reshape(seq_len, width)
    grad_values = grad_values_acc.astype(jnp.bfloat16).reshape(seq_len, width)
    grad_wq = jnp.einsum("id,ie->de", normed, grad_queries, preferred_element_type=jnp.float32)
    grad_wk = jnp.einsum("id,ie->de", normed, grad_keys, preferred_element_type=jnp.float32)
    grad_wv = jnp.einsum("id,ie->de", normed, grad_values, preferred_element_type=jnp.float32)
    grad_normed = jnp.einsum("ie,de->id", grad_queries, wq_full, preferred_element_type=jnp.float32)
    grad_normed = grad_normed + jnp.einsum(
        "ie,de->id", grad_keys, wk_full, preferred_element_type=jnp.float32
    )
    grad_normed = grad_normed + jnp.einsum(
        "ie,de->id", grad_values, wv_full, preferred_element_type=jnp.float32
    )
    first_norm, first_back = jax.vjp(norm_apply, hidden, gain_first)
    grad_hidden_part, grad_ga = first_back(grad_normed)
    grad_local = (grad_middle + grad_hidden_part).astype(jnp.bfloat16)[None]
    part_q, part_k, part_v, part_o, part_ga, part_tab = (
        lax.psum_scatter(grad_wq, "shard", scatter_dimension=0, tiled=True),
        lax.psum_scatter(grad_wk, "shard", scatter_dimension=0, tiled=True),
        lax.psum_scatter(grad_wv, "shard", scatter_dimension=0, tiled=True),
        lax.psum_scatter(grad_wo, "shard", scatter_dimension=0, tiled=True),
        lax.psum_scatter(grad_ga, "shard", scatter_dimension=0, tiled=True),
        lax.psum_scatter(grad_tab, "shard", scatter_dimension=0, tiled=True),
    )
    part_in, part_out, part_gm = (
        lax.psum_scatter(
            grad_win.astype(jnp.bfloat16), "shard", scatter_dimension=0, tiled=True
        ).astype(jnp.float32),
        lax.psum_scatter(
            grad_wout.astype(jnp.bfloat16), "shard", scatter_dimension=0, tiled=True
        ).astype(jnp.float32),
        lax.psum_scatter(
            grad_gm.astype(jnp.bfloat16), "shard", scatter_dimension=0, tiled=True
        ).astype(jnp.float32),
    )
    sum_q, sum_k, sum_v, sum_o, sum_in, sum_out, sum_ga, sum_gm, sum_tab = lax.psum(
        (part_q, part_k, part_v, part_o, part_in, part_out, part_ga, part_gm, part_tab), "rep"
    )
    wanted_slot = inverse[device]
    input_grad = pick_piece(
        jnp.zeros_like(grad_local),
        lax.all_gather(grad_local, ("rep", "shard"), axis=0, tiled=True),
        jnp.int32(0),
        wanted_slot,
    )
    return (
        layer_out,
        input_grad,
        sum_q,
        sum_k,
        sum_v,
        sum_o,
        sum_in,
        sum_out,
        sum_ga,
        sum_gm,
        sum_tab,
    )


def solution(mesh):
    in_specs = (
        P(("rep", "shard"), None, None),
        P(("rep", "shard"), None, None),
        P(),
        P(),
        P(),
        P("shard", None),
        P("shard", None),
        P("shard", None),
        P("shard", None),
        P("shard", None),
        P("shard", None),
        P("shard"),
        P("shard"),
        P("shard", None),
    )
    out_specs = (
        P(("rep", "shard"), None, None),
        P(("rep", "shard"), None, None),
        P("shard", None),
        P("shard", None),
        P("shard", None),
        P("shard", None),
        P("shard", None),
        P("shard", None),
        P("shard"),
        P("shard"),
        P("shard", None),
    )
    return jax.shard_map(local, mesh=mesh, in_specs=in_specs, out_specs=out_specs, check_vma=False)
```

profile of v0, /device:TPU:0, one launch (start us, length us, event | category | flops | bytes accessed | tf_op | source)
XLA Modules:
  0.0 1072.9 jit_solution(8959720015859187505)
XLA Ops:
  16.4 13.7 %all-gather.2 = bf16[8,4,16]{2,1,0:T(4,128)(2,1)S(1)} all-gather(bf16[1,4,16]{2,1,0:T(4,128)(2,1)} %bitcast.143), channel_id=1, replica_groups=mesh['rep'=4,'shard'=8] {'shard'}, dimensions={0}, use_global_device_ids=true | all-gather | bytes 1152 | tf_op jit(solution)/shard_map/all_gather | solution.py:88
  31.1 8.8 all-gather.1
  40.0 10.3 all-gather.3
  50.3 4.3 tile.4
  54.6 8.5 tile.10
  63.1 7.1 slice.30
  70.2 12.1 %reshape.180 = f32[16,256,510]{2,1,0:T(8,128)} reshape(f32[16,130560]{1,0:T(8,128)} %slice.30) | data formatting | bytes 16711680 | tf_op jit(solution)/shard_map/reshape | solution.py:27
  82.3 4.6 slice.31
  86.9 5.9 copy.61
  95.3 33.4 %all-gather.13.cloned.1.call-done = bf16[32,256,1024]{2,1,0:T(8,128)(2,1)} async-done(((bf16[1,256,1024]{2,1,0:T(8,128)(2,1)}), bf16[32,256,1024]{2,1,0:T(8,128)(2,1)}) %all-gather.13.cloned.1.call-update) | async-done | bytes 16777232 | tf_op jit(solution)/shard_map/all_gather | solution.py:70
  129.9 27.6 %all-gather.17.cloned.1.call-done = bf16[1024,1024]{1,0:T(8,128)(2,1)} async-done(((bf16[128,1024]{1,0:T(8,128)(2,1)}), bf16[1024,1024]{1,0:T(8,128)(2,1)}) %all-gather.17.cloned.1.call-update) | async-done | bytes 2097168 | tf_op jit(solution)/shard_map/all_gather | solution.py:83
  157.6 2.5 convolution_convert_fusion.6
  160.3 27.5 %all-gather.19.cloned.1.call-done = bf16[1024,1024]{1,0:T(8,128)(2,1)} async-done(((bf16[128,1024]{1,0:T(8,128)(2,1)}), bf16[1024,1024]{1,0:T(8,128)(2,1)}) %all-gather.19.cloned.1.call-update) | async-done | bytes 2097168 | tf_op jit(solution)/shard_map/all_gather | solution.py:84
  187.8 2.5 convolution_convert_fusion.5
  190.6 27.3 %all-gather.15.cloned.1.call-done = bf16[1024,1024]{1,0:T(8,128)(2,1)} async-done(((bf16[128,1024]{1,0:T(8,128)(2,1)}), bf16[1024,1024]{1,0:T(8,128)(2,1)}) %all-gather.15.cloned.1.call-update) | async-done | bytes 2097168 | tf_op jit(solution)/shard_map/all_gather | solution.py:85
  217.9 2.5 convolution_convert_fusion.7
  220.7 3.4 fusion.68
  227.0 21.0 %all-gather.21.cloned.1.call-done = bf16[1024,1024]{1,0:T(8,128)(2,1)} async-done(((bf16[128,1024]{1,0:T(8,128)(2,1)}), bf16[1024,1024]{1,0:T(8,128)(2,1)}) %all-gather.21.cloned.1.call-update) | async-done | bytes 2097168 | tf_op jit(solution)/shard_map/all_gather | solution.py:86
  248.0 2.5 multiply_reduce_fusion.3
  250.5 80.5 %all-gather.23.cloned.1.call-done = bf16[1024,4096]{1,0:T(8,128)(2,1)} async-done(((bf16[128,4096]{1,0:T(8,128)(2,1)}), bf16[1024,4096]{1,0:T(8,128)(2,1)}) %all-gather.23.cloned.1.call-update) | async-done | bytes 8388624 | tf_op jit(solution)/shard_map/all_gather | solution.py:129
  331.0 15.8 %multiply_convert_fusion.1 = (bf16[256,4096]{1,0:T(8,128)(2,1)}, f32[256,4096]{1,0:T(8,128)}, f32[256,4096]{1,0:T(8,128)}) fusion(bf16[1024,4096]{1,0:T(8,128)(2,1)} %all-gather.23.cloned.1.call-done, f32[256,1024]{1,0:T(8,128)S(1)} %get-tuple-element.33, f32[1024]{0:T(1024)S(1)} %bitcast.129, f32[256]{0:T(256)S(1)} %fusion.54), kind=kOutput, calls=%fused_computation.8 | convolution fusion | flops 2216427520 | bytes 19928064 | tf_op jit(solution)/shard_map/dot_general | solution.py:135
  346.8 66.4 %all-gather.25.cloned.1.call-done = bf16[4096,1024]{1,0:T(8,128)(2,1)} async-done(((bf16[512,1024]{1,0:T(8,128)(2,1)}), bf16[4096,1024]{1,0:T(8,128)(2,1)}) %all-gather.25.cloned.1.call-update) | async-done | bytes 8388624 | tf_op jit(solution)/shard_map/all_gather | solution.py:130
  413.2 11.5 %add_convert_fusion = bf16[256,4096]{1,0:T(8,128)(2,1)S(1)} fusion(f32[256,4096]{1,0:T(8,128)} %get-tuple-element.29, f32[256,4096]{1,0:T(8,128)} %get-tuple-element.34, bf16[4096,1024]{1,0:T(8,128)(2,1)} %all-gather.25.cloned.1.call-done, bf16[1,256,1024]{2,1,0:T(8,128)(2,1)S(1)} %copy-done.19, f32[256]{0:T(256)S(1)} %fusion.56), kind=kOutput, calls=%fused_computation.7 | convolution fusion | flops 2162950144 | bytes 19399680 | tf_op jit(solution)/shard_map/id,fd->if/dot_general | solution.py:143
  424.8 2.6 multiply_reduce_fusion.1
  427.8 2.7 fusion.36
  433.3 3.3 fusion.18
  436.6 4.0 fusion.58
  440.8 3.4 multiply_reduce_fusion
  446.6 4.0 fusion.62
  453.5 3.9 fusion.60
  457.4 7.7 convolution_convert_fusion.1
  465.2 7.3 convolution_convert_fusion
  472.6 2.7 fusion.69
  490.2 3.9 pad.10.clone
  494.1 8.8 reshape.186
  503.0 26.7 %reduce-scatter.11.cloned.1.call-done = f32[128,1024]{1,0:T(8,128)} async-done(((f32[1024,1024]{1,0:T(8,128)}), f32[128,1024]{1,0:T(8,128)}) %reduce-scatter.11.cloned.1.call-update) | async-done | bytes 524304 | tf_op jit(solution)/shard_map/reduce_scatter | solution.py:204
  529.7 50.3 %reduce-scatter.7.cloned.1.call-done = f32[128,1024]{1,0:T(8,128)} async-done(((f32[1024,1024]{1,0:T(8,128)}), f32[128,1024]{1,0:T(8,128)}) %reduce-scatter.7.cloned.1.call-update) | async-done | bytes 524304 | tf_op jit(solution)/shard_map/reduce_scatter | solution.py:202
  580.0 50.5 %reduce-scatter.9.cloned.1.call-done = f32[128,1024]{1,0:T(8,128)} async-done(((f32[1024,1024]{1,0:T(8,128)}), f32[128,1024]{1,0:T(8,128)}) %reduce-scatter.9.cloned.1.call-update) | async-done | bytes 524304 | tf_op jit(solution)/shard_map/reduce_scatter | solution.py:203
  630.5 5.9 pad_convert_fusion
  636.4 12.1 %reshape.192 = f32[16,256,511]{2,1,0:T(8,128)} reshape(f32[16,130816]{1,0:T(8,128)} %pad_convert_fusion) | data formatting | bytes 16744448 | tf_op jit(solution)/shard_map/reshape | solution.py:37
  648.5 4.7 reduce_sum.92
  653.6 28.0 %all-reduce.5 = (f32[1024]{0:T(1024)S(1)}, f32[32,16]{1,0:T(8,128)S(1)}) all-reduce(f32[1024]{0:T(1024)S(1)} %get-tuple-element.13, f32[32,16]{1,0:T(8,128)S(1)} %fusion.46), channel_id=9, replica_groups=mesh['rep'=4,'shard'=8] {'shard'}, use_global_device_ids=true, to_apply=%region_21.22.clone | all-reduce | flops 1536 | bytes 12288
  681.7 14.4 %all-reduce.3 = bf16[1024]{0:T(1024)(128)(2,1)S(1)} all-reduce(bf16[1024]{0:T(1024)(128)(2,1)S(1)} %get-tuple-element.15), channel_id=10, replica_groups=mesh['rep'=4,'shard'=8] {'shard'}, use_global_device_ids=true, to_apply=%region_24.25.clone | all-reduce | flops 1024 | bytes 4096
  696.2 6.6 fusion.24
  702.8 18.5 %reduce-scatter.15.cloned.1.call-done = bf16[128,4096]{1,0:T(8,128)(2,1)} async-done(((bf16[1024,4096]{1,0:T(8,128)(2,1)}), bf16[128,4096]{1,0:T(8,128)(2,1)}) %reduce-scatter.15.cloned.1.call-update) | async-done | bytes 1048592 | tf_op jit(solution)/shard_map/reduce_scatter | solution.py:210
  721.3 90.3 %reduce-scatter.17.cloned.1.call-done = bf16[512,1024]{1,0:T(8,128)(2,1)} async-done(((bf16[4096,1024]{1,0:T(8,128)(2,1)}), bf16[512,1024]{1,0:T(8,128)(2,1)}) %reduce-scatter.17.cloned.1.call-update) | async-done | bytes 1048592 | tf_op jit(solution)/shard_map/reduce_scatter | solution.py:213
  811.6 202.4 %all-reduce.12 = (f32[128,4096]{1,0:T(8,128)}, f32[512,1024]{1,0:T(8,128)}, f32[128]{0:T(128)}, f32[128]{0:T(128)}, f32[4,16]{1,0:T(4,128)}) all-reduce(bf16[128,4096]{1,0:T(8,128)(2,1)} %reduce-scatter.15.cloned.1.call-done, bf16[512,1024]{1,0:T(8,128)(2,1)} %reduce-scatter.17.cloned.1.call-done, ...), channel_id=1, replica_groups=mesh['rep'=4,'shard'=8] {'rep'}, use_global_device_ids=true, to_apply=%region_17.18 | all-reduce | flops 1048896 | bytes 6294016 | tf_op jit(solution)/shard_map/psum | solution.py:220
  1015.9 42.5 %all-reduce.11.cloned.1.call-done = (f32[128,1024]{1,0:T(8,128)}, f32[128,1024]{1,0:T(8,128)}, f32[128,1024]{1,0:T(8,128)}, f32[128,1024]{1,0:T(8,128)}) async-done(((f32[128,1024]{1,0:T(8,128)}, f32[128,1024]{1,0:T(8,128)}, f32[128,1024]{1,0:T(8,128)}, f32[128,1024]{1,0:T(8,128)}), (f32[128,1024]{1,0:T(8,128)}, f32[128,1024]{1,0:T(8,128)}, f32[128,1024]{1,0:T(8,128)}, ...) | async-done | bytes 2097168 | tf_op jit(solution)/shard_map/psum | solution.py:220
  (130 shorter events, 43.9 us)
Async XLA Ops:
  7.2 121.5 %all-gather.13.cloned.1.call-start = ((), (), s32[]{:S(2)}) async-start(), calls=%async_computation.6 | async-start | bytes 17301504 | tf_op jit(solution)/shard_map/all_gather | solution.py:70
  7.9 149.7 %all-gather.17.cloned.1.call-start = ((), (), s32[]{:S(2)}) async-start(), calls=%async_computation.8 | async-start | bytes 2359296 | tf_op jit(solution)/shard_map/all_gather | solution.py:83
  8.7 179.2 %all-gather.19.cloned.1.call-start = ((), (), s32[]{:S(2)}) async-start(), calls=%async_computation.9 | async-start | bytes 2359296 | tf_op jit(solution)/shard_map/all_gather | solution.py:84
  9.4 208.5 %all-gather.15.cloned.1.call-start = ((), (), s32[]{:S(2)}) async-start(), calls=%async_computation.7 | async-start | bytes 2359296 | tf_op jit(solution)/shard_map/all_gather | solution.py:85
  10.0 238.0 %all-gather.21.cloned.1.call-start = ((), (), s32[]{:S(2)}) async-start(), calls=%async_computation.10 | async-start | bytes 2359296 | tf_op jit(solution)/shard_map/all_gather | solution.py:86
  10.6 320.5 %all-gather.23.cloned.1.call-start = ((), (), s32[]{:S(2)}) async-start(), calls=%async_computation.11 | async-start | bytes 9437184 | tf_op jit(solution)/shard_map/all_gather | solution.py:129
  11.1 402.1 %all-gather.25.cloned.1.call-start = ((), (), s32[]{:S(2)}) async-start(), calls=%async_computation.12 | async-start | bytes 9437184 | tf_op jit(solution)/shard_map/all_gather | solution.py:130
  11.9 491.1 %reduce-scatter.13.cloned.1.call-start = ((), (), s32[]{:S(2)}) async-start(), calls=%async_computation.16 | async-start | bytes 4718592 | tf_op jit(solution)/shard_map/reduce_scatter | solution.py:205
  86.9 6.5 copy-start.23
  160.3 60.3 %copy-start.5 = (bf16[256,1024]{0,1:T(8,128)(2,1)}, bf16[256,1024]{0,1:T(8,128)(2,1)S(1)}, u32[]{:S(2)}) copy-start(bf16[256,1024]{0,1:T(8,128)(2,1)S(1)} %copy.48) | copy-start | bytes 1572868
  190.6 33.5 %copy-start.6 = (bf16[256,1024]{0,1:T(8,128)(2,1)}, bf16[256,1024]{0,1:T(8,128)(2,1)S(1)}, u32[]{:S(2)}) copy-start(bf16[256,1024]{0,1:T(8,128)(2,1)S(1)} %copy.49) | copy-start | bytes 1572868
  220.6 4.0 copy-start.11
  224.1 2.1 copy-start
  227.0 119.8 %copy-start.17 = (bf16[16,64,256]{2,1,0:T(8,128)(2,1)}, bf16[16,64,256]{2,1,0:T(8,128)(2,1)S(1)}, u32[]{:S(2)}) copy-start(bf16[16,64,256]{2,1,0:T(8,128)(2,1)S(1)} %fusion.21) | copy-start | bytes 1572868
  250.5 177.0 %copy-start.2 = (f32[256,1024]{1,0:T(8,128)}, f32[256,1024]{1,0:T(8,128)S(1)}, u32[]{:S(2)}) copy-start(f32[256,1024]{1,0:T(8,128)S(1)} %get-tuple-element.33) | copy-start | bytes 3145732
  331.0 82.2 %copy-start.19 = (bf16[1,256,1024]{2,1,0:T(8,128)(2,1)S(1)}, bf16[1,256,1024]{2,1,0:T(8,128)(2,1)}, u32[]{:S(2)}) copy-start(bf16[1,256,1024]{2,1,0:T(8,128)(2,1)} %param.15) | copy-start | bytes 1572868
  413.2 11.6 %copy-start.20 = (bf16[1024,4096]{1,0:T(8,128)(2,1)S(1)}, bf16[1024,4096]{1,0:T(8,128)(2,1)}, u32[]{:S(2)}) copy-start(bf16[1024,4096]{1,0:T(8,128)(2,1)} %all-gather.23.cloned.1.call-done) | copy-start | bytes 25165828
  424.8 2.6 copy-start.14
  424.8 3.0 copy-start.18
  427.8 2.7 copy-start.4
  430.5 99.2 %reduce-scatter.11.cloned.1.call-start = ((), (), s32[]{:S(2)}) async-start(), calls=%async_computation.15 | async-start | bytes 4718592 | tf_op jit(solution)/shard_map/reduce_scatter | solution.py:204
  436.6 4.1 copy-start.15
  436.6 4.1 copy-start.12
  440.7 139.3 %reduce-scatter.7.cloned.1.call-start = ((), (), s32[]{:S(2)}) async-start(), calls=%async_computation.13 | async-start | bytes 4718592 | tf_op jit(solution)/shard_map/reduce_scatter | solution.py:202
  440.8 3.6 copy-start.1
  444.3 1.0 copy-start.7
  445.8 0.8 copy-start.8
  450.6 179.8 %reduce-scatter.9.cloned.1.call-start = ((), (), s32[]{:S(2)}) async-start(), calls=%async_computation.14 | async-start | bytes 4718592 | tf_op jit(solution)/shard_map/reduce_scatter | solution.py:203
  452.7 0.8 copy-start.9
  457.4 263.9 %reduce-scatter.15.cloned.1.call-start = ((), (), s32[]{:S(2)}) async-start(), calls=%async_computation.17 | async-start | bytes 9437184 | tf_op jit(solution)/shard_map/reduce_scatter | solution.py:210
  465.1 346.5 %reduce-scatter.17.cloned.1.call-start = ((), (), s32[]{:S(2)}) async-start(), calls=%async_computation.18 | async-start | bytes 9437184 | tf_op jit(solution)/shard_map/reduce_scatter | solution.py:213
  472.5 541.5 %all-gather.27.cloned.1.call-start = ((), (), s32[]{:S(2)}) async-start(), calls=%async_computation.19 | async-start | bytes 17301504 | tf_op jit(solution)/shard_map/all_gather | solution.py:226
  472.6 2.7 copy-start.13
  472.6 4.5 copy-start.16
  472.6 4.5 copy-start.21
  477.1 4.6 copy-start.24
  477.1 8.1 copy-start.25
  481.4 577.0 %all-reduce.11.cloned.1.call-start = ((), (), s32[]{:S(2)}) async-start(), calls=%async_computation.20 | async-start | bytes 4194304 | tf_op jit(solution)/shard_map/psum | solution.py:220
  648.5 4.8 copy-start.22
  648.5 47.7 %copy-start.3 = (f32[256,1024]{1,0:T(8,128)S(1)}, f32[256,1024]{1,0:T(8,128)}, u32[]{:S(2)}) copy-start(f32[256,1024]{1,0:T(8,128)} %copy-done.2) | copy-start | bytes 3145732
  648.5 47.7 %copy-start.10 = (bf16[256,4096]{1,0:T(8,128)(2,1)S(1)}, bf16[256,4096]{1,0:T(8,128)(2,1)}, u32[]{:S(2)}) copy-start(bf16[256,4096]{1,0:T(8,128)(2,1)} %get-tuple-element.28) | copy-start | bytes 6291460
Sparse Core Ops, SparseCore 0:
  11.0 117.6 all-gather.12
  130.3 27.2 all-gather.16
  159.2 28.5 all-gather.18
  189.3 28.5 all-gather.14
  219.3 28.5 all-gather.20
  249.4 81.5 all-gather.22
  332.6 80.5 all-gather.24
  430.6 48.5 reduce-scatter.12
  481.5 48.1 reduce-scatter.10
  531.8 48.1 reduce-scatter.6
  582.3 48.1 reduce-scatter.8
  632.6 88.6 reduce-scatter.14
  723.6 87.9 reduce-scatter.16
  815.0 158.5 all-gather.26
  976.7 81.6 all-reduce.10
where the time goes:
time: 1080 us; the launch traced here: 1070 us
  waiting for transfers between devices  567 us (52%)
  blocking collectives  278 us (26%)
  matrix products  98.6 us (9%)
  local copies, waits for them, and re-layouts  85.5 us (8%)
  between operations  22.1 us (2%)
  other arithmetic  21 us (2%)
    psum x1, blocking collectives, local(): lax.psum((part_q, part_k, part_v, part_o, part_in, part_out, part_ga, par...  202 us
    reduce_scatter x1, waiting for transfers between devices, local(): lax.psum_scatter(grad_wout.astype(jnp.bfloat16), 'shard', scatter_dimensi...  90.3 us
    all_gather x1, waiting for transfers between devices, local(): lax.all_gather(w_inner, 'shard', axis=0, tiled=True)  80.5 us
    all_gather x1, waiting for transfers between devices, local(): lax.all_gather(w_outer, 'shard', axis=0, tiled=True)  66.4 us
    reduce_scatter x1, waiting for transfers between devices, local(): lax.psum_scatter(grad_wk, 'shard', scatter_dimension=0, tiled=True)  50.5 us
    reduce_scatter x1, waiting for transfers between devices, local(): lax.psum_scatter(grad_wq, 'shard', scatter_dimension=0, tiled=True)  50.3 us
    psum x1, waiting for transfers between devices, local(): lax.psum((part_q, part_k, part_v, part_o, part_in, part_out, part_ga, par...  42.5 us
    unnamed x2, blocking collectives  42.4 us
  transfers between devices with their start and end apart: 15, of which 13 were waited for; matrix products, arithmetic and copies ran while one was open for 17% of the time, Pallas kernels for 0%

commit v1 on v0

v1 whole, which is shorter than its diff:
```python
import functools

import jax
import jax.numpy as jnp
from jax import lax
from jax.experimental import pallas as pl
from jax.experimental.pallas import tpu as pltpu
from jax.sharding import PartitionSpec as P

EPSILON = 1e-06
MASKED = -1000000000.0
AXES = ("rep", "shard")
BF16 = jnp.bfloat16
F32 = jnp.float32
INV_SQRT2 = 0.7071067811865476
INV_SQRT2PI = 0.3989422804014327

VMEM = pl.BlockSpec(memory_space=pltpu.VMEM)
SMEM = pl.BlockSpec(memory_space=pltpu.SMEM)


def shaped(shape, dtype=BF16):
    return jax.ShapeDtypeStruct(shape, dtype)


def call(body, outs, *args, scalars=1, scratch=(), aliases=None, flops=0, limit=48):
    out_bytes = sum(o.dtype.itemsize * o.size for o in outs)
    in_bytes = sum(a.dtype.itemsize * a.size for a in args)
    return pl.pallas_call(
        body,
        out_shape=outs,
        in_specs=[SMEM] * scalars + [VMEM] * (len(args) - scalars),
        out_specs=[VMEM] * len(outs),
        scratch_shapes=list(scratch),
        input_output_aliases=aliases or {},
        cost_estimate=pl.CostEstimate(
            flops=flops, bytes_accessed=in_bytes + out_bytes, transcendentals=0
        ),
        compiler_params=pltpu.CompilerParams(vmem_limit_bytes=limit * 1024 * 1024),
    )(*args)


def dot(a, b):
    return jnp.dot(a, b, preferred_element_type=F32)


def dot_nt(a, b):
    return lax.dot_general(a, b, (((1,), (1,)), ((), ())), preferred_element_type=F32)


def dot_tn(a, b):
    return lax.dot_general(a, b, (((0,), (0,)), ((), ())), preferred_element_type=F32)


def add(a, b):
    return (a.astype(F32) + b.astype(F32)).astype(BF16)


def row_blocks(sc, j, zs, hb):
    zz = lax.rem(sc[0] + zs - j, zs)
    first = pl.multiple_of((2 * zz + sc[1]) * hb, hb)
    second = pl.multiple_of((2 * zz + 1 - sc[1]) * hb, hb)
    return first, second


def norm_kernel(own, sib, gain, normed):
    half = own.shape[0]
    for at, src in ((0, own), (half, sib)):
        v = src[...].astype(F32)
        scale = lax.rsqrt(jnp.mean(v * v, axis=-1, keepdims=True) + EPSILON)
        normed[at : at + half, :] = (v * scale * gain[...]).astype(BF16)


def toeplitz(row, n):
    wide = jnp.broadcast_to(row, (n, 2 * n))
    return pltpu.roll(wide, n + 1, 1, stride=1, stride_axis=0)[:, :n]


def probabilities(q, kk, bias, length):
    n = q.shape[0]
    s = dot_nt(q, kk) + bias
    col = lax.broadcasted_iota(jnp.int32, (n, n), 1)
    s = jnp.where(col < length, s, MASKED)
    e = jnp.exp(s - jnp.max(s, axis=-1, keepdims=True))
    return e / jnp.sum(e, axis=-1, keepdims=True)


def attn_kernel(zs, hb, hd, sc, normed, off, *refs):
    pieces, (w, qkv, mixed) = refs[:zs], refs[zs:]
    for j in range(zs):
        first, second = row_blocks(sc, j, zs, hb)
        w[pl.ds(first, hb), :] = pieces[j][:hb, : 3 * hb]
        w[pl.ds(second, hb), :] = pieces[j][hb:, : 3 * hb]
    qkv[...] = dot(normed[...], w[...]).astype(BF16)
    half = normed.shape[0] // 2
    for h in range(hb // hd):
        bias = toeplitz(off[h : h + 1, :], half)
        for s in range(2):
            rows = slice(s * half, (s + 1) * half)
            q, kk, v = (qkv[rows, i * hb + h * hd : i * hb + (h + 1) * hd] for i in range(3))
            p = probabilities(q, kk, bias, sc[3 + s]).astype(BF16)
            mixed[rows, h * hd : (h + 1) * hd] = dot(p, v).astype(BF16)


def mixer_kernel(zs, rs, hb, sc, *refs):
    mixed_parts, pieces = refs[:rs], refs[rs : rs + rs * zs]
    mixed, wo, partial = refs[rs + rs * zs :]
    for m in range(rs):
        mixed[:, m * hb : (m + 1) * hb] = mixed_parts[m][...]
    for m in range(rs):
        col = pl.multiple_of(lax.bitwise_xor(sc[2], m) * (2 * hb), 2 * hb)
        for j in range(zs):
            block = lax.bitwise_xor(lax.rem(sc[0] + zs - j, zs), sc[2])
            piece = pieces[m * zs + j]
            both = jnp.concatenate([piece[:hb, 3 * hb :], piece[hb:, 3 * hb :]], axis=1)
            wo[pl.ds(pl.multiple_of(block * hb, hb), hb), pl.ds(col, 2 * hb)] = both
    partial[...] = dot(mixed[...], wo[...]).astype(BF16)


def middle_kernel(own, sib, part, other, gain, middle, normed2):
    half = own.shape[0]
    for s, src in ((0, own), (1, sib)):
        rows = slice(s * half, (s + 1) * half)
        swapped = slice((1 - s) * half, (2 - s) * half)
        v = src[...].astype(F32) + part[rows, :].astype(F32) + other[swapped, :].astype(F32)
        middle[rows, :] = v
        scale = lax.rsqrt(jnp.mean(v * v, axis=-1, keepdims=True) + EPSILON)
        normed2[rows, :] = (v * scale * gain[...]).astype(BF16)


def ffn_kernel(zs, hb, sub, first_chunk, sc, normed2, normed2t, gl, *refs):
    n_in = 2 * zs + (0 if first_chunk else 2)
    pieces_i, pieces_o = refs[:zs], refs[zs : 2 * zs]
    acc_in = refs[2 * zs : n_in]
    outer, gn2, gi, go, w1, w2, act_t = refs[n_in:]
    for j in range(zs):
        first, second = row_blocks(sc, j, zs, hb)
        w1[pl.ds(first, hb), :] = pieces_i[j][:hb, :]
        w1[pl.ds(second, hb), :] = pieces_i[j][hb:, :]
        zz = lax.rem(sc[0] + zs - j, zs)
        w2[pl.ds(pl.multiple_of(zz * sub, sub), sub), :] = pieces_o[j][...]
    h = dot(normed2[...], w1[...])
    cdf = 0.5 * (1.0 + lax.erf(h * INV_SQRT2))
    pdf = jnp.exp(-0.5 * h * h) * INV_SQRT2PI
    act = (h * cdf).astype(BF16)
    ga = dot_nt(gl[...], w2[...])
    gh = (ga * (cdf + h * pdf)).astype(BF16)
    act_t[...] = act.T
    out_part = dot(act, w2[...])
    gn_part = dot_nt(gh, w1[...])
    if not first_chunk:
        out_part = out_part + acc_in[0][...]
        gn_part = gn_part + acc_in[1][...]
    outer[...] = out_part
    gn2[...] = gn_part
    for j in range(zs):
        first, second = row_blocks(sc, j, zs, hb)
        gi[j, :hb, :] = dot(normed2t[pl.ds(first, hb), :], gh).astype(BF16)
        gi[j, hb:, :] = dot(normed2t[pl.ds(second, hb), :], gh).astype(BF16)
        zz = lax.rem(sc[0] + zs - j, zs)
        rows = pl.ds(pl.multiple_of(zz * sub, sub), sub)
        go[j] = dot(act_t[rows, :], gl[...]).astype(BF16)


def middle_back_kernel(zs, rs, hb, sc, part, other, middle, gl, gain, mixed, wo, *refs):
    grad_mid, gm, ggain, gwo, gatt, full = refs
    half = part.shape[0] // 2
    width = part.shape[1]
    for s in range(2):
        rows = slice(s * half, (s + 1) * half)
        swapped = slice((1 - s) * half, (2 - s) * half)
        gn = part[rows, :] + other[swapped, :].astype(F32)
        v = middle[rows, :]
        scale = lax.rsqrt(jnp.mean(v * v, axis=-1, keepdims=True) + EPSILON)
        gg = gn * gain[...]
        inner = jnp.sum(gg * v, axis=-1, keepdims=True) * (1.0 / width)
        g = gl[rows, :].astype(F32) + scale * gg - v * (scale * scale * scale * inner)
        if s == 0:
            grad_mid[...] = g
            ggain[...] = jnp.sum(gn * v * scale, axis=0, keepdims=True)
        gatt[rows, :] = g.astype(BF16)
    gm[...] = dot_nt(gatt[...], wo[...]).astype(BF16)
    full[...] = dot_tn(mixed[...], gatt[...]).astype(BF16)
    for j in range(zs):
        block = lax.bitwise_xor(lax.rem(sc[0] + zs - j, zs), sc[2])
        gwo[j] = full[pl.ds(pl.multiple_of(block * hb, hb), hb), :]


def attn_back_kernel(zs, hb, hd, at, sc, normedt, off, qkv, gmix, *refs):
    gqkv, gw, diag = refs
    half = qkv.shape[0] // 2
    flip = (
        lax.broadcasted_iota(jnp.int32, (half, half), 0)
        + lax.broadcasted_iota(jnp.int32, (half, half), 1)
        == half - 1
    ).astype(BF16)
    for h in range(hb // hd):
        bias = toeplitz(off[h : h + 1, :], half)
        flipped = jnp.zeros((half, half), F32)
        for s in range(2):
            rows = slice(s * half, (s + 1) * half)
            q, kk, v = (qkv[rows, i * hb + h * hd : i * hb + (h + 1) * hd] for i in range(3))
            gm = gmix[rows, at + h * hd : at + (h + 1) * hd]
            p = probabilities(q, kk, bias, sc[3 + s])
            gp = dot_nt(gm, v)
            delta = jnp.sum(p * gp, axis=-1, keepdims=True)
            gs = (p * (gp - delta)).astype(BF16)
            flipped = flipped + dot(flip, gs)
            cols = [slice(i * hb + h * hd, i * hb + (h + 1) * hd) for i in range(3)]
            gqkv[rows, cols[0]] = dot(gs, kk).astype(BF16)
            gqkv[rows, cols[1]] = dot_tn(gs, q).astype(BF16)
            gqkv[rows, cols[2]] = dot_tn(p.astype(BF16), gm).astype(BF16)
        wide = jnp.concatenate([flipped, jnp.zeros((half, half), F32)], axis=1)
        skewed = pltpu.roll(wide, 0, 1, stride=1, stride_axis=0)
        diag[h : h + 1, :] = jnp.sum(skewed, axis=0, keepdims=True)
    for j in range(zs):
        first, second = row_blocks(sc, j, zs, hb)
        gw[j, :hb, :] = dot(normedt[pl.ds(first, hb), :], gqkv[...]).astype(BF16)
        gw[j, hb:, :] = dot(normedt[pl.ds(second, hb), :], gqkv[...]).astype(BF16)


def grad_normed_kernel(rs, *refs):
    grads, weights, (own, sib) = refs[:rs], refs[rs : 2 * rs], refs[2 * rs :]
    half = own.shape[0]
    total = dot_nt(grads[0][...], weights[0][...])
    for m in range(1, rs):
        total = total + dot_nt(grads[m][...], weights[m][...])
    own[...] = total[:half, :]
    sib[...] = total[half:, :].astype(BF16)


def input_back_kernel(own, other, grad_mid, x, gain, out, ggain):
    gn = own[...] + other[...].astype(F32)
    v = x[...].astype(F32)
    scale = lax.rsqrt(jnp.mean(v * v, axis=-1, keepdims=True) + EPSILON)
    gg = gn * gain[...]
    inner = jnp.mean(gg * v, axis=-1, keepdims=True)
    g = grad_mid[...] + scale * gg - v * (scale * scale * scale * inner)
    out[...] = g.astype(BF16)
    ggain[...] = jnp.sum(gn * v * scale, axis=0, keepdims=True)


def layer_kernel(sc, middle, own, other, out):
    half = own.shape[0]
    row = lax.broadcasted_iota(jnp.int32, own.shape, 0)
    v = middle[...] + own[...] + other[...].astype(F32)
    out[...] = jnp.where(row < sc[3], v, 0.0).astype(BF16)


def shuffle_kernel(count, index, src, out):
    for e in range(count):
        out[e] = src[index[e]]


def shuffle(index, blocks):
    body = functools.partial(shuffle_kernel, blocks.shape[0])
    return call(body, [shaped(blocks.shape)], index.astype(jnp.int32), blocks)[0]


def solution(mesh):
    rs, ss = mesh.shape["rep"], mesh.shape["shard"]
    zs = ss // 2
    count = rs * ss

    def pairs(move):
        table = []
        for i in range(count):
            r, z, k = i // ss, (i % ss) // 2, i % 2
            r, z, k = move(r, z, k)
            table.append((i, (r * zs + z) * 2 + k))
        return table

    core_pairs = pairs(lambda r, z, k: (r, z, 1 - k))
    ring_pairs = pairs(lambda r, z, k: (r, (z + 1) % zs, k))
    rep_pairs = {m: pairs(lambda r, z, k, m=m: (r ^ m, z, k)) for m in range(1, rs)}
    z_pairs = {m: pairs(lambda r, z, k, m=m: (r, z ^ m, k)) for m in range(1, zs)}

    def send(value, table):
        return lax.ppermute(value, AXES, table)

    bits = [1 << b for b in range(rs.bit_length() - 1)]

    def hop(m, turn):
        mine = [b for b in bits if m & b]
        return mine[turn % len(mine)]

    by_size = sorted(range(1, rs), key=lambda m: (bin(m).count("1"), m))

    def gather(own):
        got = [[None] * rs for _ in range(zs)]
        got[0] = list(own)
        v = own[0]
        for j in range(1, zs):
            v = send(v, ring_pairs)
            got[j][0] = v
        for m in by_size:
            for j in range(1, zs):
                b = hop(m, j)
                got[j][m] = send(got[j][m ^ b], rep_pairs[b])
        return got

    def sum_reps(parts, turn):
        parts = list(parts)
        for m in reversed(by_size):
            b = hop(m, turn)
            parts[m ^ b] = add(parts[m ^ b], send(parts[m], rep_pairs[b]))
        return parts[0]

    def spread_reps(mine, turn):
        parts = [mine] + [None] * (rs - 1)
        for m in by_size:
            b = hop(m, turn)
            parts[m] = send(parts[m ^ b], rep_pairs[b])
        return parts

    def sum_ring(parts):
        v = parts[1]
        for j in range(2, zs):
            v = add(send(v, ring_pairs), parts[j])
        return add(send(v, ring_pairs), parts[0])

    def exchange(blocks, whole_core=False):
        _, p, width = blocks.shape
        v = blocks.reshape(rs, 2 * zs, p, width)
        v = [v[0]] + [send(v[m], rep_pairs[m]) for m in range(1, rs)]
        v = jnp.stack(v).reshape(rs, zs, 2, p, width)
        v = [v[:, 0]] + [send(v[:, m], z_pairs[m]) for m in range(1, zs)]
        v = jnp.stack(v, axis=1)
        if not whole_core:
            other = send(v[:, :, 1], core_pairs)
            return jnp.stack([v[:, :, 0], other], axis=2).reshape(blocks.shape)
        other = send(v, core_pairs)
        mine = jnp.stack([v[:, :, 0], other[:, :, 1]], axis=2).reshape(blocks.shape)
        theirs = jnp.stack([v[:, :, 1], other[:, :, 0]], axis=2).reshape(blocks.shape)
        return mine, theirs

    def local(
        inputs,
        cotangent,
        seq_lengths,
        dealing,
        rel_buckets,
        w_query,
        w_key,
        w_value,
        w_mixer,
        w_inner,
        w_outer,
        gain_attn,
        gain_mlp,
        bias_table,
    ):
        seq_len, width = inputs.shape[1], inputs.shape[2]
        n_buckets, heads = bias_table.shape[0] * ss, bias_table.shape[1]
        hb = w_query.shape[0]
        fb = w_outer.shape[0]
        sub = fb // rs
        cols = zs * sub
        hd = width // heads
        nh = hb // hd
        tokens = 2 * seq_len

        r, c = lax.axis_index("rep"), lax.axis_index("shard")
        z, k = c // 2, c % 2
        me = r * ss + c
        ids = jnp.arange(count, dtype=jnp.int32)
        inverse = jnp.sum(
            jnp.where(dealing[None, :] == ids[:, None], ids[None, :], 0), axis=1
        ).astype(jnp.int32)
        own_len, sib_len = seq_lengths[me], seq_lengths[me ^ 1]
        sc = jnp.stack([z, k, r, own_len, sib_len]).astype(jnp.int32)

        x_own = inputs[0]
        x_sib = send(x_own, core_pairs)

        outer_own = [lax.dynamic_slice(w_outer, ((r ^ m) * sub, 0), (sub, width)) for m in range(rs)]

        def head_cols(m, core):
            at = (2 * (r ^ m) + core) * hb
            return [lax.dynamic_slice(w, (0, at), (hb, hb)) for w in (w_query, w_key, w_value)]

        def inner_cols(m, core):
            at = [(2 * b + core) * fb + (r ^ m) * sub for b in range(zs)]
            return jnp.concatenate(
                [lax.dynamic_slice(w_inner, (0, a), (hb, sub)) for a in at], axis=1
            )

        attn_sent = jnp.stack([jnp.concatenate(head_cols(m, 1 - k), axis=1) for m in range(rs)])
        attn_got = send(attn_sent, core_pairs)
        attn_own = []
        for m in range(rs):
            mix = lax.dynamic_slice(w_mixer, (0, (r ^ m) * 2 * hb), (hb, 2 * hb))
            top = jnp.concatenate(head_cols(m, k) + [mix[:, :hb]], axis=1)
            low = jnp.concatenate([attn_got[m], mix[:, hb:]], axis=1)
            attn_own.append(jnp.concatenate([top, low], axis=0))
        inner_sent = jnp.stack([inner_cols(m, 1 - k) for m in range(rs)])
        inner_got = send(inner_sent, core_pairs)
        inner_own = [
            jnp.concatenate([inner_cols(m, k), inner_got[m]], axis=0) for m in range(rs)
        ]
        attn_w = gather(attn_own)
        outer_w = gather(outer_own)
        inner_w = gather(inner_own)

        small = jnp.concatenate([gain_attn, gain_mlp, bias_table.reshape(-1)])[None]
        small = jnp.concatenate([small, send(small, core_pairs)], axis=0)
        for b in [1 << i for i in range(zs.bit_length() - 1)]:
            small = jnp.concatenate([small, send(small, z_pairs[b])], axis=0)
        shards = jnp.arange(ss, dtype=jnp.int32)
        order = (shards[:, None] == (shards ^ c)[None, :]).astype(BF16)
        small = dot(order, small)
        gain_a = small[:, :hb].reshape(1, width)
        gain_m = small[:, hb : 2 * hb].reshape(1, width)
        table = small[:, 2 * hb :].reshape(n_buckets, heads)
        groups = jnp.arange(rs, dtype=jnp.int32) ^ r
        head_ids = ((2 * groups + k) * nh)[:, None] + jnp.arange(nh, dtype=jnp.int32)[None]
        head_ids = head_ids.reshape(-1)
        pick = (jnp.arange(heads, dtype=jnp.int32)[:, None] == head_ids[None, :]).astype(BF16)
        padded = jnp.concatenate([rel_buckets, jnp.full((1,), -1, jnp.int32)])
        hot = (padded[None, :] == jnp.arange(n_buckets, dtype=jnp.int32)[:, None]).astype(BF16)
        my_table = dot(table.astype(BF16), pick).astype(BF16)
        offsets = lax.dot_general(
            my_table, hot, (((0,), (0,)), ((), ())), preferred_element_type=F32
        ).reshape(rs, nh, 2 * seq_len)

        rows = seq_len // count
        cot = shuffle(ids ^ me, cotangent[0].reshape(count, rows, width))
        cot = exchange(cot)
        cot = shuffle(inverse[ids ^ me] ^ me, cot)
        cot_own, cot_sib = exchange(cot, whole_core=True)
        both = jnp.concatenate([cot_own, cot_sib], axis=0)
        both = shuffle(jnp.concatenate([ids ^ me, (ids ^ me) + count]), both)
        place = jnp.arange(seq_len, dtype=jnp.int32)
        valid = jnp.concatenate([place < own_len, place < sib_len])[:, None]
        gl = jnp.where(valid, both.reshape(tokens, width), jnp.zeros((), BF16))

        normed = call(norm_kernel, [shaped((tokens, width))], x_own, x_sib, gain_a, scalars=0)[0]
        normed_t = normed.T
        w_heads, qkv, mixed_parts = [], [], []
        for m in range(rs):
            w, q, mix = call(
                functools.partial(attn_kernel, zs, hb, hd),
                [shaped((width, 3 * hb)), shaped((tokens, 3 * hb)), shaped((tokens, hb))],
                sc,
                normed,
                offsets[m],
                *[attn_w[j][m] for j in range(zs)],
                flops=2 * tokens * width * 3 * hb,
            )
            w_heads.append(w)
            qkv.append(q)
            mixed_parts.append(mix)
        mixed, wo, part = call(
            functools.partial(mixer_kernel, zs, rs, hb),
            [shaped((tokens, rs * hb)), shaped((rs * hb, width)), shaped((tokens, width))],
            sc,
            *mixed_parts,
            *[attn_w[j][m] for m in range(rs) for j in range(zs)],
            flops=2 * tokens * width * rs * hb,
        )
        other = send(part, core_pairs)
        middle, normed2 = call(
            middle_kernel,
            [shaped((tokens, width), F32), shaped((tokens, width))],
            x_own,
            x_sib,
            part,
            other,
            gain_m,
            scalars=0,
        )
        normed2_t = normed2.T

        acc = []
        grad_inner, grad_outer = [], []
        for m in range(rs):
            n_in = 4 + 2 * zs
            outs = call(
                functools.partial(ffn_kernel, zs, hb, sub, m == 0),
                [
                    shaped((tokens, width), F32),
                    shaped((tokens, width), F32),
                    shaped((zs, 2 * hb, cols)),
                    shaped((zs, sub, width)),
                ],
                sc,
                normed2,
                normed2_t,
                gl,
                *[inner_w[j][m] for j in range(zs)],
                *[outer_w[j][m] for j in range(zs)],
                *acc,
                scratch=[
                    pltpu.VMEM((width, cols), BF16),
                    pltpu.VMEM((cols, width), BF16),
                    pltpu.VMEM((cols, tokens), BF16),
                ],
                aliases={} if m == 0 else {n_in: 0, n_in + 1: 1},
                flops=12 * tokens * width * cols,
            )
            acc = outs[:2]
            grad_inner.append(outs[2])
            grad_outer.append(outs[3])
        outer_part, gn2_part = acc

        gn2_other = send(gn2_part.astype(BF16), core_pairs)
        outer_other = send(outer_part[seq_len:].astype(BF16), core_pairs)

        inner_sum = sum_reps(grad_inner, 0)
        inner_sum = sum_ring([inner_sum[j] for j in range(zs)])
        outer_ring = [sum_ring([g[j] for j in range(zs)]) for g in grad_outer]

        grad_mid, gmix, ggain_m, grad_wo = call(
            functools.partial(middle_back_kernel, zs, rs, hb),
            [
                shaped((seq_len, width), F32),
                shaped((tokens, rs * hb)),
                shaped((1, width), F32),
                shaped((zs, hb, width)),
            ],
            sc,
            gn2_part,
            gn2_other,
            middle,
            gl,
            gain_m,
            mixed,
            wo,
            scratch=[pltpu.VMEM((tokens, width), BF16), pltpu.VMEM((rs * hb, width), BF16)],
            flops=4 * tokens * width * rs * hb,
        )
        mixer_ring = sum_ring([grad_wo[j] for j in range(zs)])

        layer = call(
            layer_kernel,
            [shaped((seq_len, width))],
            sc,
            middle[:seq_len],
            outer_part[:seq_len],
            outer_other,
        )[0]
        layer = shuffle(ids ^ me, layer.reshape(count, rows, width))
        layer = exchange(layer)
        layer = shuffle(dealing[ids ^ me] ^ me, layer)
        layer = shuffle(ids ^ me, exchange(layer)).reshape(1, seq_len, width)

        grad_heads, gqkv, diag = [None] * rs, [None] * rs, [None] * rs
        for m in reversed(range(rs)):
            gqkv[m], grad_heads[m], diag[m] = call(
                functools.partial(attn_back_kernel, zs, hb, hd, m * hb),
                [
                    shaped((tokens, 3 * hb)),
                    shaped((zs, 2 * hb, 3 * hb)),
                    shaped((nh, 2 * seq_len), F32),
                ],
                sc,
                normed_t,
                offsets[m],
                qkv[m],
                gmix,
                flops=2 * tokens * width * 3 * hb,
            )
        heads_sum = sum_reps(grad_heads, 1)
        heads_sum = sum_ring([heads_sum[j] for j in range(zs)])
        gn_own, gn_sib = call(
            functools.partial(grad_normed_kernel, rs),
            [shaped((seq_len, width), F32), shaped((seq_len, width))],
            *gqkv,
            *w_heads,
            scalars=0,
            flops=2 * tokens * width * 3 * hb * rs,
        )
        gn_other = send(gn_sib, core_pairs)
        input_grad, ggain_a = call(
            input_back_kernel,
            [shaped((seq_len, width)), shaped((1, width), F32)],
            gn_own,
            gn_other,
            grad_mid,
            x_own,
            gain_a,
            scalars=0,
        )

        by_bucket = lax.dot_general(
            hot.astype(F32),
            jnp.concatenate(diag, axis=0),
            (((1,), (1,)), ((), ())),
            precision=lax.Precision.HIGHEST,
        )
        grad_table = lax.dot_general(
            by_bucket,
            pick.astype(F32),
            (((1,), (1,)), ((), ())),
            precision=lax.Precision.HIGHEST,
        )
        tiny = jnp.concatenate([ggain_a[0], ggain_m[0], grad_table.reshape(-1)])
        tiny = tiny.reshape(-1, 128)
        tiny = tiny + send(tiny, core_pairs)
        for b in [1 << i for i in range(zs.bit_length() - 1)]:
            tiny = tiny + send(tiny, z_pairs[b])
        for b in bits:
            tiny = tiny + send(tiny, rep_pairs[b])
        tiny = tiny.reshape(-1)
        sum_ga = lax.dynamic_slice(tiny, (c * hb,), (hb,))
        sum_gm = lax.dynamic_slice(tiny, (width + c * hb,), (hb,))
        tab = tiny[2 * width :].reshape(n_buckets, heads)
        sum_tab = lax.dynamic_slice(tab, (c * (n_buckets // ss), 0), (n_buckets // ss, heads))

        mix_rows = hb // rs
        late = [
            jnp.concatenate(
                [
                    outer_ring[m],
                    lax.dynamic_slice(mixer_ring, ((r ^ m) * mix_rows, 0), (mix_rows, width)),
                ],
                axis=0,
            )
            for m in range(rs)
        ]
        late = jnp.stack(spread_reps(sum_reps(late, 1), 0))
        late = jnp.take(late, groups, axis=0).astype(F32)
        sum_out = late[:, :sub].reshape(fb, width)
        sum_o = late[:, sub:].reshape(hb, width)

        def halves(final):
            final = jnp.take(jnp.stack(final), groups, axis=0)
            mine = final[:, :hb]
            theirs = send(final[:, hb:], core_pairs)
            low = jnp.where(k == 0, mine, theirs)
            high = jnp.where(k == 0, theirs, mine)
            return jnp.stack([low, high], axis=1)

        inner_final = halves(spread_reps(inner_sum, 1))
        inner_final = inner_final.reshape(rs, 2, hb, zs, sub)
        sum_in = jnp.transpose(inner_final, (2, 3, 1, 0, 4)).reshape(hb, -1).astype(F32)
        heads_final = halves(spread_reps(heads_sum, 0)).reshape(rs, 2, hb, 3, hb)
        heads_final = jnp.transpose(heads_final, (3, 2, 0, 1, 4)).reshape(3, hb, width)
        sum_q, sum_k, sum_v = (heads_final[i].astype(F32) for i in range(3))

        return (
            layer,
            input_grad[None],
            sum_q,
            sum_k,
            sum_v,
            sum_o,
            sum_in,
            sum_out,
            sum_ga,
            sum_gm,
            sum_tab,
        )

    tokens_spec = P(AXES, None, None)
    rows_spec, part_spec = P("shard", None), P("shard")
    in_specs = (
        (tokens_spec,) * 2 + (P(),) * 3 + (rows_spec,) * 6 + (part_spec,) * 2 + (rows_spec,)
    )
    out_specs = (tokens_spec,) * 2 + (rows_spec,) * 6 + (part_spec,) * 2 + (rows_spec,)
    return jax.shard_map(local, mesh=mesh, in_specs=in_specs, out_specs=out_specs, check_vma=False)
```

time: 1080 us -> 521 us (0.48)
  waiting for transfers between devices: 567 us -> 201 us
  blocking collectives: 278 us -> 0 us
  starting transfers between devices: 1.06 us -> 129 us
  matrix products: 98.6 us -> 0.77 us
  Pallas kernels: 0 us -> 90.7 us
  local copies, waits for them, and re-layouts: 85.5 us -> 55 us
  between operations: 22.1 us -> 3.35 us
    all_gather x8 -> x0, waiting for transfers between devices: 284 us -> none  [the longest x1 80.5 us: local(): lax.all_gather(w_inner, 'shard', axis=0, tiled=True)]
    reduce_scatter x6 -> x0, waiting for transfers between devices: 236 us -> none  [the longest x1 90.3 us: local(): lax.psum_scatter(grad_wout.astype(jnp.bfloat16), 'shard', scatter_dimensi...]
    psum x1 -> x0, blocking collectives: 202 us -> none  [local(): lax.psum((part_q, part_k, part_v, part_o, part_in, part_out, part_ga, par...]
    ppermute x0 -> x120, waiting for transfers between devices: none -> 201 us  [send(): return lax.ppermute(value, AXES, table)]
    ppermute x0 -> x120, starting transfers between devices: none -> 129 us  [send(): return lax.ppermute(value, AXES, table)]
    dot_general x26 -> x4, matrix products: 98.6 us -> 0.77 us  [the longest x1 0.3 us: local(): lax.dot_general(my_table, hot, (((0,), (0,)), ((), ())), preferred_elemen...]
    pallas_call x0 -> x25, Pallas kernels: none -> 90.7 us  [call(): pl.pallas_call(body, out_shape=outs, in_specs=[SMEM] * scalars + [VMEM] *...]
    psum x1 -> x0, waiting for transfers between devices: 42.5 us -> none  [local(): lax.psum((part_q, part_k, part_v, part_o, part_in, part_out, part_ga, par...]
  transfers between devices with their start and end apart: 15 -> 120, of which waited for: 13 -> 55; matrix products, arithmetic and copies ran while one was open for 17% -> 11% of each run, Pallas kernels for 0% -> 14%
where the time goes in v1:
time: 521 us; the launch traced here: 512 us
  waiting for transfers between devices  201 us (39%)
  starting transfers between devices  129 us (25%)
  Pallas kernels  90.7 us (17%)
  local copies, waits for them, and re-layouts  55 us (11%)
  other arithmetic  31.7 us (6%)
    ppermute x120, waiting for transfers between devices, send(): return lax.ppermute(value, AXES, table)  201 us
    ppermute x120, starting transfers between devices, send(): return lax.ppermute(value, AXES, table)  129 us
    pallas_call x25, Pallas kernels, call(): pl.pallas_call(body, out_shape=outs, in_specs=[SMEM] * scalars + [VMEM] *...  90.7 us
    unnamed x239, local copies, waits for them, and re-layouts  24.8 us
  transfers between devices with their start and end apart: 120, of which 55 were waited for; matrix products, arithmetic and copies ran while one was open for 11% of the time, Pallas kernels for 14%

profile of v1, /device:TPU:0, one launch (start us, length us, event | category | flops | bytes accessed | tf_op | source)
XLA Modules:
  0.0 511.7 jit_solution(13778348292987523469)
XLA Ops:
  24.8 3.1 collective-permute-start.3
  36.7 3.7 collective-permute-done.21
  40.4 6.3 %collective-permute-done.22 = bf16[4,2,8,1024]{3,2,0,1:T(8,128)(2,1)S(1)} collective-permute-done((bf16[4,2,8,1024]{3,2,0,1:T(8,128)(2,1)S(1)}, bf16[4,2,8,1024]{3,2,0,1:T(8,128)(2,1)S(1)}, u32[]{:S(2)}, u32[]{:S(2)}) %collective-permute-start.22) | collective-permute-done | bytes 131104 | tf_op jit(solution)/shard_map/ppermute | solution.py:279
  54.2 3.4 collective-permute-done.5.refs_1_.refs_5_
  61.9 6.7 %collective-permute-done.6.refs_2_.refs_6_ = bf16[256,512]{1,0:T(8,128)(2,1)S(1)} collective-permute-done((bf16[256,512]{1,0:T(8,128)(2,1)S(1)}, bf16[256,512]{1,0:T(8,128)(2,1)S(1)}, u32[]{:S(2)}, u32[]{:S(2)}) %collective-permute-start.6) | collective-permute-done | bytes 262176 | tf_op jit(solution)/shard_map/ppermute | solution.py:279
  69.2 5.2 %collective-permute-done.42.refs_5_ = bf16[128,1024]{1,0:T(8,128)(2,1)} collective-permute-done((bf16[128,1024]{1,0:T(8,128)(2,1)S(1)}, bf16[128,1024]{1,0:T(8,128)(2,1)}, u32[]{:S(2)}, u32[]{:S(2)}) %collective-permute-start.42) | collective-permute-done | bytes 262176 | tf_op jit(solution)/shard_map/ppermute | solution.py:279
  77.6 7.0 %collective-permute-done.28 = bf16[4,2,8,1024]{3,2,1,0:T(8,128)(2,1)S(1)} collective-permute-done((bf16[4,2,8,1024]{3,2,1,0:T(8,128)(2,1)S(1)}, bf16[4,2,8,1024]{3,2,1,0:T(8,128)(2,1)S(1)}, u32[]{:S(2)}, u32[]{:S(2)}) %collective-permute-start.28) | collective-permute-done | bytes 131104 | tf_op jit(solution)/shard_map/ppermute | solution.py:279
  98.7 3.7 collective-permute-done.10.refs_3_.refs_11_
  129.1 4.8 collective-permute-start.36
  136.1 8.9 %collective-permute-done.36.refs_2_ = bf16[256,512]{1,0:T(8,128)(2,1)} collective-permute-done((bf16[256,512]{1,0:T(8,128)(2,1)}, bf16[256,512]{1,0:T(8,128)(2,1)}, u32[]{:S(2)}, u32[]{:S(2)}) %collective-permute-start.36) | collective-permute-done | bytes 262176 | tf_op jit(solution)/shard_map/ppermute | solution.py:279
  147.0 3.0 shard_map.227
  156.2 7.3 %shard_map.231 = (f32[512,1024]{1,0:T(8,128)}, f32[512,1024]{1,0:T(8,128)}, bf16[4,256,512]{2,1,0:T(8,128)(2,1)S(1)}, bf16[4,128,1024]{2,1,0:T(8,128)(2,1)S(1)}) custom-call(s32[5]{0:T(128)S(1)} %stack.236.sc, bf16[512,1024]{1,0:T(8,128)(2,1)S(1)} %get-tuple-element.70.normed2, bf16[1024,512]{1,0:T(8,128)(2,1)} %bitcast.335, ...), custom_call_target="tpu_custom_call" | custom-call | flops 3221225472 | bytes 11534356 | tf_op jit(solution)/shard_map/pallas_call | solution.py:29
  168.5 4.1 collective-permute-done.55.refs_2_
  177.0 8.7 %shard_map.232 = (f32[512,1024]{1,0:T(8,128)}, f32[512,1024]{1,0:T(8,128)}, bf16[4,256,512]{2,1,0:T(8,128)(2,1)}, bf16[4,128,1024]{2,1,0:T(8,128)(2,1)S(1)}) custom-call(s32[5]{0:T(128)S(1)} %stack.236.sc, bf16[512,1024]{1,0:T(8,128)(2,1)S(1)} %get-tuple-element.70.normed2, ...), custom_call_target="tpu_custom_call", output_to_operand_aliasing={{0}: (12, {}), {1}: (13, {})} | custom-call | flops 3221225472 | bytes 15728660 | tf_op jit(solution)/shard_map/pallas_call | solution.py:29
  191.2 4.4 collective-permute-done.52.refs_3_
  198.1 8.0 %shard_map.233 = (f32[512,1024]{1,0:T(8,128)}, f32[512,1024]{1,0:T(8,128)}, bf16[4,256,512]{2,1,0:T(8,128)(2,1)S(1)}, bf16[4,128,1024]{2,1,0:T(8,128)(2,1)S(1)}) custom-call(s32[5]{0:T(128)S(1)} %stack.236.sc, bf16[512,1024]{1,0:T(8,128)(2,1)S(1)} %copy-done.5, bf16[1024,512]{1,0:T(8,128)(2,1)} %bitcast.337, ...), custom_call_target="tpu_custom_call", output_to_operand_aliasing={{0}: (12, {}), {1}: (13, {})} | custom-call | flops 3221225472 | bytes 15728660 | tf_op jit(solution)/shard_map/pallas_call | solution.py:29
  206.3 2.8 collective-permute-done.41.refs_3_
  209.1 20.7 %shard_map.234 = (f32[512,1024]{1,0:T(8,128)}, f32[512,1024]{1,0:T(8,128)}, bf16[4,256,512]{2,1,0:T(8,128)(2,1)}, bf16[4,128,1024]{2,1,0:T(8,128)(2,1)S(1)}) custom-call(s32[5]{0:T(128)S(1)} %stack.236.sc, bf16[512,1024]{1,0:T(8,128)(2,1)S(1)} %copy-done.5, bf16[1024,512]{1,0:T(8,128)(2,1)} %bitcast.338, ...), custom_call_target="tpu_custom_call", output_to_operand_aliasing={{0}: (12, {}), {1}: (13, {})} | custom-call | flops 3221225472 | bytes 15728660 | tf_op jit(solution)/shard_map/pallas_call | solution.py:29
  237.8 5.8 %collective-permute-done.84 = bf16[128,1024]{1,0:T(8,128)(2,1)S(1)} collective-permute-done((bf16[128,1024]{1,0:T(8,128)(2,1)S(1)}, bf16[128,1024]{1,0:T(8,128)(2,1)S(1)}, u32[]{:S(2)}, u32[]{:S(2)}) %collective-permute-start.84) | collective-permute-done | bytes 262176 | tf_op jit(solution)/shard_map/ppermute | solution.py:279
  244.1 5.1 collective-permute-done.90
  249.3 5.5 %collective-permute-done.94 = bf16[128,1024]{1,0:T(8,128)(2,1)S(1)} collective-permute-done((bf16[128,1024]{1,0:T(8,128)(2,1)S(1)}, bf16[128,1024]{1,0:T(8,128)(2,1)S(1)}, u32[]{:S(2)}, u32[]{:S(2)}) %collective-permute-start.94) | collective-permute-done | bytes 262176 | tf_op jit(solution)/shard_map/ppermute | solution.py:279
  255.3 5.1 collective-permute-done.97
  261.0 5.1 collective-permute-done.85
  268.5 3.2 collective-permute-done.91
  273.0 4.2 collective-permute-done.95
  278.9 3.3 collective-permute-done.98
  284.7 3.3 collective-permute-done.60
  288.6 6.3 %collective-permute-done.86 = bf16[128,1024]{1,0:T(8,128)(2,1)S(1)} collective-permute-done((bf16[128,1024]{1,0:T(8,128)(2,1)S(1)}, bf16[128,1024]{1,0:T(8,128)(2,1)S(1)}, u32[]{:S(2)}, u32[]{:S(2)}) %collective-permute-start.86) | collective-permute-done | bytes 262176 | tf_op jit(solution)/shard_map/ppermute | solution.py:279
  295.7 4.8 collective-permute-done.92
  311.2 7.2 %collective-permute-done.96 = bf16[128,1024]{1,0:T(8,128)(2,1)S(1)} collective-permute-done((bf16[128,1024]{1,0:T(8,128)(2,1)S(1)}, bf16[128,1024]{1,0:T(8,128)(2,1)S(1)}, u32[]{:S(2)}, u32[]{:S(2)}) %collective-permute-start.96) | collective-permute-done | bytes 262176 | tf_op jit(solution)/shard_map/ppermute | solution.py:279
  322.1 4.6 shard_map.239
  329.3 3.8 shard_map.243
  334.8 3.8 shard_map.242
  339.5 3.8 shard_map.241
  344.1 4.0 shard_map.240
  357.9 3.3 shard_map.244
  362.8 5.7 %collective-permute-start.65 = (bf16[8,8,1024]{2,1,0:T(8,128)(2,1)S(1)}, bf16[8,8,1024]{2,1,0:T(8,128)(2,1)S(1)}, u32[]{:S(2)}, u32[]{:S(2)}) collective-permute-start(bf16[8,8,1024]{2,1,0:T(8,128)(2,1)S(1)} %get-tuple-element.191), channel_id=1, source_target_pairs={{0,8},{1,9},{2,10},{3,11},{4,12},{5,13},{6,14},{7,15},{8,0},{9,1},... | collective-permute-start | bytes 393224 | tf_op jit(solution)/shard_map/ppermute | solution.py:279
  383.4 3.4 collective-permute-done.87
  390.6 5.7 %collective-permute-done.70 = bf16[4,2,8,1024]{3,2,0,1:T(8,128)(2,1)S(1)} collective-permute-done((bf16[4,2,8,1024]{3,2,0,1:T(8,128)(2,1)S(1)}, bf16[4,2,8,1024]{3,2,0,1:T(8,128)(2,1)S(1)}, u32[]{:S(2)}, u32[]{:S(2)}) %collective-permute-start.70) | collective-permute-done | bytes 131104 | tf_op jit(solution)/shard_map/ppermute | solution.py:279
  396.2 6.3 %collective-permute-start.116 = (f32[20,128]{1,0:T(8,128)S(1)}, f32[20,128]{1,0:T(8,128)S(1)}, u32[]{:S(2)}, u32[]{:S(2)}) collective-permute-start(f32[20,128]{1,0:T(8,128)S(1)} %fusion.49), channel_id=1, source_target_pairs={{0,2},{1,3},{2,0},{3,1},{4,6},{5,7},{6,4},{7,5},{8,10},{9,11},{10,... | collective-permute-start | bytes 30728 | tf_op jit(solution)/shard_map/ppermute | solution.py:279
  405.2 3.6 collective-permute-done.117
  413.2 3.6 collective-permute-done.75
  419.4 6.7 %collective-permute-done.89 = bf16[128,1024]{1,0:T(8,128)(2,1)S(1)} collective-permute-done((bf16[128,1024]{1,0:T(8,128)(2,1)S(1)}, bf16[128,1024]{1,0:T(8,128)(2,1)S(1)}, u32[]{:S(2)}, u32[]{:S(2)}) %collective-permute-start.89) | collective-permute-done | bytes 262176 | tf_op jit(solution)/shard_map/ppermute | solution.py:279
  430.9 9.3 %collective-permute-done.100 = bf16[160,1024]{1,0:T(8,128)(2,1)S(1)} collective-permute-done((bf16[160,1024]{1,0:T(8,128)(2,1)S(1)}, bf16[160,1024]{1,0:T(8,128)(2,1)S(1)}, u32[]{:S(2)}, u32[]{:S(2)}) %collective-permute-start.100) | collective-permute-done | bytes 327712 | tf_op jit(solution)/shard_map/ppermute | solution.py:279
  445.8 6.4 %collective-permute-done.109 = bf16[256,512]{1,0:T(8,128)(2,1)S(1)} collective-permute-done((bf16[256,512]{1,0:T(8,128)(2,1)S(1)}, bf16[256,512]{1,0:T(8,128)(2,1)S(1)}, u32[]{:S(2)}, u32[]{:S(2)}) %collective-permute-start.109) | collective-permute-done | bytes 262176 | tf_op jit(solution)/shard_map/ppermute | solution.py:279
  454.9 5.9 %collective-permute-done.77 = bf16[256,384]{1,0:T(8,128)(2,1)S(1)} collective-permute-done((bf16[256,384]{1,0:T(8,128)(2,1)S(1)}, bf16[256,384]{1,0:T(8,128)(2,1)S(1)}, u32[]{:S(2)}, u32[]{:S(2)}) %collective-permute-start.77) | collective-permute-done | bytes 196640 | tf_op jit(solution)/shard_map/ppermute | solution.py:279
  460.9 4.3 collective-permute-done.110
  481.8 4.5 collective-permute-done.104
  (622 shorter events, 249.0 us)
Async XLA Ops:
  5.6 69.1 %collective-permute-start.32 = (bf16[4,128,512]{2,1,0:T(8,128)(2,1)}, bf16[4,128,512]{2,1,0:T(8,128)(2,1)}, u32[]{:S(2)}, u32[]{:S(2)}) collective-permute-start(bf16[4,128,512]{2,1,0:T(8,128)(2,1)} %pad_maximum_fusion.11), channel_id=1, source_target_pairs={{0,1},{1,0},{2,3},{3,2},{4,5},{5,4},{6,7},{7,6},{8,9},{9,8},{10,11... | collective-permute-start | bytes 1572872 | tf_op jit(solution)/shard_map/ppermute | solution.py:279
  7.4 23.6 %collective-permute-start.18 = (bf16[8,8,1024]{2,1,0:T(8,128)(2,1)}, bf16[8,8,1024]{2,1,0:T(8,128)(2,1)}, u32[]{:S(2)}, u32[]{:S(2)}) collective-permute-start(bf16[8,8,1024]{2,1,0:T(8,128)(2,1)} %get-tuple-element.227), channel_id=1, source_target_pairs={{0,8},{1,9},{2,10},{3,11},{4,12},{5,13},{6,14},{7,15},{8,0},{9,1},... | collective-permute-start | bytes 393224 | tf_op jit(solution)/shard_map/ppermute | solution.py:279
  9.9 21.1 %collective-permute-start.19 = (bf16[8,8,1024]{2,1,0:T(8,128)(2,1)}, bf16[8,8,1024]{2,1,0:T(8,128)(2,1)}, u32[]{:S(2)}, u32[]{:S(2)}) collective-permute-start(bf16[8,8,1024]{2,1,0:T(8,128)(2,1)} %get-tuple-element.226), channel_id=1, source_target_pairs={{0,16},{1,17},{2,18},{3,19},{4,20},{5,21},{6,22},{7,23},{8,24},{9,... | collective-permute-start | bytes 393224 | tf_op jit(solution)/shard_map/ppermute | solution.py:279
  11.4 19.6 %collective-permute-start.20 = (bf16[8,8,1024]{2,1,0:T(8,128)(2,1)S(1)}, bf16[8,8,1024]{2,1,0:T(8,128)(2,1)}, u32[]{:S(2)}, u32[]{:S(2)}) collective-permute-start(bf16[8,8,1024]{2,1,0:T(8,128)(2,1)S(1)} %get-tuple-element.225), channel_id=1, source_target_pairs={{0,24},{1,25},{2,26},{3,27},{4,28},{5,29},{6,30},{7,31},{8,16},{9,... | collective-permute-start | bytes 393224 | tf_op jit(solution)/shard_map/ppermute | solution.py:279
  29.9 17.1 %collective-permute-start.4 = (bf16[4,128,384]{2,1,0:T(8,128)(2,1)S(1)}, bf16[4,128,384]{2,1,0:T(8,128)(2,1)S(1)}, u32[]{:S(2)}, u32[]{:S(2)}) collective-permute-start(bf16[4,128,384]{2,1,0:T(8,128)(2,1)S(1)} %pad_maximum_fusion.18), channel_id=1, source_target_pairs={{0,1},{1,0},{2,3},{3,2},{4,5},{5,4},{6,7},{7,6},{8,9},{9,8},{10,11... | collective-permute-start | bytes 1179656 | tf_op jit(solution)/shard_map/ppermute | solution.py:279
  58.5 17.6 %collective-permute-start = (bf16[256,1024]{1,0:T(8,128)(2,1)S(1)}, bf16[256,1024]{1,0:T(8,128)(2,1)S(1)}, u32[]{:S(2)}, u32[]{:S(2)}) collective-permute-start(bf16[256,1024]{1,0:T(8,128)(2,1)S(1)} %bitcast.307), channel_id=1, source_target_pairs={{0,1},{1,0},{2,3},{3,2},{4,5},{5,4},{6,7},{7,6},{8,9},{9,8},{10,11... | collective-permute-start | bytes 1572872 | tf_op jit(solution)/shard_map/ppermute | solution.py:279
  68.6 20.8 %collective-permute-start.7 = (bf16[256,512]{1,0:T(8,128)(2,1)S(1)}, bf16[256,512]{1,0:T(8,128)(2,1)S(1)}, u32[]{:S(2)}, u32[]{:S(2)}) collective-permute-start(bf16[256,512]{1,0:T(8,128)(2,1)S(1)} %collective-permute-done.6.refs_2_.refs_6_), channel_id=1, source_target_pairs={{0,2},{1,3},{2,4},{3,5},{4,6},{5,7},{6,0},{7,1},{8,10},{9,11},{10,... | collective-permute-start | bytes 786440 | tf_op jit(solution)/shard_map/ppermute | solution.py:279
  74.7 17.1 %collective-permute-start.30 = (bf16[4,2,8,1024]{3,2,1,0:T(8,128)(2,1)S(1)}, bf16[4,2,8,1024]{3,2,1,0:T(8,128)(2,1)S(1)}, u32[]{:S(2)}, u32[]{:S(2)}) collective-permute-start(bf16[4,2,8,1024]{3,2,1,0:T(8,128)(2,1)S(1)} %get-tuple-element.211), channel_id=1, source_target_pairs={{0,6},{1,7},{2,4},{3,5},{4,2},{5,3},{6,0},{7,1},{8,14},{9,15},{10,... | collective-permute-start | bytes 393224 | tf_op jit(solution)/shard_map/ppermute | solution.py:279
  76.1 17.3 %collective-permute-start.8 = (bf16[256,512]{1,0:T(8,128)(2,1)S(1)}, bf16[256,512]{1,0:T(8,128)(2,1)S(1)}, u32[]{:S(2)}, u32[]{:S(2)}) collective-permute-start(bf16[256,512]{1,0:T(8,128)(2,1)S(1)} %collective-permute-done.5.refs_1_.refs_5_), channel_id=1, source_target_pairs={{0,8},{1,9},{2,10},{3,11},{4,12},{5,13},{6,14},{7,15},{8,0},{9,1},... | collective-permute-start | bytes 786440 | tf_op jit(solution)/shard_map/ppermute | solution.py:279
  91.8 20.6 %collective-permute-start.11 = (bf16[256,512]{1,0:T(8,128)(2,1)S(1)}, bf16[256,512]{1,0:T(8,128)(2,1)S(1)}, u32[]{:S(2)}, u32[]{:S(2)}) collective-permute-start(bf16[256,512]{1,0:T(8,128)(2,1)S(1)} %collective-permute-done.5.refs_1_.refs_5_), channel_id=1, source_target_pairs={{0,16},{1,17},{2,18},{3,19},{4,20},{5,21},{6,22},{7,23},{8,24},{9,... | collective-permute-start | bytes 786440 | tf_op jit(solution)/shard_map/ppermute | solution.py:279
  93.4 24.8 %collective-permute-start.14 = (bf16[256,512]{1,0:T(8,128)(2,1)S(1)}, bf16[256,512]{1,0:T(8,128)(2,1)S(1)}, u32[]{:S(2)}, u32[]{:S(2)}) collective-permute-start(bf16[256,512]{1,0:T(8,128)(2,1)S(1)} %collective-permute-done.8.refs_1_.refs_9_), channel_id=1, source_target_pairs={{0,16},{1,17},{2,18},{3,19},{4,20},{5,21},{6,22},{7,23},{8,24},{9,... | collective-permute-start | bytes 786440 | tf_op jit(solution)/shard_map/ppermute | solution.py:279
  93.9 18.6 %collective-permute-start.13 = (bf16[256,512]{1,0:T(8,128)(2,1)S(1)}, bf16[256,512]{1,0:T(8,128)(2,1)S(1)}, u32[]{:S(2)}, u32[]{:S(2)}) collective-permute-start(bf16[256,512]{1,0:T(8,128)(2,1)S(1)} %collective-permute-done.7.refs_3_.refs_7_), channel_id=1, source_target_pairs={{0,16},{1,17},{2,18},{3,19},{4,20},{5,21},{6,22},{7,23},{8,24},{9,... | collective-permute-start | bytes 786440 | tf_op jit(solution)/shard_map/ppermute | solution.py:279
  97.2 21.2 %collective-permute-start.15 = (bf16[256,512]{1,0:T(8,128)(2,1)S(1)}, bf16[256,512]{1,0:T(8,128)(2,1)S(1)}, u32[]{:S(2)}, u32[]{:S(2)}) collective-permute-start(bf16[256,512]{1,0:T(8,128)(2,1)S(1)} %collective-permute-done.12.refs_2_.refs_14_), channel_id=1, source_target_pairs={{0,8},{1,9},{2,10},{3,11},{4,12},{5,13},{6,14},{7,15},{8,0},{9,1},... | collective-permute-start | bytes 786440 | tf_op jit(solution)/shard_map/ppermute | solution.py:279
  102.4 16.1 %collective-permute-start.16 = (bf16[256,512]{1,0:T(8,128)(2,1)S(1)}, bf16[256,512]{1,0:T(8,128)(2,1)S(1)}, u32[]{:S(2)}, u32[]{:S(2)}) collective-permute-start(bf16[256,512]{1,0:T(8,128)(2,1)S(1)} %collective-permute-done.10.refs_3_.refs_11_), channel_id=1, source_target_pairs={{0,16},{1,17},{2,18},{3,19},{4,20},{5,21},{6,22},{7,23},{8,24},{9,... | collective-permute-start | bytes 786440 | tf_op jit(solution)/shard_map/ppermute | solution.py:279
  112.5 38.9 %collective-permute-start.43 = (bf16[128,1024]{1,0:T(8,128)(2,1)}, bf16[128,1024]{1,0:T(8,128)(2,1)}, u32[]{:S(2)}, u32[]{:S(2)}) collective-permute-start(bf16[128,1024]{1,0:T(8,128)(2,1)} %collective-permute-done.42.refs_5_), channel_id=1, source_target_pairs={{0,8},{1,9},{2,10},{3,11},{4,12},{5,13},{6,14},{7,15},{8,0},{9,1},... | collective-permute-start | bytes 786440 | tf_op jit(solution)/shard_map/ppermute | solution.py:279
  123.8 21.7 %collective-permute-start.17 = (bf16[512,1024]{1,0:T(8,128)(2,1)}, bf16[512,1024]{1,0:T(8,128)(2,1)}, u32[]{:S(2)}, u32[]{:S(2)}) collective-permute-start(bf16[512,1024]{1,0:T(8,128)(2,1)} %get-tuple-element.68.part), channel_id=1, source_target_pairs={{0,1},{1,0},{2,3},{3,2},{4,5},{5,4},{6,7},{7,6},{8,9},{9,8},{10,11... | collective-permute-start | bytes 3145736 | tf_op jit(solution)/shard_map/ppermute | solution.py:279
  127.5 24.4 %collective-permute-start.53 = (bf16[128,1024]{1,0:T(8,128)(2,1)}, bf16[128,1024]{1,0:T(8,128)(2,1)}, u32[]{:S(2)}, u32[]{:S(2)}) collective-permute-start(bf16[128,1024]{1,0:T(8,128)(2,1)} %collective-permute-done.42.refs_5_), channel_id=1, source_target_pairs={{0,16},{1,17},{2,18},{3,19},{4,20},{5,21},{6,22},{7,23},{8,24},{9,... | collective-permute-start | bytes 786440 | tf_op jit(solution)/shard_map/ppermute | solution.py:279
  129.1 24.3 %collective-permute-start.48 = (bf16[128,1024]{1,0:T(8,128)(2,1)}, bf16[128,1024]{1,0:T(8,128)(2,1)}, u32[]{:S(2)}, u32[]{:S(2)}) collective-permute-start(bf16[128,1024]{1,0:T(8,128)(2,1)} %collective-permute-done.45.refs_6_), channel_id=1, source_target_pairs={{0,2},{1,3},{2,4},{3,5},{4,6},{5,7},{6,0},{7,1},{8,10},{9,11},{10,... | collective-permute-start | bytes 786440 | tf_op jit(solution)/shard_map/ppermute | solution.py:279
  153.9 18.7 %collective-permute-start.55 = (bf16[256,512]{1,0:T(8,128)(2,1)}, bf16[256,512]{1,0:T(8,128)(2,1)S(1)}, u32[]{:S(2)}, u32[]{:S(2)}) collective-permute-start(bf16[256,512]{1,0:T(8,128)(2,1)} %collective-permute-done.36.refs_2_), channel_id=1, source_target_pairs={{0,8},{1,9},{2,10},{3,11},{4,12},{5,13},{6,14},{7,15},{8,0},{9,1},... | collective-permute-start | bytes 786440 | tf_op jit(solution)/shard_map/ppermute | solution.py:279
  155.4 20.0 %collective-permute-start.40 = (bf16[256,512]{1,0:T(8,128)(2,1)}, bf16[256,512]{1,0:T(8,128)(2,1)S(1)}, u32[]{:S(2)}, u32[]{:S(2)}) collective-permute-start(bf16[256,512]{1,0:T(8,128)(2,1)} %collective-permute-done.39.refs_3_), channel_id=1, source_target_pairs={{0,8},{1,9},{2,10},{3,11},{4,12},{5,13},{6,14},{7,15},{8,0},{9,1},... | collective-permute-start | bytes 786440 | tf_op jit(solution)/shard_map/ppermute | solution.py:279
  163.6 22.1 %collective-permute-start.44 = (bf16[128,1024]{1,0:T(8,128)(2,1)}, bf16[128,1024]{1,0:T(8,128)(2,1)S(1)}, u32[]{:S(2)}, u32[]{:S(2)}) collective-permute-start(bf16[128,1024]{1,0:T(8,128)(2,1)} %collective-permute-done.43.refs_5_), channel_id=1, source_target_pairs={{0,16},{1,17},{2,18},{3,19},{4,20},{5,21},{6,22},{7,23},{8,24},{9,... | collective-permute-start | bytes 786440 | tf_op jit(solution)/shard_map/ppermute | solution.py:279
  164.9 22.3 %collective-permute-start.51 = (bf16[256,512]{1,0:T(8,128)(2,1)}, bf16[256,512]{1,0:T(8,128)(2,1)S(1)}, u32[]{:S(2)}, u32[]{:S(2)}) collective-permute-start(bf16[256,512]{1,0:T(8,128)(2,1)} %collective-permute-done.33.refs_1_), channel_id=1, source_target_pairs={{0,16},{1,17},{2,18},{3,19},{4,20},{5,21},{6,22},{7,23},{8,24},{9,... | collective-permute-start | bytes 786440 | tf_op jit(solution)/shard_map/ppermute | solution.py:279
  167.0 20.8 %collective-permute-start.54 = (bf16[128,1024]{1,0:T(8,128)(2,1)}, bf16[128,1024]{1,0:T(8,128)(2,1)S(1)}, u32[]{:S(2)}, u32[]{:S(2)}) collective-permute-start(bf16[128,1024]{1,0:T(8,128)(2,1)} %collective-permute-done.48.refs_7_), channel_id=1, source_target_pairs={{0,16},{1,17},{2,18},{3,19},{4,20},{5,21},{6,22},{7,23},{8,24},{9,... | collective-permute-start | bytes 786440 | tf_op jit(solution)/shard_map/ppermute | solution.py:279
  172.6 17.4 %collective-permute-start.37 = (bf16[256,512]{1,0:T(8,128)(2,1)}, bf16[256,512]{1,0:T(8,128)(2,1)S(1)}, u32[]{:S(2)}, u32[]{:S(2)}) collective-permute-start(bf16[256,512]{1,0:T(8,128)(2,1)} %collective-permute-done.36.refs_2_), channel_id=1, source_target_pairs={{0,16},{1,17},{2,18},{3,19},{4,20},{5,21},{6,22},{7,23},{8,24},{9,... | collective-permute-start | bytes 786440 | tf_op jit(solution)/shard_map/ppermute | solution.py:279
  175.5 20.1 %collective-permute-start.52 = (bf16[256,512]{1,0:T(8,128)(2,1)}, bf16[256,512]{1,0:T(8,128)(2,1)S(1)}, u32[]{:S(2)}, u32[]{:S(2)}) collective-permute-start(bf16[256,512]{1,0:T(8,128)(2,1)} %collective-permute-done.39.refs_3_), channel_id=1, source_target_pairs={{0,16},{1,17},{2,18},{3,19},{4,20},{5,21},{6,22},{7,23},{8,24},{9,... | collective-permute-start | bytes 786440 | tf_op jit(solution)/shard_map/ppermute | solution.py:279
  185.7 20.4 %collective-permute-start.47 = (bf16[128,1024]{1,0:T(8,128)(2,1)S(1)}, bf16[128,1024]{1,0:T(8,128)(2,1)S(1)}, u32[]{:S(2)}, u32[]{:S(2)}) collective-permute-start(bf16[128,1024]{1,0:T(8,128)(2,1)S(1)} %collective-permute-done.46.refs_6_), channel_id=1, source_target_pairs={{0,8},{1,9},{2,10},{3,11},{4,12},{5,13},{6,14},{7,15},{8,0},{9,1},... | collective-permute-start | bytes 786440 | tf_op jit(solution)/shard_map/ppermute | solution.py:279
  187.2 18.8 %collective-permute-start.35 = (bf16[256,512]{1,0:T(8,128)(2,1)S(1)}, bf16[256,512]{1,0:T(8,128)(2,1)S(1)}, u32[]{:S(2)}, u32[]{:S(2)}) collective-permute-start(bf16[256,512]{1,0:T(8,128)(2,1)S(1)} %collective-permute-done.34.refs_1_), channel_id=1, source_target_pairs={{0,16},{1,17},{2,18},{3,19},{4,20},{5,21},{6,22},{7,23},{8,24},{9,... | collective-permute-start | bytes 786440 | tf_op jit(solution)/shard_map/ppermute | solution.py:279
  187.7 18.5 %collective-permute-start.50 = (bf16[128,1024]{1,0:T(8,128)(2,1)S(1)}, bf16[128,1024]{1,0:T(8,128)(2,1)S(1)}, u32[]{:S(2)}, u32[]{:S(2)}) collective-permute-start(bf16[128,1024]{1,0:T(8,128)(2,1)S(1)} %collective-permute-done.49.refs_7_), channel_id=1, source_target_pairs={{0,16},{1,17},{2,18},{3,19},{4,20},{5,21},{6,22},{7,23},{8,24},{9,... | collective-permute-start | bytes 786440 | tf_op jit(solution)/shard_map/ppermute | solution.py:279
  190.0 16.3 %collective-permute-start.38 = (bf16[256,512]{1,0:T(8,128)(2,1)S(1)}, bf16[256,512]{1,0:T(8,128)(2,1)S(1)}, u32[]{:S(2)}, u32[]{:S(2)}) collective-permute-start(bf16[256,512]{1,0:T(8,128)(2,1)S(1)} %collective-permute-done.37.refs_2_), channel_id=1, source_target_pairs={{0,8},{1,9},{2,10},{3,11},{4,12},{5,13},{6,14},{7,15},{8,0},{9,1},... | collective-permute-start | bytes 786440 | tf_op jit(solution)/shard_map/ppermute | solution.py:279
  231.7 90.4 %collective-permute-start.72 = (bf16[512,1024]{1,0:T(8,128)(2,1)S(1)}, bf16[512,1024]{1,0:T(8,128)(2,1)S(1)}, u32[]{:S(2)}, u32[]{:S(2)}) collective-permute-start(bf16[512,1024]{1,0:T(8,128)(2,1)S(1)} %convert_element_type.381), channel_id=1, source_target_pairs={{0,1},{1,0},{2,3},{3,2},{4,5},{5,4},{6,7},{7,6},{8,9},{9,8},{10,11... | collective-permute-start | bytes 3145736 | tf_op jit(solution)/shard_map/ppermute | solution.py:279
  231.8 136.8 %collective-permute-start.105 = (bf16[4,256,512]{2,1,0:T(8,128)(2,1)}, bf16[4,256,512]{2,1,0:T(8,128)(2,1)}, u32[]{:S(2)}, u32[]{:S(2)}) collective-permute-start(bf16[4,256,512]{2,1,0:T(8,128)(2,1)} %get-tuple-element.109), channel_id=1, source_target_pairs={{0,8},{1,9},{2,10},{3,11},{4,12},{5,13},{6,14},{7,15},{8,0},{9,1},... | collective-permute-start | bytes 3145736 | tf_op jit(solution)/shard_map/ppermute | solution.py:279
  235.5 19.3 %collective-permute-start.94 = (bf16[128,1024]{1,0:T(8,128)(2,1)S(1)}, bf16[128,1024]{1,0:T(8,128)(2,1)S(1)}, u32[]{:S(2)}, u32[]{:S(2)}) collective-permute-start(bf16[128,1024]{1,0:T(8,128)(2,1)S(1)} %slice_bitcast_fusion.11), channel_id=1, source_target_pairs={{0,2},{1,3},{2,4},{3,5},{4,6},{5,7},{6,0},{7,1},{8,10},{9,11},{10,... | collective-permute-start | bytes 786440 | tf_op jit(solution)/shard_map/ppermute | solution.py:279
  243.6 16.9 %collective-permute-start.97 = (bf16[128,1024]{1,0:T(8,128)(2,1)S(1)}, bf16[128,1024]{1,0:T(8,128)(2,1)S(1)}, u32[]{:S(2)}, u32[]{:S(2)}) collective-permute-start(bf16[128,1024]{1,0:T(8,128)(2,1)S(1)} %slice_bitcast_fusion.10), channel_id=1, source_target_pairs={{0,2},{1,3},{2,4},{3,5},{4,6},{5,7},{6,0},{7,1},{8,10},{9,11},{10,... | collective-permute-start | bytes 786440 | tf_op jit(solution)/shard_map/ppermute | solution.py:279
  249.2 17.4 %collective-permute-start.57 = (bf16[256,1024]{1,0:T(8,128)(2,1)S(1)}, bf16[256,1024]{1,0:T(8,128)(2,1)S(1)}, u32[]{:S(2)}, u32[]{:S(2)}) collective-permute-start(bf16[256,1024]{1,0:T(8,128)(2,1)S(1)} %slice.619), channel_id=1, source_target_pairs={{0,1},{1,0},{2,3},{3,2},{4,5},{5,4},{6,7},{7,6},{8,9},{9,8},{10,11... | collective-permute-start | bytes 1572872 | tf_op jit(solution)/shard_map/ppermute | solution.py:279
  284.2 16.3 %collective-permute-start.92 = (bf16[128,1024]{1,0:T(8,128)(2,1)S(1)}, bf16[128,1024]{1,0:T(8,128)(2,1)S(1)}, u32[]{:S(2)}, u32[]{:S(2)}) collective-permute-start(bf16[128,1024]{1,0:T(8,128)(2,1)S(1)} %fusion.11), channel_id=1, source_target_pairs={{0,2},{1,3},{2,4},{3,5},{4,6},{5,7},{6,0},{7,1},{8,10},{9,11},{10,... | collective-permute-start | bytes 786440 | tf_op jit(solution)/shard_map/ppermute | solution.py:279
  288.1 16.4 %collective-permute-start.61 = (bf16[4,2,8,1024]{3,2,0,1:T(8,128)(2,1)S(1)}, bf16[4,2,8,1024]{3,2,0,1:T(8,128)(2,1)S(1)}, u32[]{:S(2)}, u32[]{:S(2)}) collective-permute-start(bf16[4,2,8,1024]{3,2,0,1:T(8,128)(2,1)S(1)} %get-tuple-element.197), channel_id=1, source_target_pairs={{0,2},{1,3},{2,0},{3,1},{4,6},{5,7},{6,4},{7,5},{8,10},{9,11},{10,... | collective-permute-start | bytes 393224 | tf_op jit(solution)/shard_map/ppermute | solution.py:279
  304.5 121.7 %collective-permute-start.107 = (bf16[4,256,512]{2,1,0:T(8,128)(2,1)}, bf16[4,256,512]{2,1,0:T(8,128)(2,1)}, u32[]{:S(2)}, u32[]{:S(2)}) collective-permute-start(bf16[4,256,512]{2,1,0:T(8,128)(2,1)} %get-tuple-element.110), channel_id=1, source_target_pairs={{0,8},{1,9},{2,10},{3,11},{4,12},{5,13},{6,14},{7,15},{8,0},{9,1},... | collective-permute-start | bytes 3145736 | tf_op jit(solution)/shard_map/ppermute | solution.py:279
  318.4 42.7 %collective-permute-start.64 = (bf16[4,4,8,1024]{3,2,1,0:T(8,128)(2,1)}, bf16[4,4,8,1024]{3,2,1,0:T(8,128)(2,1)}, u32[]{:S(2)}, u32[]{:S(2)}) collective-permute-start(bf16[4,4,8,1024]{3,2,1,0:T(8,128)(2,1)} %get-tuple-element.193), channel_id=1, source_target_pairs={{0,1},{1,0},{2,3},{3,2},{4,5},{5,4},{6,7},{7,6},{8,9},{9,8},{10,11... | collective-permute-start | bytes 786440 | tf_op jit(solution)/shard_map/ppermute | solution.py:279
  361.2 18.9 %collective-permute-start.73 = (bf16[256,1024]{1,0:T(8,128)(2,1)S(1)}, bf16[256,1024]{1,0:T(8,128)(2,1)S(1)}, u32[]{:S(2)}, u32[]{:S(2)}) collective-permute-start(bf16[256,1024]{1,0:T(8,128)(2,1)S(1)} %get-tuple-element.95), channel_id=1, source_target_pairs={{0,1},{1,0},{2,3},{3,2},{4,5},{5,4},{6,7},{7,6},{8,9},{9,8},{10,11... | collective-permute-start | bytes 1572872 | tf_op jit(solution)/shard_map/ppermute | solution.py:279
  372.8 55.5 %collective-permute-start.106 = (bf16[4,256,512]{2,1,0:T(8,128)(2,1)S(1)}, bf16[4,256,512]{2,1,0:T(8,128)(2,1)S(1)}, u32[]{:S(2)}, u32[]{:S(2)}) collective-permute-start(bf16[4,256,512]{2,1,0:T(8,128)(2,1)S(1)} %add_convert_fusion.2), channel_id=1, source_target_pairs={{0,16},{1,17},{2,18},{3,19},{4,20},{5,21},{6,22},{7,23},{8,24},{9,... | collective-permute-start | bytes 3145736 | tf_op jit(solution)/shard_map/ppermute | solution.py:279
  388.9 27.8 %collective-permute-start.75 = (bf16[4,256,384]{2,1,0:T(8,128)(2,1)S(1)}, bf16[4,256,384]{2,1,0:T(8,128)(2,1)S(1)}, u32[]{:S(2)}, u32[]{:S(2)}) collective-permute-start(bf16[4,256,384]{2,1,0:T(8,128)(2,1)S(1)} %copy-done.55), channel_id=1, source_target_pairs={{0,16},{1,17},{2,18},{3,19},{4,20},{5,21},{6,22},{7,23},{8,24},{9,... | collective-permute-start | bytes 2359304 | tf_op jit(solution)/shard_map/ppermute | solution.py:279
  390.6 18.8 %collective-permute-start.88 = (bf16[128,1024]{1,0:T(8,128)(2,1)S(1)}, bf16[128,1024]{1,0:T(8,128)(2,1)S(1)}, u32[]{:S(2)}, u32[]{:S(2)}) collective-permute-start(bf16[128,1024]{1,0:T(8,128)(2,1)S(1)} %fusion.15), channel_id=1, source_target_pairs={{0,2},{1,3},{2,4},{3,5},{4,6},{5,7},{6,0},{7,1},{8,10},{9,11},{10,... | collective-permute-start | bytes 786440 | tf_op jit(solution)/shard_map/ppermute | solution.py:279
  408.8 33.7 %collective-permute-start.74 = (bf16[4,256,384]{2,1,0:T(8,128)(2,1)S(1)}, bf16[4,256,384]{2,1,0:T(8,128)(2,1)S(1)}, u32[]{:S(2)}, u32[]{:S(2)}) collective-permute-start(bf16[4,256,384]{2,1,0:T(8,128)(2,1)S(1)} %copy-done.53), channel_id=1, source_target_pairs={{0,16},{1,17},{2,18},{3,19},{4,20},{5,21},{6,22},{7,23},{8,24},{9,... | collective-permute-start | bytes 2359304 | tf_op jit(solution)/shard_map/ppermute | solution.py:279
  413.1 55.6 %collective-permute-start.71 = (bf16[4,4,8,1024]{3,2,1,0:T(8,128)(2,1)S(1)}, bf16[4,4,8,1024]{3,2,1,0:T(8,128)(2,1)S(1)}, u32[]{:S(2)}, u32[]{:S(2)}) collective-permute-start(bf16[4,4,8,1024]{3,2,1,0:T(8,128)(2,1)S(1)} %get-tuple-element.183), channel_id=1, source_target_pairs={{0,1},{1,0},{2,3},{3,2},{4,5},{5,4},{6,7},{7,6},{8,9},{9,8},{10,11... | collective-permute-start | bytes 786440 | tf_op jit(solution)/shard_map/ppermute | solution.py:279
  426.1 17.9 %collective-permute-start.76 = (bf16[4,256,384]{2,1,0:T(8,128)(2,1)S(1)}, bf16[4,256,384]{2,1,0:T(8,128)(2,1)S(1)}, u32[]{:S(2)}, u32[]{:S(2)}) collective-permute-start(bf16[4,256,384]{2,1,0:T(8,128)(2,1)S(1)} %add_convert_fusion.4), channel_id=1, source_target_pairs={{0,8},{1,9},{2,10},{3,11},{4,12},{5,13},{6,14},{7,15},{8,0},{9,1},... | collective-permute-start | bytes 2359304 | tf_op jit(solution)/shard_map/ppermute | solution.py:279
  440.2 30.0 %collective-permute-start.119 = (f32[20,128]{1,0:T(8,128)S(1)}, f32[20,128]{1,0:T(8,128)S(1)}, u32[]{:S(2)}, u32[]{:S(2)}) collective-permute-start(f32[20,128]{1,0:T(8,128)S(1)} %add.672), channel_id=1, source_target_pairs={{0,16},{1,17},{2,18},{3,19},{4,20},{5,21},{6,22},{7,23},{8,24},{9,... | collective-permute-start | bytes 30728 | tf_op jit(solution)/shard_map/ppermute | solution.py:279
  453.1 20.1 %collective-permute-start.103 = (bf16[160,1024]{1,0:T(8,128)(2,1)S(1)}, bf16[160,1024]{1,0:T(8,128)(2,1)S(1)}, u32[]{:S(2)}, u32[]{:S(2)}) collective-permute-start(bf16[160,1024]{1,0:T(8,128)(2,1)S(1)} %add_convert_fusion.6), channel_id=1, source_target_pairs={{0,16},{1,17},{2,18},{3,19},{4,20},{5,21},{6,22},{7,23},{8,24},{9,... | collective-permute-start | bytes 983048 | tf_op jit(solution)/shard_map/ppermute | solution.py:279
  473.3 16.2 %collective-permute-start.112 = (bf16[256,512]{1,0:T(8,128)(2,1)S(1)}, bf16[256,512]{1,0:T(8,128)(2,1)}, u32[]{:S(2)}, u32[]{:S(2)}) collective-permute-start(bf16[256,512]{1,0:T(8,128)(2,1)S(1)} %fusion.1), channel_id=1, source_target_pairs={{0,16},{1,17},{2,18},{3,19},{4,20},{5,21},{6,22},{7,23},{8,24},{9,... | collective-permute-start | bytes 786440 | tf_op jit(solution)/shard_map/ppermute | solution.py:279
  (190 other events, 2231.3 us)

commit v2 on v0

v2 whole, which is shorter than its diff:
```python
import functools

import jax
import jax.numpy as jnp
from jax import lax
from jax.experimental import pallas as pl
from jax.experimental.pallas import tpu as pltpu
from jax.sharding import PartitionSpec as P

EPSILON = 1e-06
MASKED = -1000000000.0
AXES = ("rep", "shard")
BF16 = jnp.bfloat16
F32 = jnp.float32
INV_SQRT2 = 0.7071067811865476
INV_SQRT2PI = 0.3989422804014327
PAD = 16

VMEM = pl.BlockSpec(memory_space=pltpu.VMEM)
SMEM = pl.BlockSpec(memory_space=pltpu.SMEM)
ANY = pl.BlockSpec(memory_space=pl.ANY)
HBM = pl.BlockSpec(memory_space=pltpu.HBM)


def shaped(shape, dtype=BF16):
    return jax.ShapeDtypeStruct(shape, dtype)


def kept(shape, dtype=BF16):
    return pltpu.VMEM(shape, dtype)


def stored(shape, dtype=BF16):
    return pltpu.HBM(shape, dtype)


class Sequence:
    def __init__(self):
        self.last = None

    def __call__(self, body, outs, *args, scalars=0, hbm=0, scratch=(), limit=12, after=()):
        n = len(args)
        args = [pltpu.with_memory_space_constraint(a, pltpu.HBM) if i >= n - hbm else a for i, a in enumerate(args)]
        specs = [SMEM] * scalars + [VMEM] * (n - scalars - hbm) + [HBM] * hbm
        extra = list(after) + ([] if self.last is None else [self.last])
        m = len(extra)

        def run(*refs):
            body(*refs[:n], *refs[n + m :])

        result = pl.pallas_call(
            run,
            out_shape=outs,
            in_specs=specs + [ANY] * m,
            out_specs=[VMEM] * len(outs),
            scratch_shapes=list(scratch),
            cost_estimate=pl.CostEstimate(flops=0, bytes_accessed=0, transcendentals=0),
            compiler_params=pltpu.CompilerParams(vmem_limit_bytes=limit * 1024 * 1024),
        )(*args, *extra)
        self.last = result[-1]
        return result

    def arrived(self, value):
        self(token_kernel, [kept((8, 128), F32)], after=[value], limit=4)


def dot(a, b):
    return jnp.dot(a, b, preferred_element_type=F32)


def dot_nt(a, b):
    return lax.dot_general(a, b, (((1,), (1,)), ((), ())), preferred_element_type=F32)


def dot_tn(a, b):
    return lax.dot_general(a, b, (((0,), (0,)), ((), ())), preferred_element_type=F32)


def lanes(block, size):
    return pl.ds(pl.multiple_of(block * size, size), size)


class Geometry:
    def __init__(self, rs, zs, hb, fb, heads, seq_len, width):
        self.rs, self.zs, self.hb, self.fb = rs, zs, hb, fb
        self.seq_len, self.width = seq_len, width
        self.tokens = 2 * seq_len
        self.bits = rs.bit_length() - 1
        self.sub = fb // rs
        self.cols = zs * self.sub
        self.hd = width // heads
        self.nh = hb // self.hd
        self.chips = rs * zs
        self.rows = seq_len // self.chips
        self.aligned = hb % 128 == 0 and self.sub % 128 == 0
        self.parts = width // self.cols

    def turned(self, m):
        out = 0
        for b in range(self.bits):
            out = out + (((m >> b) & 1) << (self.bits - 1 - b))
        return out

    def here(self):
        return Here(self)


class Here:
    def __init__(self, g):
        self.g = g
        self.r = lax.axis_index("rep").astype(jnp.int32)
        c = lax.axis_index("shard").astype(jnp.int32)
        self.z = lax.div(c, jnp.int32(2))
        self.k = lax.rem(c, jnp.int32(2))
        self.me = self.r * (2 * g.zs) + c

    def code(self, m, k=None):
        k = self.k if k is None else k
        return m + k * (self.g.turned(m) - m)

    def quarter(self, m):
        return self.r if m == 0 else lax.bitwise_xor(self.r, self.code(jnp.int32(m)))

    def behind(self, j):
        return self.z if j == 0 else lax.rem(self.z + (self.g.zs - j), jnp.int32(self.g.zs))

    def shard(self, j, h):
        return 2 * self.behind(j) + (1 - self.k if h else self.k)


class Box:
    pass


class Copies:
    def __init__(self, sem):
        self.sem, self.all = sem, []

    def start(self, src, dst):
        copy = pltpu.make_async_copy(src, dst, self.sem)
        copy.start()
        self.all.append(copy)

    def wait(self):
        for copy in self.all:
            copy.wait()


def fetch_heads(g, at, copies, s, core, weights, dst, row):
    hb = g.hb
    for i, w in enumerate(weights):
        part = dst.at[pl.ds(row, hb), pl.ds(i * hb, hb)]
        copies.start(w.at[:, lanes(2 * s + core, hb)], part)


def fetch_inner(g, at, copies, s, core, wi, dst, row, col):
    hb, sub = g.hb, g.sub
    for b in range(g.zs):
        place = pl.ds(pl.multiple_of((2 * b + core) * g.fb + s * sub, sub), sub)
        copies.start(wi.at[:, place], dst.at[pl.ds(row, hb), pl.ds(col + b * sub, sub)])


def send_prep_kernel(g, wq, wk, wv, wi, out, sem):
    at, hb = g.here(), g.hb
    copies, other = Copies(sem), 1 - at.k
    for m in range(g.rs):
        s = lax.bitwise_xor(at.r, at.code(jnp.int32(m), other))
        fetch_heads(g, at, copies, s, other, (wq, wk, wv), out, m * hb)
        fetch_inner(g, at, copies, s, other, wi, out, m * hb, 3 * hb)
    copies.wait()


def attn_prep_kernel(g, small, other, got, wq, wk, wv, wm, out, sem):
    at, hb = g.here(), g.hb
    copies = Copies(sem)
    fetch_heads(g, at, copies, at.r, at.k, (wq, wk, wv), out, 0)
    for h in range(2):
        part = out.at[pl.ds(h * hb, hb), pl.ds(3 * hb, hb)]
        copies.start(wm.at[:, lanes(2 * at.r + h, hb)], part)
    out[hb : 2 * hb, : 3 * hb] = got[:hb, : 3 * hb]
    row = lax.broadcasted_iota(jnp.int32, (PAD, 4 * hb), 0)
    theirs = pltpu.roll(other[...].astype(F32), 1, 0)
    out[2 * hb :, :] = jnp.where(row == 0, small[...].astype(F32), theirs).astype(BF16)
    copies.wait()


def ffn_prep_kernel(g, got, wi, wu, out, sem):
    at, hb, sub, cols = g.here(), g.hb, g.sub, g.cols
    copies = Copies(sem)
    fetch_inner(g, at, copies, at.r, at.k, wi, out, 0, 0)
    for i in range(g.parts):
        part = out.at[pl.ds(2 * hb + i * sub, sub), :]
        copies.start(wu.at[lanes(at.r, sub), pl.ds(i * cols, cols)], part)
    out[hb : 2 * hb, :] = got[:hb, 3 * hb :]
    copies.wait()


def stack_kernel(rows, *refs):
    *ins, out = refs
    for i, ref in enumerate(ins):
        out[i] = ref[:rows, :]


def token_kernel(out):
    out[...] = jnp.zeros_like(out)


def deal_first_kernel(g, labels, src, *outs):
    at = g.here()
    for out, some in zip(outs, labels):
        for i, (f, zz) in enumerate(some):
            chip = lax.bitwise_xor(at.r, at.code(jnp.int32(f))) * g.zs
            out[i] = src[chip + lax.bitwise_xor(at.z, zz)]


def deal_stage_kernel(places, n_in, *refs):
    ins, outs = refs[:n_in], refs[n_in:]
    for out, some in zip(outs, places):
        for i, (a, b) in enumerate(some):
            out[i] = ins[a][b]


def deal_middle_kernel(g, labels, back, table, own, got, *refs):
    outs, (lookup,) = refs[:-1], refs[-1:]
    at = g.here()
    if back:
        for s in range(2 * g.chips):
            lookup[table[s]] = jnp.int32(s)
    else:
        lookup = table
    for out, some in zip(outs, labels):
        for i, (f, zz) in enumerate(some):
            chip = lax.bitwise_xor(at.r, at.code(jnp.int32(f))) * g.zs
            dest = (chip + lax.bitwise_xor(at.z, zz)) * 2 + at.k
            src = lookup[dest]
            core = lax.rem(src, 2)
            src = lax.div(src, 2)
            sz, sr = lax.rem(src, g.zs), lax.div(src, g.zs)
            sf = at.code(lax.bitwise_xor(at.r, sr), core)
            place = sf * g.zs + lax.bitwise_xor(at.z, sz)
            mine = own[place].astype(F32)
            theirs = got[place].astype(F32)
            out[i] = jnp.where(core == at.k, mine, theirs).astype(BF16)


def deal_last_kernel(g, places, n_in, masked, lengths, *refs):
    ins, (out, pool) = refs[:n_in], refs[n_in:]
    at = g.here()
    for e, (a, b) in enumerate(places):
        pool[e] = ins[a][b]
    for chip in range(g.chips):
        f = at.code(lax.bitwise_xor(at.r, chip // g.zs))
        value = pool[f * g.zs + lax.bitwise_xor(at.z, chip % g.zs)]
        if masked:
            row = lax.broadcasted_iota(jnp.int32, value.shape, 0) + chip * g.rows
            value = jnp.where(row < lengths[at.me], value.astype(F32), 0.0).astype(BF16)
        out[chip] = value


def sum_kernel(picks, *refs):
    *ins, out = refs
    total = None
    for ref, pick in zip(ins, picks):
        v = (ref[...] if pick is None else ref[pick]).astype(F32)
        total = v if total is None else total + v
    out[...] = total.astype(out.dtype)


def cut_sum_kernel(g, *refs):
    n = len(refs) - g.zs
    for j, out in enumerate(refs[n:]):
        out[...] = sum(ref[j].astype(F32) for ref in refs[:n]).astype(BF16)


def outer_end_kernel(g, *refs):
    half, sub = g.rs // 2, g.sub
    outs = refs[-2:]
    for i in range(2):
        own, got = refs[2 * i : 2 * i + 2]
        for c in range(half):
            m = i * half + c
            rows = slice(c * sub, (c + 1) * sub)
            v = own[rows, :].astype(F32) + got[rows, :].astype(F32)
            outs[m % 2][m // 2] = v.astype(BF16)


def outer_pair_kernel(g, keep, got, *outs):
    for i, out in enumerate(outs):
        out[...] = (keep[i].astype(F32) + got[i].astype(F32)).astype(BF16)


def inner_split_kernel(g, *refs):
    *ins, keep, give = refs
    total = sum(ref[...].astype(F32) for ref in ins).astype(BF16)
    keep[...] = total[: g.hb]
    give[...] = total[g.hb :]


def ffn_pack_kernel(g, keep, got, *refs):
    *ins, out = refs
    first = g.here().k == 0
    hb, sub = g.hb, g.sub
    for b in range(g.zs):
        cols = slice(b * sub, (b + 1) * sub)
        mine, theirs = keep[:, cols].astype(F32), got[:, cols].astype(F32)
        out[:hb, 2 * b * sub : (2 * b + 1) * sub] = jnp.where(first, mine, theirs).astype(BF16)
        out[:hb, (2 * b + 1) * sub : (2 * b + 2) * sub] = jnp.where(first, theirs, mine).astype(BF16)
    out[hb:, :] = sum(ref[...].astype(F32) for ref in ins).astype(BF16)


def ffn_end_kernel(g, *refs):
    at, parts, (inner, outer) = g.here(), refs[: g.rs], refs[g.rs :]
    hb, sub = g.hb, g.sub
    for m in range(g.rs):
        s = at.quarter(m)
        outer[lanes(s, sub), :] = parts[m][hb:, :].astype(F32)
        if g.aligned:
            for b in range(2 * g.zs):
                place = pl.ds(pl.multiple_of(b * g.fb + s * sub, sub), sub)
                inner[:, place] = parts[m][:hb, b * sub : (b + 1) * sub].astype(F32)
        else:
            inner[s] = parts[m][:hb, : 2 * g.zs * sub].astype(F32)


def attn_split_kernel(g, *refs):
    *ins, keep, mixer, give = refs
    hb = g.hb
    total = sum(ref[...].astype(F32) for ref in ins).astype(BF16)
    keep[:hb, :] = total[:hb, : 3 * hb]
    keep[hb:, :] = total[2 * hb :, : 3 * hb]
    mixer[:, :hb] = total[:hb, 3 * hb :]
    mixer[:, hb:] = total[hb : 2 * hb, 3 * hb :]
    give[:hb, :] = total[hb : 2 * hb, : 3 * hb]
    give[hb:, :] = total[2 * hb :, : 3 * hb]


def attn_pack_kernel(g, keep, mixer, got, out):
    first = g.here().k == 0
    hb = g.hb
    for b in range(3):
        cols = slice(b * hb, (b + 1) * hb)
        mine, theirs = keep[:, cols].astype(F32), got[:, cols].astype(F32)
        out[:, 2 * b * hb : (2 * b + 1) * hb] = jnp.where(first, mine, theirs).astype(BF16)
        out[:, (2 * b + 1) * hb : (2 * b + 2) * hb] = jnp.where(first, theirs, mine).astype(BF16)
    out[:hb, 6 * hb :] = mixer[...]
    out[hb:, 6 * hb :] = jnp.zeros((PAD, 2 * hb), BF16)


def attn_end_kernel(g, *refs):
    at, parts, outs = g.here(), refs[: g.rs], refs[g.rs :]
    hb, size = g.hb, 2 * g.hb
    gains, table = outs[4:]
    total = None
    for m in range(g.rs):
        q = at.quarter(m)
        for i in range(4):
            outs[i][:, lanes(q, size)] = parts[m][:hb, size * i : size * (i + 1)].astype(F32)
        tiles = parts[m][hb:, :].astype(F32)
        pair = []
        for core in range(2):
            both = [tiles[:, (2 * b + core) * hb : (2 * b + core + 1) * hb] for b in range(3)]
            for i in range(g.nh):
                head = (2 * q + core) * g.nh + i
                table[pl.ds(head, 1), :] = both[2][2 + i : 3 + i, :]
            pair.append(both)
        own = [jnp.where(at.k == 0, pair[0][b][0:1], pair[1][b][0:1]) for b in range(2)]
        their = [jnp.where(at.k == 0, pair[1][b][1:2], pair[0][b][1:2]) for b in range(2)]
        some = [own[b] + their[b] for b in range(2)]
        total = some if total is None else [total[b] + some[b] for b in range(2)]
    for b in range(2):
        gains[b : b + 1, :] = total[b]


def to_relative(g, at, src, dst):
    hb = g.hb
    for j in range(g.zs):
        for h in range(2):
            e = 2 * j + h
            dst[:, e * hb : (e + 1) * hb] = src[:, lanes(at.shard(j, h), hb)]


def norm_kernel(g, own, sib, gain, normed, normed_t, scaled, *scratch):
    half = own.shape[0]
    plain, plain_scaled = scratch if g.aligned else (normed, scaled)
    for start, src in ((0, own), (half, sib)):
        v = src[...].astype(F32)
        scale = lax.rsqrt(jnp.mean(v * v, axis=-1, keepdims=True) + EPSILON)
        plain[start : start + half, :] = (v * scale * gain[...]).astype(BF16)
        plain_scaled[start : start + half, :] = (v * scale).astype(BF16)
    if g.aligned:
        to_relative(g, g.here(), plain, normed)
        to_relative(g, g.here(), plain_scaled, scaled)
    normed_t[...] = normed[...].T


def toeplitz(row, n):
    wide = jnp.broadcast_to(row, (n, 2 * n))
    return pltpu.roll(wide, n + 1, 1, stride=1, stride_axis=0)[:, :n]


def probabilities(q, kk, bias, length):
    n = q.shape[0]
    s = dot_nt(q, kk) + bias
    col = lax.broadcasted_iota(jnp.int32, (n, n), 1)
    s = jnp.where(col < length, s, MASKED)
    e = jnp.exp(s - jnp.max(s, axis=-1, keepdims=True))
    return e * (1.0 / jnp.sum(e, axis=-1, keepdims=True))


def two_lengths(at, lengths):
    return lengths[at.me], lengths[lax.bitwise_xor(at.me, 1)]


def attn_kernel(g, m, lengths, normed, off, first, rest, *refs):
    hb, hd = g.hb, g.hd
    at = g.here()
    both = two_lengths(at, lengths)
    if m == 0 or not g.aligned:
        qkv, mixed, w = refs
        w[: 2 * hb, :] = first[: 2 * hb, : 3 * hb]
        copies = None
    else:
        weights, (qkv, mixed, w, sem) = refs[:3], refs[3:]
        copies = Copies(sem)
        fetch_heads(g, at, copies, at.quarter(m), at.k, weights, w, 0)
        w[hb : 2 * hb, :] = first[m * hb : (m + 1) * hb, : 3 * hb]
    for j in range(1, g.zs):
        w[2 * hb * j : 2 * hb * (j + 1), :] = rest[j - 1, :, : 3 * hb]
    if copies is not None:
        copies.wait()
    qkv[...] = dot(normed[...], w[...]).astype(BF16)
    half = normed.shape[0] // 2
    for h in range(g.nh):
        bias = toeplitz(off[h : h + 1, :], half)
        for s in range(2):
            rows = slice(s * half, (s + 1) * half)
            q, kk, v = (qkv[rows, i * hb + h * hd : i * hb + (h + 1) * hd] for i in range(3))
            p = probabilities(q, kk, bias, both[s]).astype(BF16)
            mixed[rows, h * hd : (h + 1) * hd] = dot(p, v).astype(BF16)


def turned_head(g, at, block):
    return at.code(lax.bitwise_xor(block, at.r))


def mixer_kernel(g, *refs):
    rs, zs, hb = g.rs, g.zs, g.hb
    at = g.here()
    mixed_parts, own, rest = refs[:rs], refs[rs], refs[rs + 1 : 2 * rs + 1]
    mixed, wo, partial = refs[2 * rs + 1 :]
    for m in range(rs):
        mixed[:, m * hb : (m + 1) * hb] = mixed_parts[m][...]
    wo[lanes(turned_head(g, at, at.z), hb), :] = own[...]
    for m in range(rs):
        for j in range(1, zs):
            rows = lanes(turned_head(g, at, at.behind(j)), hb)
            piece = rest[m][j - 1, :, 3 * hb :]
            both = jnp.concatenate([piece[:hb], piece[hb:]], axis=1)
            wo[rows, lanes(at.quarter(m), 2 * hb)] = both
    partial[...] = dot(mixed[...], wo[...]).astype(BF16)


def middle_kernel(g, own, sib, part, other, gain, *refs):
    middle, normed2, normed2_t = refs[:3]
    plain = refs[3] if g.aligned else normed2
    half = own.shape[0]
    for s, src in ((0, own), (1, sib)):
        rows = slice(s * half, (s + 1) * half)
        swapped = slice((1 - s) * half, (2 - s) * half)
        v = src[...].astype(F32) + part[rows, :].astype(F32) + other[swapped, :].astype(F32)
        middle[rows, :] = v
        scale = lax.rsqrt(jnp.mean(v * v, axis=-1, keepdims=True) + EPSILON)
        plain[rows, :] = (v * scale * gain[...]).astype(BF16)
    if g.aligned:
        to_relative(g, g.here(), plain, normed2)
    normed2_t[...] = normed2[...].T


def ffn_kernel(g, chunks, last, normed2, normed2_t, *refs):
    hb, sub, zs, cols = g.hb, g.sub, g.zs, g.cols
    at = g.here()
    half = g.seq_len
    n = chunks
    rest, refs = refs[: n * (zs - 1)], refs[n * (zs - 1) :]
    firsts, refs = refs[: n if not g.aligned else 2 - last], refs[n if not g.aligned else 2 - last :]
    if last:
        gl, outer_in, gn2_in, refs = *refs[:3], refs[3:]
    else:
        gl_own, gl_sib, refs = *refs[:2], refs[2:]
    if g.aligned:
        wi, wu, refs = *refs[:2], refs[2:]
    if last:
        outer_own, swap, refs = *refs[:2], refs[2:]
    else:
        gl, outer, gn2, refs = *refs[:3], refs[3:]
        gl[:half, :] = gl_own[...]
        gl[half:, :] = gl_sib[...]
    grads, outs, refs = refs[:n], refs[n : n + zs], refs[n + zs :]
    w1s, w2s, go = refs[:n], refs[n : 2 * n], refs[2 * n]
    copies = Copies(refs[2 * n + 1]) if g.aligned else None
    for i in range(n):
        m = i + (n if last else 0)
        w1, w2 = w1s[i], w2s[i]
        mine = pl.ds(pl.multiple_of(at.z * sub, sub), sub)
        if m and g.aligned:
            s = at.quarter(m)
            fetch_inner(g, at, copies, s, at.k, wi, w1, 0, 0)
            copies.start(wu.at[lanes(s, sub), :], w2.at[mine, :])
            w1[hb : 2 * hb, :] = firsts[-1][m * hb : (m + 1) * hb, 3 * hb :]
        else:
            piece = firsts[i]
            w1[: 2 * hb, :] = piece[: 2 * hb, :]
            for b in range(g.parts):
                rows = slice(2 * hb + b * sub, 2 * hb + (b + 1) * sub)
                w2[mine, b * cols : (b + 1) * cols] = piece[rows, :]
        for j in range(1, zs):
            piece = rest[i * (zs - 1) + j - 1]
            w1[2 * hb * j : 2 * hb * (j + 1), :] = piece[: 2 * hb, :]
            place = lanes(at.behind(j), sub)
            for b in range(g.parts):
                rows = slice(2 * hb + b * sub, 2 * hb + (b + 1) * sub)
                w2[place, b * cols : (b + 1) * cols] = piece[rows, :]
    if copies is not None:
        copies.wait()
    out_sum, gn_sum = None, None
    for i in range(n):
        w1, w2 = w1s[i], w2s[i]
        h = dot(normed2[...], w1[...])
        cdf = 0.5 * (1.0 + lax.erf(h * INV_SQRT2))
        pdf = jnp.exp(-0.5 * h * h) * INV_SQRT2PI
        act = (h * cdf).astype(BF16)
        ga = dot_nt(gl[...], w2[...])
        gh = (ga * (cdf + h * pdf)).astype(BF16)
        grads[i][...] = dot(normed2_t[...], gh).astype(BF16).reshape(zs, 2 * hb, cols)
        full = dot_tn(act, gl[...]).astype(BF16)
        for b in range(zs):
            place = lax.rem(at.z + (zs - b), zs)
            go[place, i * sub : (i + 1) * sub, :] = full[b * sub : (b + 1) * sub, :]
        out_part = dot(act, w2[...])
        gn_part = dot_nt(gh, w1[...])
        out_sum = out_part if out_sum is None else out_sum + out_part
        gn_sum = gn_part if gn_sum is None else gn_sum + gn_part
    for j in range(zs):
        outs[j][...] = go[j]
    if last:
        out_sum = out_sum + outer_in[...]
        outer_own[...] = out_sum[:half]
        swap[g.tokens :, :] = out_sum[half:].astype(BF16)
        swap[: g.tokens, :] = (gn_sum + gn2_in[...]).astype(BF16)
    else:
        outer[...] = out_sum
        gn2[...] = gn_sum


def absolute_sum(g, at, part, other, rows, swapped, total):
    hb = g.hb
    if not g.aligned:
        total[...] = part[rows, :].astype(F32) + other[swapped, :].astype(F32)
        return
    for j in range(g.zs):
        for h in range(2):
            mine, theirs = 2 * j + h, 2 * j + 1 - h
            a = part[rows, mine * hb : (mine + 1) * hb].astype(F32)
            b = other[swapped, theirs * hb : (theirs + 1) * hb].astype(F32)
            total[:, lanes(at.shard(j, h), hb)] = a + b


def middle_back_kernel(g, part, other, middle, gl, gain, mixed, wo, *refs):
    grad_mid, gm, ggain, gwo, gatt, total = refs[:6]
    at, hb = g.here(), g.hb
    half, width = g.seq_len, g.width
    for s in range(2):
        rows = slice(s * half, (s + 1) * half)
        swapped = slice((1 - s) * half, (2 - s) * half)
        absolute_sum(g, at, part, other, rows, swapped, total)
        gn = total[...]
        v = middle[rows, :]
        scale = lax.rsqrt(jnp.mean(v * v, axis=-1, keepdims=True) + EPSILON)
        gg = gn * gain[...]
        inner = jnp.sum(gg * v, axis=-1, keepdims=True) * (1.0 / width)
        grad = gl[rows, :].astype(F32) + scale * gg - v * (scale * scale * scale * inner)
        if s == 0:
            grad_mid[...] = grad
            sums = jnp.sum(gn * v * scale, axis=0, keepdims=True)
            if g.aligned:
                refs[6][...] = sums
                to_relative(g, at, refs[6], ggain)
            else:
                ggain[...] = sums
        gatt[rows, :] = grad.astype(BF16)
    gm[...] = dot_nt(gatt[...], wo[...]).astype(BF16)
    full = dot_tn(mixed[...], gatt[...]).astype(BF16)
    for m in range(g.rs):
        place = lax.rem(at.z + (g.zs - at.quarter(m)), g.zs)
        gwo[place] = full[m * hb : (m + 1) * hb, :]


def attn_back_kernel(g, m, step, lengths, normed_t, off, qkv, gmix, gwo, hot, scaled, w, *refs):
    hb, hd = g.hb, g.hd
    at = g.here()
    both = two_lengths(at, lengths)
    half = g.seq_len
    extra, refs = (refs[:1], refs[1:]) if m == 0 else ((), refs)
    before, refs = (refs[0], refs[1:]) if step else (None, refs)
    gw, *gn, gqkv = refs
    flip = (
        lax.broadcasted_iota(jnp.int32, (half, half), 0)
        + lax.broadcasted_iota(jnp.int32, (half, half), 1)
        == half - 1
    ).astype(BF16)
    table = []
    for h in range(g.nh):
        bias = toeplitz(off[h : h + 1, :], half)
        flipped = jnp.zeros((half, half), F32)
        for s in range(2):
            rows = slice(s * half, (s + 1) * half)
            q, kk, v = (qkv[rows, i * hb + h * hd : i * hb + (h + 1) * hd] for i in range(3))
            gm = gmix[rows, m * hb + h * hd : m * hb + (h + 1) * hd]
            p = probabilities(q, kk, bias, both[s])
            gp = dot_nt(gm, v)
            delta = jnp.sum(p * gp, axis=-1, keepdims=True)
            gs = (p * (gp - delta)).astype(BF16)
            flipped = flipped + dot(flip, gs)
            cols = [slice(i * hb + h * hd, i * hb + (h + 1) * hd) for i in range(3)]
            gqkv[rows, cols[0]] = dot(gs, kk).astype(BF16)
            gqkv[rows, cols[1]] = dot_tn(gs, q).astype(BF16)
            gqkv[rows, cols[2]] = dot_tn(p.astype(BF16), gm).astype(BF16)
        wide = jnp.concatenate([flipped, jnp.zeros((half, half), F32)], axis=1)
        skewed = pltpu.roll(wide, 0, 1, stride=1, stride_axis=0)
        diag = jnp.broadcast_to(jnp.sum(skewed, axis=0, keepdims=True), (8, 2 * half))
        top = diag.astype(BF16)
        table.append(dot_nt(top, hot[...]) + dot_nt((diag - top.astype(F32)).astype(BF16), hot[...]))
    gw[:, : 2 * hb, : 3 * hb] = (
        dot(normed_t[...], gqkv[...]).astype(BF16).reshape(g.zs, 2 * hb, 3 * hb)
    )
    row = lax.broadcasted_iota(jnp.int32, (PAD, hb), 0)
    buckets = jnp.zeros((PAD, hb), F32)
    for i, t in enumerate(table):
        buckets = jnp.where(row == 2 + i, jnp.broadcast_to(t[0:1], (PAD, hb)), buckets)
    for j in range(g.zs):
        piece = gwo[j, :, lanes(at.quarter(m), 2 * hb)]
        gw[j, :hb, 3 * hb :] = piece[:, :hb]
        gw[j, hb : 2 * hb, 3 * hb :] = piece[:, hb:]
        part = dot_nt(gqkv[...], w[2 * hb * j : 2 * hb * (j + 1), :])
        cols = slice(2 * hb * j, 2 * hb * (j + 1))
        gain = jnp.sum(part * scaled[:, cols].astype(F32), axis=0, keepdims=True)
        tile = [gain[:, :hb], gain[:, hb:]]
        tile = jnp.where(row == 0, tile[0], jnp.where(row == 1, tile[1], 0.0))
        gw[j, 2 * hb :, :hb] = tile.astype(BF16)
        if m == 0:
            tile = [extra[0][:, (2 * j + h) * hb : (2 * j + h + 1) * hb] for h in range(2)]
            tile = jnp.where(row == 0, tile[0], jnp.where(row == 1, tile[1], 0.0))
        else:
            tile = jnp.zeros((PAD, hb), F32)
        gw[j, 2 * hb :, hb : 2 * hb] = tile.astype(BF16)
        gw[j, 2 * hb :, 2 * hb : 3 * hb] = buckets.astype(BF16)
        gw[j, 2 * hb :, 3 * hb :] = jnp.zeros((PAD, hb), BF16)
        if before is not None:
            part = part + before[:, cols]
        if len(gn) == 1:
            gn[0][:, cols] = part
        else:
            gn[0][:, cols] = part[:half]
            gn[1][:, cols] = part[half:].astype(BF16)


def input_back_kernel(g, own, other, grad_mid, x, gain, out, total):
    everything = slice(None)
    absolute_sum(g, g.here(), own, other, everything, everything, total)
    gn = total[...]
    v = x[...].astype(F32)
    scale = lax.rsqrt(jnp.mean(v * v, axis=-1, keepdims=True) + EPSILON)
    gg = gn * gain[...]
    inner = jnp.mean(gg * v, axis=-1, keepdims=True)
    grad = grad_mid[...] + scale * gg - v * (scale * scale * scale * inner)
    out[...] = grad.astype(BF16)


def layer_kernel(g, lengths, middle, own, other, out):
    half = own.shape[0]
    row = lax.broadcasted_iota(jnp.int32, own.shape, 0)
    v = middle[:half, :] + own[...] + other[g.tokens :, :].astype(F32)
    out[...] = jnp.where(row < lengths[g.here().me], v, 0.0).astype(BF16)


CORE, SMALL, INPUT, MIDDLE, SWAP, NORMED, INNER, ATTN, COT, COT_SIB, LAYER = range(11)
RING_A, RING_F, HOP_A, HOP_F, GI, GI_SUM, GH, GH_SUM, OA, OB, LATE, SPREAD_F, SPREAD_T = range(11, 24)

ORDER = (
    4, 0, ((COT, 0), 2), 5, 1, 6, 7, 3, 2, 12, 14, 8, 13, 15, 9, ((HOP_F, 1), 2), 16, 10,
    ((HOP_F, 1), 3), 17, ((HOP_F, 3), 3), ((COT, 5), 0), ((COT, 5), 2), 18, 11, ((HOP_F, 3), 2),
    ((COT, 0), 0), 19, 20, 21, 23, 24, 22, 28, 32, 29, 31, 25, 33, (GI, 2), 26, 36, 30, 34, 44, 27,
    46, 37, 35, 48, 45, 47, 38, 50, 51, 49, 39, 40, 52, 41, 53, (SPREAD_F, 2), 42, 43, 54, 55,
)


def solution(mesh):
    rs, ss = mesh.shape["rep"], mesh.shape["shard"]
    zs = ss // 2
    count = rs * ss
    nb = rs.bit_length() - 1

    def pairs(move):
        table = []
        for i in range(count):
            r, z, k = i // ss, (i % ss) // 2, i % 2
            r, z, k = move(r, z, k)
            table.append((i, (r * zs + z) * 2 + k))
        return table

    core_pairs = pairs(lambda r, z, k: (r, z, 1 - k))
    up_pairs = pairs(lambda r, z, k: (r, (z + 1) % zs, k))
    rep_pairs = [
        pairs(lambda r, z, k, b=b: (r ^ (1 << (nb - 1 - b if k else b)), z, k)) for b in range(nb)
    ]
    z_pairs = {m: pairs(lambda r, z, k, m=m: (r, z ^ m, k)) for m in range(1, zs)}

    def send(value, table):
        return lax.ppermute(value, AXES, table)

    by_size = sorted(range(1, rs), key=lambda m: (bin(m).count("1"), m))

    def high(m):
        return m.bit_length() - 1

    def low(m):
        return (m & -m).bit_length() - 1

    def local(
        inputs,
        cotangent,
        seq_lengths,
        dealing,
        rel_buckets,
        w_query,
        w_key,
        w_value,
        w_mixer,
        w_inner,
        w_outer,
        gain_attn,
        gain_mlp,
        bias_table,
    ):
        seq = Sequence()
        bind = functools.partial
        n_buckets, heads = bias_table.shape[0] * ss, bias_table.shape[1]
        g = Geometry(rs, zs, w_query.shape[0], w_outer.shape[0], heads, *inputs.shape[1:])
        hb, fb, sub, cols, nh = g.hb, g.fb, g.sub, g.cols, g.nh
        seq_len, width, tokens = g.seq_len, g.width, g.tokens
        chips, rows = g.chips, g.rows
        chunks = rs // 2

        r, c = lax.axis_index("rep"), lax.axis_index("shard")
        z, k = c // 2, c % 2
        shards = jnp.arange(ss, dtype=jnp.int32)
        x_own = inputs[0]
        d = Box()
        parts = {}

        def relative():
            return 2 * ((z + zs - shards // 2) % zs) + (k ^ (shards % 2))

        def permute_cols(x, order):
            return jnp.take(x.reshape(-1, ss, hb), order, axis=1).reshape(x.shape)

        val = {}
        steps = []

        def put(name, value, table):
            val[name] = send(value, table)

        def step(run, *args):
            steps.append(bind(run, *args))

        labels = [(f, zz) for f in range(rs) for zz in range(zs)]

        def groups_of(stage):
            if stage == nb:
                return [[e for e in labels if e[1] == zz] for zz in range(zs)]
            clear = [e for e in labels if not (e[0] >> stage) & 1]
            return [clear, [e for e in labels if e not in clear]]

        def block_shapes(groups):
            outs = [shaped((len(some), rows, width)) for some in groups]
            return outs if len(outs) == 1 else [stored(outs[0].shape)] + outs[1:]

        def dispatch(key, outs, stage):
            groups = groups_of(stage)
            val[key] = outs[0]
            state = [(key, groups[0])]
            for i, (out, some) in enumerate(zip(outs[1:], groups[1:])):
                put((key, i), out, z_pairs[i + 1] if stage == nb else rep_pairs[stage])
                state.append(((key, i), some))
            return state

        def places(state, some):
            at = {e: (a, b) for a, (_, named) in enumerate(state) for b, e in enumerate(named)}
            return [at[e] for e in some]

        def values(state):
            return [val[name] for name, _ in state]

        def deal_first(what, stage):
            groups = groups_of(stage)
            value = parts[what].reshape(chips, rows, width)
            outs = seq(bind(deal_first_kernel, g, groups), block_shapes(groups), value)
            parts[what] = dispatch((what, 0), outs, stage)

        def deal_stage(what, number, stage):
            groups, state = groups_of(stage), parts[what]
            body = bind(deal_stage_kernel, [places(state, some) for some in groups], len(state))
            outs = seq(body, block_shapes(groups), *values(state))
            parts[what] = dispatch((what, number), outs, stage)

        def deal_core(what):
            state = parts[what]
            body = bind(deal_stage_kernel, [places(state, labels)], len(state))
            parts[what] = seq(body, block_shapes([labels]), *values(state))[0]
            put((what, CORE), parts[what], core_pairs)

        def deal_middle(what, number, stage, back):
            groups = groups_of(stage)
            body = bind(deal_middle_kernel, g, groups, back)
            lookup = [pltpu.SMEM((count,), jnp.int32)]
            args = dealing, parts[what], val[what, CORE]
            outs = seq(body, block_shapes(groups), *args, scalars=1, scratch=lookup)
            parts[what] = dispatch((what, number), outs, stage)

        def deal_last(what, masked):
            state = parts[what]
            body = bind(deal_last_kernel, g, places(state, labels), len(state), masked)
            pool = [pltpu.VMEM((chips, rows, width), BF16)]
            shape = [shaped((chips, rows, width))]
            out = seq(body, shape, seq_lengths, *values(state), scalars=1, scratch=pool)[0]
            parts[what] = out.reshape(seq_len, width)

        def deal(what, first, second, back, end):
            step(deal_first, what, first[0])
            for i, stage in list(enumerate(first))[1:]:
                step(deal_stage, what, i, stage)
            step(deal_core, what)
            n = len(first)
            step(deal_middle, what, n, second[0], back)
            for i, stage in list(enumerate(second))[1:]:
                step(deal_stage, what, n + i, stage)
            step(end)

        copy_sem = pltpu.SemaphoreType.DMA(())

        def slices(m, core):
            s = r ^ (m + core * (g.turned(m) - m))
            at = (2 * s + core) * hb
            parts = [lax.dynamic_slice(w, (0, at), (hb, hb)) for w in (w_query, w_key, w_value)]
            at = [(2 * b + core) * fb + s * sub for b in range(zs)]
            inner = [lax.dynamic_slice(w_inner, (0, a), (hb, sub)) for a in at]
            mix = lax.dynamic_slice(w_mixer, (0, s * 2 * hb), (hb, 2 * hb))
            outer = lax.dynamic_slice(w_outer, (s * sub, 0), (sub, width))
            outer = [outer[:, i * cols : (i + 1) * cols] for i in range(g.parts)]
            return parts, inner, mix, outer

        def start_core():
            if g.aligned:
                sent = seq(
                    bind(send_prep_kernel, g),
                    [shaped((rs * hb, 3 * hb + cols))],
                    w_query,
                    w_key,
                    w_value,
                    w_inner,
                    hbm=4,
                    scratch=[copy_sem],
                )[0]
            else:
                sent = []
                for m in range(rs):
                    parts, inner, _, _ = slices(m, 1 - k)
                    sent.append(jnp.concatenate(parts + inner, axis=1))
                sent = jnp.concatenate(sent, axis=0)
            put(CORE, sent, core_pairs)
            small = jnp.concatenate([gain_attn, gain_mlp, bias_table.reshape(-1)])
            d.n_small = small.shape[0]
            d.small = jnp.pad(small[None], ((0, PAD - 1), (0, 4 * hb - small.shape[0])))
            put(SMALL, d.small, core_pairs)

        def start_attn():
            got = val[CORE]
            if g.aligned:
                own = seq(
                    bind(attn_prep_kernel, g),
                    [shaped((2 * hb + PAD, 4 * hb))],
                    d.small,
                    val[SMALL],
                    got,
                    w_query,
                    w_key,
                    w_value,
                    w_mixer,
                    hbm=4,
                    scratch=[copy_sem],
                )
            else:
                own = []
                for m in range(rs):
                    parts, _, mix, _ = slices(m, k)
                    top = jnp.concatenate(parts + [mix[:, :hb]], axis=1)
                    bottom = [got[m * hb : (m + 1) * hb, : 3 * hb], mix[:, hb:]]
                    own.append(jnp.concatenate([top, jnp.concatenate(bottom, axis=1)], axis=0))
                mine, theirs = d.small, val[SMALL]
                both = jnp.concatenate([mine[:1], theirs[:1], mine[2:]], axis=0)
                own[0] = jnp.concatenate([own[0], both], axis=0)
            d.attn_own = own
            ring(RING_A, own[0])

        def start_ffn():
            got = val[CORE]
            if g.aligned:
                own = seq(
                    bind(ffn_prep_kernel, g),
                    [shaped((4 * hb, cols))],
                    got,
                    w_inner,
                    w_outer,
                    hbm=2,
                    scratch=[copy_sem],
                )
            else:
                own = []
                for m in range(rs):
                    _, inner, _, outer = slices(m, k)
                    bottom = got[m * hb : (m + 1) * hb, 3 * hb :]
                    own.append(
                        jnp.concatenate([jnp.concatenate(inner, axis=1), bottom] + outer, axis=0)
                    )
            d.ffn_own = own
            ring(RING_F, own[0])
            for j in range(1, zs):
                hops((HOP_F, j), val[RING_F, j])

        def ring(name, value):
            for j in range(1, zs):
                put((name, j), value if j == 1 else val[name, j - 1], up_pairs)

        def hops(name, value):
            val[name, 0] = value
            for m in by_size:
                put((name, m), val[name, m ^ (1 << high(m))], rep_pairs[high(m)])

        def stack_attn():
            pieces = [val[RING_A, j] for j in range(1, zs)]
            shape = [shaped((zs - 1, 2 * hb, 4 * hb))]
            hops(HOP_A, seq(bind(stack_kernel, 2 * hb), shape, *pieces)[0])

        def rest_of(j, m):
            return val[(HOP_F, j), m]

        def small_params():
            n_small = d.n_small
            pieces = [d.attn_own[0]] + [val[RING_A, j] for j in range(1, zs)]
            some = [piece[2 * hb : 2 * hb + 2, :n_small] for piece in pieces]
            order = (shards[:, None] == relative()[None, :]).astype(BF16)
            some = dot(order, jnp.concatenate(some, axis=0))
            d.gain_a = some[:, :hb].reshape(1, width)
            d.gain_m = some[:, hb : 2 * hb].reshape(1, width)
            table = some[:, 2 * hb :].reshape(n_buckets, heads)
            quarters = jnp.arange(rs, dtype=jnp.int32)
            quarters = r ^ (quarters + k * (g.turned(quarters) - quarters))
            head_ids = ((2 * quarters + k) * nh)[:, None] + jnp.arange(nh, dtype=jnp.int32)[None]
            pick = jnp.arange(heads, dtype=jnp.int32)[:, None] == head_ids.reshape(1, -1)
            padded = jnp.concatenate([rel_buckets, jnp.full((1,), -1, jnp.int32)])
            hot = padded[None, :] == jnp.arange(hb, dtype=jnp.int32)[:, None]
            d.hot = hot.astype(BF16)
            my_table = dot(table.astype(BF16), pick.astype(BF16)).astype(BF16)
            d.offsets = lax.dot_general(
                my_table,
                d.hot[:n_buckets],
                (((0,), (0,)), ((), ())),
                preferred_element_type=F32,
            ).reshape(rs, nh, 2 * seq_len)

        spare = [pltpu.VMEM((tokens, width), BF16)] if g.aligned else []

        def norm():
            small_params()
            normed, normed_t, scaled = seq(
                bind(norm_kernel, g),
                [shaped((tokens, width)), stored((width, tokens)), stored((tokens, width))],
                x_own,
                val[INPUT],
                d.gain_a,
                scratch=spare * 2,
            )
            if not g.aligned:
                normed = permute_cols(normed, relative())
                scaled = permute_cols(scaled, relative())
                normed_t = normed.T
            d.normed, d.normed_t, d.scaled = normed, normed_t, scaled
            d.qkv, d.mixed_parts, d.attn_w = ([None] * rs for _ in range(3))

        def attend(m):
            own = m == 0 or not g.aligned
            weights = () if own else (w_query, w_key, w_value)
            d.qkv[m], d.mixed_parts[m], d.attn_w[m] = seq(
                bind(attn_kernel, g, m),
                [stored((tokens, 3 * hb)), stored((tokens, hb)), stored((width, 3 * hb))],
                seq_lengths,
                d.normed,
                d.offsets[m],
                d.attn_own[m] if own else val[CORE],
                val[HOP_A, m],
                *weights,
                scalars=1,
                hbm=len(weights),
                scratch=() if own else [copy_sem],
            )

        def mixer():
            d.mixed, d.wo, d.partial = seq(
                bind(mixer_kernel, g),
                [stored((tokens, rs * hb)), stored((rs * hb, width)), shaped((tokens, width))],
                *d.mixed_parts,
                w_mixer,
                *[val[HOP_A, m] for m in range(rs)],
            )
            put(MIDDLE, d.partial, core_pairs)

        def middle():
            d.middle, normed2, normed2_t = seq(
                bind(middle_kernel, g),
                [stored((tokens, width), F32), shaped((tokens, width)), shaped((width, tokens))],
                x_own,
                val[INPUT],
                d.partial,
                val[MIDDLE],
                d.gain_m,
                scratch=spare,
            )
            if not g.aligned:
                normed2 = permute_cols(normed2, relative())
                normed2_t = normed2.T
            d.normed2, d.normed2_t = normed2, normed2_t

        def ffn(part):
            some = range(part * chunks, (part + 1) * chunks)
            if not g.aligned:
                firsts = [d.ffn_own[m] for m in some]
            else:
                firsts = ([] if part else [d.ffn_own[0]]) + [val[CORE]]
            if part == 0:
                more = parts[COT], val[COT_SIB]
                head = [shaped((tokens, width))] + [shaped((tokens, width), F32)] * 2
            else:
                more = (d.gl, *d.acc)
                head = [shaped((seq_len, width), F32), shaped((tokens + seq_len, width))]
            weights = (w_inner, w_outer) if g.aligned else ()
            scratch = [pltpu.VMEM((width, cols), BF16)] * chunks
            scratch += [pltpu.VMEM((cols, width), BF16)] * chunks
            scratch += [pltpu.VMEM((zs, chunks * sub, width), BF16)]
            outs = seq(
                bind(ffn_kernel, g, chunks, part == 1),
                head
                + [shaped((zs, 2 * hb, cols))] * chunks
                + [shaped((chunks * sub, width))] * zs,
                d.normed2,
                d.normed2_t,
                *[rest_of(j, m) for m in some for j in range(1, zs)],
                *firsts,
                *more,
                *weights,
                hbm=len(weights),
                scratch=scratch + ([copy_sem] if g.aligned else []),
                limit=28,
            )
            parts[GI] = (parts[GI] if part else []) + list(outs[len(head) : -zs])
            parts[(OA, OB)[part]] = outs[-zs:]
            if part == 0:
                d.gl, d.acc = outs[0], outs[1:3]
            else:
                d.outer_part, swap = outs[:2]
                if not g.aligned:
                    first = permute_cols(swap[:tokens], jnp.argsort(relative()))
                    swap = jnp.concatenate([first, swap[tokens:]], axis=0)
                d.swap = swap
                put(SWAP, swap, core_pairs)
            for m in some:
                if m % 2:
                    hop_start(GI, m)
            name = (OA, OB)[part]
            put((name, 1), parts[name][1], up_pairs)

        def add(*terms):
            shape = [shaped(terms[0].shape)]
            return seq(bind(sum_kernel, [None] * len(terms)), shape, *terms)[0]

        def sum_step(name, j):
            put((name, j), add(val[name, j - 1], parts[name][j]), up_pairs)

        def hop_start(name, m):
            put((name, m), parts[name][m], rep_pairs[low(m)])

        def hop_add(name, ring, m):
            some = parts[name]
            bits = [b for b in range(nb) if not (m >> b) & 1 and low(m | 1 << b) == b]
            terms = [some[m]] + [val[name, m | 1 << b] for b in bits]
            if m:
                some[m] = add(*terms)
                hop_start(name, m)
            else:
                shape = [shaped(some[0].shape[1:])] * zs
                parts[ring] = seq(bind(cut_sum_kernel, g), shape, *terms)
                put((ring, 1), parts[ring][1], up_pairs)

        def outer_end():
            half, last = rs // 2, zs - 1
            d.late, give = seq(
                bind(outer_end_kernel, g),
                [shaped((half, sub, width))] * 2,
                parts[OA][0],
                val[OA, last],
                parts[OB][0],
                val[OB, last],
            )
            put((LATE, 1), give, rep_pairs[0])

        def outer_pair():
            half = rs // 2
            shape = [shaped((sub, width))] * half
            parts = list(seq(bind(outer_pair_kernel, g), shape, d.late, val[LATE, 1]))
            d.late, names = parts, []
            for i in range(half - 1, 0, -1):
                b = low(i)
                put((LATE, i + 1), parts[i], rep_pairs[b + 1])
                if i ^ (1 << b):
                    parts[i ^ (1 << b)] = add(parts[i ^ (1 << b)], val[LATE, i + 1])
                else:
                    names.append((LATE, i + 1))
            d.late_names = names

        def inner_split():
            keep, give = seq(
                bind(inner_split_kernel, g),
                [shaped((hb, cols))] * 2,
                parts[GI_SUM][0],
                val[GI_SUM, zs - 1],
            )
            d.inner_keep = keep
            put(INNER, give, core_pairs)

        def ffn_pack():
            late = [d.late[0]] + [val[name] for name in d.late_names]
            shape = [shaped((hb + sub, width))]
            body = bind(ffn_pack_kernel, g)
            hops(SPREAD_F, seq(body, shape, d.inner_keep, val[INNER], *late)[0])

        def ffn_end():
            shape = (hb, 2 * zs * fb) if g.aligned else (rs, hb, 2 * zs * sub)
            inner, d.sum_out = seq(
                bind(ffn_end_kernel, g),
                [stored(shape, F32), stored((fb, width), F32)],
                *[val[SPREAD_F, m] for m in range(rs)],
            )
            if not g.aligned:
                inner = jnp.transpose(inner.reshape(rs, hb, 2 * zs, sub), (1, 2, 0, 3))
                inner = inner.reshape(hb, -1)
            d.sum_in = inner

        def attn_split():
            d.attn_keep, d.mixer_keep, give = seq(
                bind(attn_split_kernel, g),
                [
                    shaped((hb + PAD, 3 * hb)),
                    shaped((hb, 2 * hb)),
                    shaped((hb + PAD, 3 * hb)),
                ],
                parts[GH_SUM][0],
                val[GH_SUM, zs - 1],
            )
            put(ATTN, give, core_pairs)

        def attn_pack():
            shape = [shaped((hb + PAD, 8 * hb))]
            args = d.attn_keep, d.mixer_keep, val[ATTN]
            hops(SPREAD_T, seq(bind(attn_pack_kernel, g), shape, *args)[0])

        def attn_end():
            *d.sum_attn, d.gains, d.table = seq(
                bind(attn_end_kernel, g),
                [stored((hb, width), F32)] * 4 + [shaped((8, hb), F32), shaped((heads, hb), F32)],
                *[val[SPREAD_T, m] for m in range(rs)],
            )

        def middle_back():
            more = [pltpu.VMEM((1, width), F32)] if g.aligned else []
            d.grad_mid, d.gmix, ggain, d.grad_wo = seq(
                bind(middle_back_kernel, g),
                [
                    stored((seq_len, width), F32),
                    shaped((tokens, rs * hb)),
                    shaped((1, width), F32),
                    shaped((zs, hb, width)),
                ],
                d.swap,
                val[SWAP],
                d.middle,
                d.gl,
                d.gain_m,
                d.mixed,
                d.wo,
                scratch=[pltpu.VMEM((tokens, width), BF16), pltpu.VMEM((seq_len, width), F32)]
                + more,
            )
            d.ggain_m = ggain if g.aligned else permute_cols(ggain, relative())
            parts[GH] = [None] * rs

        def attend_back(m, turn):
            if turn == rs - 1:
                outs = [shaped((seq_len, width), F32), shaped((seq_len, width))]
            else:
                outs = [shaped((tokens, width), F32)]
            outs = seq(
                bind(attn_back_kernel, g, m, turn),
                [shaped((zs, 2 * hb + PAD, 4 * hb))] + outs,
                seq_lengths,
                d.normed_t,
                d.offsets[m],
                d.qkv[m],
                d.gmix,
                d.grad_wo,
                d.hot,
                d.scaled,
                d.attn_w[m],
                *([d.ggain_m] if m == 0 else []),
                *([d.gn] if turn else []),
                scalars=1,
                scratch=[pltpu.VMEM((tokens, 3 * hb), BF16)],
            )
            parts[GH][m] = outs[0]
            if m % 2:
                hop_start(GH, m)
            if turn < rs - 1:
                d.gn = outs[1]
            else:
                own, sib = outs[1:]
                if not g.aligned:
                    back_to = jnp.argsort(relative())
                    own, sib = permute_cols(own, back_to), permute_cols(sib, back_to)
                d.gn = own
                put(NORMED, sib, core_pairs)

        def input_back():
            d.input_grad = seq(
                bind(input_back_kernel, g),
                [stored((seq_len, width))],
                d.gn,
                val[NORMED],
                d.grad_mid,
                x_own,
                d.gain_a,
                scratch=[pltpu.VMEM((seq_len, width), F32)],
            )[0]

        def layer_out():
            parts[LAYER] = seq(
                bind(layer_kernel, g),
                [shaped((seq_len, width))],
                seq_lengths,
                d.middle,
                d.outer_part,
                val[SWAP],
                scalars=1,
            )[0]

        def cot_end():
            deal_last(COT, True)
            put(COT_SIB, parts[COT], core_pairs)

        parts[COT] = cotangent[0]
        put(INPUT, x_own, core_pairs)
        bits = list(range(nb))
        step(start_core)
        step(start_attn)
        step(start_ffn)
        step(stack_attn)
        deal(COT, [nb] + bits, bits + [nb], True, cot_end)
        step(norm)
        for m in range(rs):
            step(attend, m)
        step(mixer)
        step(middle)
        step(ffn, 0)
        step(ffn, 1)
        step(middle_back)
        step(layer_out)
        back_order = [m for m in range(1, rs, 2)] + [m for m in range(rs - 2, -1, -2)]
        for turn, m in enumerate(back_order):
            step(attend_back, m, turn)
        step(input_back)
        for j in range(2, zs):
            step(sum_step, OA, j)
            step(sum_step, OB, j)
        for m in range(rs - 2, -1, -2):
            step(hop_add, GI, GI_SUM, m)
            step(hop_add, GH, GH_SUM, m)
        deal(LAYER, [nb] + bits, bits + [nb], False, bind(deal_last, LAYER, False))
        step(outer_end)
        step(outer_pair)
        for j in range(2, zs):
            step(sum_step, GI_SUM, j)
            step(sum_step, GH_SUM, j)
        step(inner_split)
        step(ffn_pack)
        step(attn_split)
        step(attn_pack)
        step(ffn_end)
        step(attn_end)
        for item in ORDER if (rs, zs) == (4, 4) else range(len(steps)):
            if isinstance(item, int):
                steps[item]()
            else:
                seq.arrived(val[item if len(item) > 1 else item[0]])

        gains, table = d.gains, d.table[:, :n_buckets].T
        sum_tab = lax.dynamic_slice(table, (c * (n_buckets // ss), 0), (n_buckets // ss, heads))
        return (
            parts[LAYER][None],
            d.input_grad[None],
            *d.sum_attn,
            d.sum_in,
            d.sum_out,
            gains[0],
            gains[1],
            sum_tab,
        )

    tokens_spec = P(AXES, None, None)
    rows_spec, part_spec = P("shard", None), P("shard")
    in_specs = (
        (tokens_spec,) * 2 + (P(),) * 3 + (rows_spec,) * 6 + (part_spec,) * 2 + (rows_spec,)
    )
    out_specs = (tokens_spec,) * 2 + (rows_spec,) * 6 + (part_spec,) * 2 + (rows_spec,)
    return jax.shard_map(local, mesh=mesh, in_specs=in_specs, out_specs=out_specs, check_vma=False)
```

time: 1080 us -> 357 us (0.33)
  waiting for transfers between devices: 567 us -> 157 us
  blocking collectives: 278 us -> 0 us
  matrix products: 98.6 us -> 1.8 us
  Pallas kernels: 0 us -> 91.8 us
  starting transfers between devices: 1.06 us -> 73.5 us
  local copies, waits for them, and re-layouts: 85.5 us -> 28 us
  between operations: 22.1 us -> 1.73 us
  other arithmetic: 21 us -> 0.86 us
    all_gather x8 -> x0, waiting for transfers between devices: 284 us -> none  [the longest x1 80.5 us: local(): lax.all_gather(w_inner, 'shard', axis=0, tiled=True)]
    reduce_scatter x6 -> x0, waiting for transfers between devices: 236 us -> none  [the longest x1 90.3 us: local(): lax.psum_scatter(grad_wout.astype(jnp.bfloat16), 'shard', scatter_dimensi...]
    psum x1 -> x0, blocking collectives: 202 us -> none  [local(): lax.psum((part_q, part_k, part_v, part_o, part_in, part_out, part_ga, par...]
    ppermute x0 -> x75, waiting for transfers between devices: none -> 157 us  [send(): return lax.ppermute(value, AXES, table)]
    dot_general x26 -> x2, matrix products: 98.6 us -> 1.8 us  [the longest x1 1.67 us: small_params(): lax.dot_general(my_table, d.hot[:n_buckets], (((0,), (0,)), ((), ())), pr...]
    pallas_call x0 -> x66, Pallas kernels: none -> 91.8 us  [__call__(): pl.pallas_call(run, out_shape=outs, in_specs=specs + [ANY] * m, out_specs...]
    ppermute x0 -> x75, starting transfers between devices: none -> 73.5 us  [send(): return lax.ppermute(value, AXES, table)]
    psum x1 -> x0, waiting for transfers between devices: 42.5 us -> none  [local(): lax.psum((part_q, part_k, part_v, part_o, part_in, part_out, part_ga, par...]
  transfers between devices with their start and end apart: 15 -> 75, of which waited for: 13 -> 31; matrix products, arithmetic and copies ran while one was open for 17% -> 2% of each run, Pallas kernels for 0% -> 22%
where the time goes in v2:
time: 357 us; the launch traced here: 355 us
  waiting for transfers between devices  157 us (44%)
  Pallas kernels  91.8 us (26%)
  starting transfers between devices  73.5 us (21%)
  local copies, waits for them, and re-layouts  28 us (8%)
    ppermute x75, waiting for transfers between devices, send(): return lax.ppermute(value, AXES, table)  157 us
    pallas_call x66, Pallas kernels, __call__(): pl.pallas_call(run, out_shape=outs, in_specs=specs + [ANY] * m, out_specs...  91.8 us
    ppermute x75, starting transfers between devices, send(): return lax.ppermute(value, AXES, table)  73.5 us
    unnamed x121, local copies, waits for them, and re-layouts  22 us
  transfers between devices with their start and end apart: 75, of which 31 were waited for; matrix products, arithmetic and copies ran while one was open for 2% of the time, Pallas kernels for 22%

profile of v2, /device:TPU:0, one launch (start us, length us, event | category | flops | bytes accessed | tf_op | source)
XLA Modules:
  0.0 355.0 jit_solution(458086856219910133)
XLA Ops:
  4.2 4.7 %collective-permute-start.5 = (bf16[4,16,1024]{2,1,0:T(8,128)(2,1)S(1)}, bf16[4,16,1024]{2,1,0:T(8,128)(2,1)S(1)}, u32[]{:S(2)}, u32[]{:S(2)}) collective-permute-start(bf16[4,16,1024]{2,1,0:T(8,128)(2,1)S(1)} %get-tuple-element.119.refs_4_), channel_id=1, source_target_pairs={{0,6},{1,7},{2,4},{3,5},{4,2},{5,3},{6,0},{7,1},{8,14},{9,15},{10,... | collective-permute-start | bytes 393224 | tf_op jit(solution)/shard_map/ppermute | solution.py:719
  9.7 3.5 collective-permute-done.5.refs_0_.refs_3_
  13.2 3.6 %collective-permute-done.3.refs_1_.refs_0_ = bf16[4,16,1024]{2,1,0:T(8,128)(2,1)S(1)} collective-permute-done((bf16[4,16,1024]{2,1,0:T(8,128)(2,1)S(1)}, bf16[4,16,1024]{2,1,0:T(8,128)(2,1)S(1)}, u32[]{:S(2)}, u32[]{:S(2)}) %collective-permute-start.3) | collective-permute-done | bytes 131104 | tf_op jit(solution)/shard_map/ppermute | solution.py:719
  16.8 3.7 %collective-permute-done.4.refs_2_ = bf16[4,16,1024]{2,1,0:T(8,128)(2,1)S(1)} collective-permute-done((bf16[4,16,1024]{2,1,0:T(8,128)(2,1)S(1)}, bf16[4,16,1024]{2,1,0:T(8,128)(2,1)S(1)}, u32[]{:S(2)}, u32[]{:S(2)}) %collective-permute-start.4) | collective-permute-done | bytes 131104 | tf_op jit(solution)/shard_map/ppermute | solution.py:719
  22.3 10.0 %collective-permute-done.6.refs_0_ = bf16[272,512]{1,0:T(8,128)(2,1)S(1)} collective-permute-done((bf16[272,512]{1,0:T(8,128)(2,1)S(1)}, bf16[272,512]{1,0:T(8,128)(2,1)S(1)}, u32[]{:S(2)}, u32[]{:S(2)}) %collective-permute-start.6) | collective-permute-done | bytes 278560 | tf_op jit(solution)/shard_map/ppermute | solution.py:719
  34.5 6.9 %collective-permute-done.7.refs_1_ = bf16[272,512]{1,0:T(8,128)(2,1)S(1)} collective-permute-done((bf16[272,512]{1,0:T(8,128)(2,1)S(1)}, bf16[272,512]{1,0:T(8,128)(2,1)S(1)}, u32[]{:S(2)}, u32[]{:S(2)}) %collective-permute-start.7) | collective-permute-done | bytes 278560 | tf_op jit(solution)/shard_map/ppermute | solution.py:719
  44.5 4.1 %collective-permute-done.10.refs_1_ = bf16[8,16,1024]{2,1,0:T(8,128)(2,1)S(1)} collective-permute-done((bf16[8,16,1024]{2,1,0:T(8,128)(2,1)S(1)}, bf16[8,16,1024]{2,1,0:T(8,128)(2,1)S(1)}, u32[]{:S(2)}, u32[]{:S(2)}) %collective-permute-start.10) | collective-permute-done | bytes 262176 | tf_op jit(solution)/shard_map/ppermute | solution.py:719
  64.2 5.2 %collective-permute-done.15.refs_2_ = bf16[512,512]{1,0:T(8,128)(2,1)} collective-permute-done((bf16[512,512]{1,0:T(8,128)(2,1)S(1)}, bf16[512,512]{1,0:T(8,128)(2,1)}, u32[]{:S(2)}, u32[]{:S(2)}) %collective-permute-start.15) | collective-permute-done | bytes 524320 | tf_op jit(solution)/shard_map/ppermute | solution.py:719
  76.2 3.7 %shard_map.230 = (bf16[512,1024]{1,0:T(8,128)(2,1)S(1)}, bf16[1024,512]{1,0:T(8,128)(2,1)}, bf16[512,1024]{1,0:T(8,128)(2,1)}) custom-call(bf16[256,1024]{1,0:T(8,128)(2,1)S(1)} %bitcast.19, bf16[256,1024]{1,0:T(8,128)(2,1)} %collective-permute-done.refs_1_, f32[1,1024]{1,0:T(1,128)S(1)} %bitcast.26, bf16[512,512]{1,0:T(8,128)(2,1)S(1)} %shard_map.229.refs_3_.refs_8_), custom_call_target="tpu_custom_call" | custom-call | tf_op jit(solution)/shard_map/pallas_call | solution.py:51
  82.8 4.8 %shard_map.231 = (bf16[512,384]{1,0:T(8,128)(2,1)}, bf16[512,128]{1,0:T(8,128)(2,1)}, bf16[1024,384]{1,0:T(8,128)(2,1)}) custom-call(s32[32]{0:T(128)S(1)} %copy-done.53, bf16[512,1024]{1,0:T(8,128)(2,1)S(1)} %get-tuple-element.127.refs_1_, f32[2,512]{1,0:T(2,128)S(1)} %get-tuple-element.251.refs_2_, ...), custom_call_target="tpu_custom_call" | custom-call | tf_op jit(solution)/shard_map/pallas_call | solution.py:51
  90.3 2.0 shard_map.232
  94.2 3.3 shard_map.233
  98.7 4.8 %shard_map.234 = (bf16[512,384]{1,0:T(8,128)(2,1)}, bf16[512,128]{1,0:T(8,128)(2,1)}, bf16[1024,384]{1,0:T(8,128)(2,1)}) custom-call(s32[32]{0:T(128)S(1)} %copy-done.53, bf16[512,1024]{1,0:T(8,128)(2,1)S(1)} %get-tuple-element.127.refs_1_, f32[2,512]{1,0:T(2,128)S(1)} %get-tuple-element.250.refs_2_, ...), custom_call_target="tpu_custom_call" | custom-call | tf_op jit(solution)/shard_map/pallas_call | solution.py:51
  107.6 4.2 %shard_map.237 = (bf16[512,384]{1,0:T(8,128)(2,1)}, bf16[512,128]{1,0:T(8,128)(2,1)}, bf16[1024,384]{1,0:T(8,128)(2,1)}) custom-call(s32[32]{0:T(128)S(1)} %copy-done.53, bf16[512,1024]{1,0:T(8,128)(2,1)S(1)} %get-tuple-element.127.refs_1_, f32[2,512]{1,0:T(2,128)S(1)} %get-tuple-element.249.refs_2_, ...), custom_call_target="tpu_custom_call" | custom-call | tf_op jit(solution)/shard_map/pallas_call | solution.py:51
  114.7 2.9 shard_map.240
  119.7 3.2 collective-permute-start.23
  124.6 7.3 %collective-permute-done.27.refs_0_.refs_7_ = bf16[512,512]{1,0:T(8,128)(2,1)S(1)} collective-permute-done((bf16[512,512]{1,0:T(8,128)(2,1)S(1)}, bf16[512,512]{1,0:T(8,128)(2,1)S(1)}, u32[]{:S(2)}, u32[]{:S(2)}) %collective-permute-start.27) | collective-permute-done | bytes 524320 | tf_op jit(solution)/shard_map/ppermute | solution.py:719
  131.9 3.2 collective-permute-start.32
  135.5 3.5 shard_map.244
  140.2 2.0 collective-permute-start.28
  142.3 2.0 collective-permute-done.29.refs_0_.refs_4_
  144.3 9.8 %shard_map.248 = (bf16[512,1024]{1,0:T(8,128)(2,1)S(1)}, f32[512,1024]{1,0:T(8,128)S(1)}, f32[512,1024]{1,0:T(8,128)S(1)}, bf16[4,256,512]{2,1,0:T(8,128)(2,1)S(...) custom-call(bf16[512,1024]{1,0:T(8,128)(2,1)S(1)} %get-tuple-element, ...), custom_call_target="tpu_custom_call" | custom-call | tf_op jit(solution)/shard_map/pallas_call | solution.py:51
  155.5 8.4 %shard_map.249 = (f32[256,1024]{1,0:T(8,128)S(1)}, bf16[768,1024]{1,0:T(8,128)(2,1)S(1)}, bf16[4,256,512]{2,1,0:T(8,128)(2,1)S(1)}, bf16[4,256,512]{2,1,0:T(8,12...) custom-call(bf16[512,1024]{1,0:T(8,128)(2,1)S(1)} %get-tuple-element, ...), custom_call_target="tpu_custom_call" | custom-call | tf_op jit(solution)/shard_map/pallas_call | solution.py:51
  167.5 3.2 shard_map.250
  170.7 4.5 %shard_map.251 = (bf16[4,272,512]{2,1,0:T(8,128)(2,1)S(1)}, f32[512,1024]{1,0:T(8,128)S(1)}) custom-call(s32[32]{0:T(128)S(1)} %copy-done.53, bf16[1024,512]{1,0:T(8,128)(2,1)S(1)} %copy-done.2, f32[2,512]{1,0:T(2,128)S(1)} %get-tuple-element.251.refs_2_, bf16[512,384]{1,0:T(8,128)(2,1)S(1)} %copy-done.26, bf16[512,512]{1,0:T(8,128)(2,1)S(1)} %get-tuple-element.160.refs_4_, ...), custom_call_target="tpu_custom_call" | custom-call | tf_op jit(solution)/shard_map/pallas_call | solution.py:51
  175.2 4.5 %shard_map.252 = (bf16[4,272,512]{2,1,0:T(8,128)(2,1)S(1)}, f32[512,1024]{1,0:T(8,128)S(1)}) custom-call(s32[32]{0:T(128)S(1)} %copy-done.53, bf16[1024,512]{1,0:T(8,128)(2,1)S(1)} %copy-done.2, f32[2,512]{1,0:T(2,128)S(1)} %get-tuple-element.249.refs_2_, bf16[512,384]{1,0:T(8,128)(2,1)S(1)} %copy-done.24, bf16[512,512]{1,0:T(8,128)(2,1)S(1)} %get-tuple-element.160.refs_4_, ...), custom_call_target="tpu_custom_call" | custom-call | tf_op jit(solution)/shard_map/pallas_call | solution.py:51
  185.3 11.6 %collective-permute-done.35.refs_0_ = bf16[256,1024]{1,0:T(8,128)(2,1)S(1)} collective-permute-done((bf16[256,1024]{1,0:T(8,128)(2,1)S(1)}, bf16[256,1024]{1,0:T(8,128)(2,1)S(1)}, u32[]{:S(2)}, u32[]{:S(2)}) %collective-permute-start.35) | collective-permute-done | bytes 524320 | tf_op jit(solution)/shard_map/ppermute | solution.py:719
  197.4 16.4 %collective-permute-done.38.refs_0_ = bf16[256,1024]{1,0:T(8,128)(2,1)S(1)} collective-permute-done((bf16[256,1024]{1,0:T(8,128)(2,1)S(1)}, bf16[256,1024]{1,0:T(8,128)(2,1)S(1)}, u32[]{:S(2)}, u32[]{:S(2)}) %collective-permute-start.38) | collective-permute-done | bytes 524320 | tf_op jit(solution)/shard_map/ppermute | solution.py:719
  214.8 4.5 %shard_map.258 = (bf16[4,272,512]{2,1,0:T(8,128)(2,1)S(1)}, f32[512,1024]{1,0:T(8,128)S(1)}) custom-call(s32[32]{0:T(128)S(1)} %copy-done.53, bf16[1024,512]{1,0:T(8,128)(2,1)S(1)} %copy-done.2, f32[2,512]{1,0:T(2,128)S(1)} %get-tuple-element.250.refs_2_, bf16[512,384]{1,0:T(8,128)(2,1)S(1)} %copy-done.23, bf16[512,512]{1,0:T(8,128)(2,1)S(1)} %get-tuple-element.160.refs_4_, ...), custom_call_target="tpu_custom_call" | custom-call | tf_op jit(solution)/shard_map/pallas_call | solution.py:51
  220.7 4.5 %shard_map.261 = (bf16[4,272,512]{2,1,0:T(8,128)(2,1)S(1)}, f32[256,1024]{1,0:T(8,128)S(1)}, bf16[256,1024]{1,0:T(8,128)(2,1)S(1)}) custom-call(s32[32]{0:T(128)S(1)} %copy-done.53, bf16[1024,512]{1,0:T(8,128)(2,1)S(1)} %copy-done.2, f32[2,512]{1,0:T(2,128)S(1)} %get-tuple-element.252.refs_2_, bf16[512,384]{1,0:T(8,128)(2,1)S(1)} %copy-done.25, ...), custom_call_target="tpu_custom_call" | custom-call | tf_op jit(solution)/shard_map/pallas_call | solution.py:51
  226.6 10.7 %collective-permute-done.49.refs_3_ = bf16[256,1024]{1,0:T(8,128)(2,1)S(1)} collective-permute-done((bf16[256,1024]{1,0:T(8,128)(2,1)S(1)}, bf16[256,1024]{1,0:T(8,128)(2,1)S(1)}, u32[]{:S(2)}, u32[]{:S(2)}) %collective-permute-start.49) | collective-permute-done | bytes 524320 | tf_op jit(solution)/shard_map/ppermute | solution.py:719
  237.3 11.2 %collective-permute-done.48.refs_1_ = bf16[256,1024]{1,0:T(8,128)(2,1)S(1)} collective-permute-done((bf16[256,1024]{1,0:T(8,128)(2,1)S(1)}, bf16[256,1024]{1,0:T(8,128)(2,1)S(1)}, u32[]{:S(2)}, u32[]{:S(2)}) %collective-permute-start.48) | collective-permute-done | bytes 524320 | tf_op jit(solution)/shard_map/ppermute | solution.py:719
  248.8 5.2 %collective-permute-done.41.refs_1_ = bf16[4,16,1024]{2,1,0:T(8,128)(2,1)S(1)} collective-permute-done((bf16[4,16,1024]{2,1,0:T(8,128)(2,1)S(1)}, bf16[4,16,1024]{2,1,0:T(8,128)(2,1)S(1)}, u32[]{:S(2)}, u32[]{:S(2)}) %collective-permute-start.41) | collective-permute-done | bytes 131104 | tf_op jit(solution)/shard_map/ppermute | solution.py:719
  259.7 9.9 %collective-permute-done.42.refs_2_ = bf16[4,16,1024]{2,1,0:T(8,128)(2,1)S(1)} collective-permute-done((bf16[4,16,1024]{2,1,0:T(8,128)(2,1)S(1)}, bf16[4,16,1024]{2,1,0:T(8,128)(2,1)S(1)}, u32[]{:S(2)}, u32[]{:S(2)}) %collective-permute-start.42) | collective-permute-done | bytes 131104 | tf_op jit(solution)/shard_map/ppermute | solution.py:719
  270.8 2.0 collective-permute-start.53
  272.8 13.8 %collective-permute-start.50 = (bf16[8,16,1024]{2,1,0:T(8,128)(2,1)S(1)}, bf16[8,16,1024]{2,1,0:T(8,128)(2,1)S(1)}, u32[]{:S(2)}, u32[]{:S(2)}) collective-permute-start(bf16[8,16,1024]{2,1,0:T(8,128)(2,1)S(1)} %get-tuple-element.193.refs_3_), channel_id=1, source_target_pairs={{0,8},{1,17},{2,10},{3,19},{4,12},{5,21},{6,14},{7,23},{8,0},{9,25... | collective-permute-start | bytes 786440 | tf_op jit(solution)/shard_map/ppermute | solution.py:719
  287.2 3.8 %collective-permute-done.50.refs_1_ = bf16[8,16,1024]{2,1,0:T(8,128)(2,1)S(1)} collective-permute-done((bf16[8,16,1024]{2,1,0:T(8,128)(2,1)S(1)}, bf16[8,16,1024]{2,1,0:T(8,128)(2,1)S(1)}, u32[]{:S(2)}, u32[]{:S(2)}) %collective-permute-start.50) | collective-permute-done | bytes 262176 | tf_op jit(solution)/shard_map/ppermute | solution.py:719
  291.7 3.2 collective-permute-done.58.refs_1_
  298.2 4.5 %collective-permute-start.73 = (bf16[256,1024]{1,0:T(8,128)(2,1)S(1)}, bf16[256,1024]{1,0:T(8,128)(2,1)S(1)}, u32[]{:S(2)}, u32[]{:S(2)}) collective-permute-start(bf16[256,1024]{1,0:T(8,128)(2,1)S(1)} %shard_map.275.refs_2_.refs_0_), channel_id=1, source_target_pairs={{0,8},{1,17},{2,10},{3,19},{4,12},{5,21},{6,14},{7,23},{8,0},{9,25... | collective-permute-start | bytes 1572872 | tf_op jit(solution)/shard_map/ppermute | solution.py:719
  306.0 5.1 %collective-permute-done.63.refs_1_ = bf16[272,512]{1,0:T(8,128)(2,1)S(1)} collective-permute-done((bf16[272,512]{1,0:T(8,128)(2,1)S(1)}, bf16[272,512]{1,0:T(8,128)(2,1)S(1)}, u32[]{:S(2)}, u32[]{:S(2)}) %collective-permute-start.63) | collective-permute-done | bytes 278560 | tf_op jit(solution)/shard_map/ppermute | solution.py:719
  311.2 7.1 %collective-permute-done.62.refs_1_ = bf16[8,16,1024]{2,1,0:T(8,128)(2,1)S(1)} collective-permute-done((bf16[8,16,1024]{2,1,0:T(8,128)(2,1)S(1)}, bf16[8,16,1024]{2,1,0:T(8,128)(2,1)S(1)}, u32[]{:S(2)}, u32[]{:S(2)}) %collective-permute-start.62) | collective-permute-done | bytes 262176 | tf_op jit(solution)/shard_map/ppermute | solution.py:719
  320.1 2.1 collective-permute-start.70
  322.1 2.0 collective-permute-start.74
  324.2 5.8 %collective-permute-done.70.refs_1_ = bf16[144,1024]{1,0:T(8,128)(2,1)S(1)} collective-permute-done((bf16[144,1024]{1,0:T(8,128)(2,1)S(1)}, bf16[144,1024]{1,0:T(8,128)(2,1)S(1)}, u32[]{:S(2)}, u32[]{:S(2)}) %collective-permute-start.70) | collective-permute-done | bytes 294944 | tf_op jit(solution)/shard_map/ppermute | solution.py:719
  330.9 6.4 %collective-permute-done.67.refs_2_ = bf16[4,16,1024]{2,1,0:T(8,128)(2,1)S(1)} collective-permute-done((bf16[4,16,1024]{2,1,0:T(8,128)(2,1)S(1)}, bf16[4,16,1024]{2,1,0:T(8,128)(2,1)S(1)}, u32[]{:S(2)}, u32[]{:S(2)}) %collective-permute-start.67) | collective-permute-done | bytes 131104 | tf_op jit(solution)/shard_map/ppermute | solution.py:719
  337.4 2.6 collective-permute-done.68.refs_3_
  340.0 4.3 %collective-permute-done.69.refs_4_ = bf16[4,16,1024]{2,1,0:T(8,128)(2,1)} collective-permute-done((bf16[4,16,1024]{2,1,0:T(8,128)(2,1)S(1)}, bf16[4,16,1024]{2,1,0:T(8,128)(2,1)}, u32[]{:S(2)}, u32[]{:S(2)}) %collective-permute-start.69) | collective-permute-done | bytes 131104 | tf_op jit(solution)/shard_map/ppermute | solution.py:719
  348.0 2.5 shard_map.285
  (311 shorter events, 95.0 us)
Async XLA Ops:
  3.6 17.6 %collective-permute-start.2 = (bf16[512,896]{1,0:T(8,128)(2,1)S(1)}, bf16[512,896]{1,0:T(8,128)(2,1)S(1)}, u32[]{:S(2)}, u32[]{:S(2)}) collective-permute-start(bf16[512,896]{1,0:T(8,128)(2,1)S(1)} %shard_map.222.refs_1_), channel_id=1, source_target_pairs={{0,1},{1,0},{2,3},{3,2},{4,5},{5,4},{6,7},{7,6},{8,9},{9,8},{10,11... | collective-permute-start | bytes 2752520 | tf_op jit(solution)/shard_map/ppermute | solution.py:719
  8.8 11.7 %collective-permute-start.4 = (bf16[4,16,1024]{2,1,0:T(8,128)(2,1)S(1)}, bf16[4,16,1024]{2,1,0:T(8,128)(2,1)S(1)}, u32[]{:S(2)}, u32[]{:S(2)}) collective-permute-start(bf16[4,16,1024]{2,1,0:T(8,128)(2,1)S(1)} %get-tuple-element.122), channel_id=1, source_target_pairs={{0,4},{1,5},{2,6},{3,7},{4,0},{5,1},{6,2},{7,3},{8,12},{9,13},{10,... | collective-permute-start | bytes 393224 | tf_op jit(solution)/shard_map/ppermute | solution.py:719
  9.6 11.7 %collective-permute-start.1 = (bf16[16,512]{1,0:T(8,128)(2,1)S(1)}, bf16[16,512]{1,0:T(8,128)(2,1)S(1)}, u32[]{:S(2)}, u32[]{:S(2)}) collective-permute-start(bf16[16,512]{1,0:T(8,128)(2,1)S(1)} %pad.4.refs_0_), channel_id=1, source_target_pairs={{0,1},{1,0},{2,3},{3,2},{4,5},{5,4},{6,7},{7,6},{8,9},{9,8},{10,11... | collective-permute-start | bytes 49160 | tf_op jit(solution)/shard_map/ppermute | solution.py:719
  44.4 27.1 %collective-permute-start = (bf16[256,1024]{1,0:T(8,128)(2,1)S(1)}, bf16[256,1024]{1,0:T(8,128)(2,1)}, u32[]{:S(2)}, u32[]{:S(2)}) collective-permute-start(bf16[256,1024]{1,0:T(8,128)(2,1)S(1)} %bitcast.18), channel_id=1, source_target_pairs={{0,1},{1,0},{2,3},{3,2},{4,5},{5,4},{6,7},{7,6},{8,9},{9,8},{10,11... | collective-permute-start | bytes 1572872 | tf_op jit(solution)/shard_map/ppermute | solution.py:719
  56.9 12.5 %collective-permute-start.15 = (bf16[512,512]{1,0:T(8,128)(2,1)S(1)}, bf16[512,512]{1,0:T(8,128)(2,1)}, u32[]{:S(2)}, u32[]{:S(2)}) collective-permute-start(bf16[512,512]{1,0:T(8,128)(2,1)S(1)} %shard_map.229.refs_3_.refs_8_), channel_id=1, source_target_pairs={{0,2},{1,3},{2,4},{3,5},{4,6},{5,7},{6,0},{7,1},{8,10},{9,11},{10,... | collective-permute-start | bytes 1572872 | tf_op jit(solution)/shard_map/ppermute | solution.py:719
  57.7 16.9 %collective-permute-start.12 = (bf16[3,256,512]{2,1,0:T(8,128)(2,1)S(1)}, bf16[3,256,512]{2,1,0:T(8,128)(2,1)}, u32[]{:S(2)}, u32[]{:S(2)}) collective-permute-start(bf16[3,256,512]{2,1,0:T(8,128)(2,1)S(1)} %shard_map.228.refs_3_.refs_4_.refs_5_), channel_id=1, source_target_pairs={{0,8},{1,17},{2,10},{3,19},{4,12},{5,21},{6,14},{7,23},{8,0},{9,25... | collective-permute-start | bytes 2359304 | tf_op jit(solution)/shard_map/ppermute | solution.py:719
  60.6 26.9 %collective-permute-start.11 = (bf16[16,16,1024]{2,1,0:T(8,128)(2,1)S(1)}, bf16[16,16,1024]{2,1,0:T(8,128)(2,1)}, u32[]{:S(2)}, u32[]{:S(2)}) collective-permute-start(bf16[16,16,1024]{2,1,0:T(8,128)(2,1)S(1)} %shard_map.227.refs_3_.refs_1_), channel_id=1, source_target_pairs={{0,1},{1,0},{2,3},{3,2},{4,5},{5,4},{6,7},{7,6},{8,9},{9,8},{10,11... | collective-permute-start | bytes 1572872 | tf_op jit(solution)/shard_map/ppermute | solution.py:719
  62.0 30.2 %collective-permute-start.13 = (bf16[3,256,512]{2,1,0:T(8,128)(2,1)S(1)}, bf16[3,256,512]{2,1,0:T(8,128)(2,1)}, u32[]{:S(2)}, u32[]{:S(2)}) collective-permute-start(bf16[3,256,512]{2,1,0:T(8,128)(2,1)S(1)} %shard_map.228.refs_3_.refs_4_.refs_5_), channel_id=1, source_target_pairs={{0,16},{1,9},{2,18},{3,11},{4,20},{5,13},{6,22},{7,15},{8,24},{9,1... | collective-permute-start | bytes 2359304 | tf_op jit(solution)/shard_map/ppermute | solution.py:719
  69.4 11.9 %collective-permute-start.24 = (bf16[512,512]{1,0:T(8,128)(2,1)}, bf16[512,512]{1,0:T(8,128)(2,1)}, u32[]{:S(2)}, u32[]{:S(2)}) collective-permute-start(bf16[512,512]{1,0:T(8,128)(2,1)} %collective-permute-done.15.refs_2_), channel_id=1, source_target_pairs={{0,2},{1,3},{2,4},{3,5},{4,6},{5,7},{6,0},{7,1},{8,10},{9,11},{10,... | collective-permute-start | bytes 1572872 | tf_op jit(solution)/shard_map/ppermute | solution.py:719
  71.5 22.3 %collective-permute-start.18 = (bf16[512,512]{1,0:T(8,128)(2,1)}, bf16[512,512]{1,0:T(8,128)(2,1)}, u32[]{:S(2)}, u32[]{:S(2)}) collective-permute-start(bf16[512,512]{1,0:T(8,128)(2,1)} %collective-permute-done.15.refs_2_), channel_id=1, source_target_pairs={{0,8},{1,17},{2,10},{3,19},{4,12},{5,21},{6,14},{7,23},{8,0},{9,25... | collective-permute-start | bytes 1572872 | tf_op jit(solution)/shard_map/ppermute | solution.py:719
  74.7 32.9 %collective-permute-start.14 = (bf16[3,256,512]{2,1,0:T(8,128)(2,1)}, bf16[3,256,512]{2,1,0:T(8,128)(2,1)S(1)}, u32[]{:S(2)}, u32[]{:S(2)}) collective-permute-start(bf16[3,256,512]{2,1,0:T(8,128)(2,1)} %collective-permute-done.12.refs_4_.refs_6_), channel_id=1, source_target_pairs={{0,16},{1,9},{2,18},{3,11},{4,20},{5,13},{6,22},{7,15},{8,24},{9,1... | collective-permute-start | bytes 2359304 | tf_op jit(solution)/shard_map/ppermute | solution.py:719
  81.3 25.7 %collective-permute-start.25 = (bf16[512,512]{1,0:T(8,128)(2,1)}, bf16[512,512]{1,0:T(8,128)(2,1)S(1)}, u32[]{:S(2)}, u32[]{:S(2)}) collective-permute-start(bf16[512,512]{1,0:T(8,128)(2,1)} %collective-permute-done.24.refs_3_), channel_id=1, source_target_pairs={{0,2},{1,3},{2,4},{3,5},{4,6},{5,7},{6,0},{7,1},{8,10},{9,11},{10,... | collective-permute-start | bytes 1572872 | tf_op jit(solution)/shard_map/ppermute | solution.py:719
  87.6 19.9 %collective-permute-start.16 = (bf16[512,512]{1,0:T(8,128)(2,1)}, bf16[512,512]{1,0:T(8,128)(2,1)S(1)}, u32[]{:S(2)}, u32[]{:S(2)}) collective-permute-start(bf16[512,512]{1,0:T(8,128)(2,1)} %collective-permute-done.15.refs_2_), channel_id=1, source_target_pairs={{0,16},{1,9},{2,18},{3,11},{4,20},{5,13},{6,22},{7,15},{8,24},{9,1... | collective-permute-start | bytes 1572872 | tf_op jit(solution)/shard_map/ppermute | solution.py:719
  92.3 11.3 %collective-permute-start.17 = (bf16[8,16,1024]{2,1,0:T(8,128)(2,1)S(1)}, bf16[8,16,1024]{2,1,0:T(8,128)(2,1)S(1)}, u32[]{:S(2)}, u32[]{:S(2)}) collective-permute-start(bf16[8,16,1024]{2,1,0:T(8,128)(2,1)S(1)} %get-tuple-element.130.refs_5_), channel_id=1, source_target_pairs={{0,8},{1,17},{2,10},{3,19},{4,12},{5,21},{6,14},{7,23},{8,0},{9,25... | collective-permute-start | bytes 786440 | tf_op jit(solution)/shard_map/ppermute | solution.py:719
  93.8 20.7 %collective-permute-start.19 = (bf16[512,512]{1,0:T(8,128)(2,1)}, bf16[512,512]{1,0:T(8,128)(2,1)S(1)}, u32[]{:S(2)}, u32[]{:S(2)}) collective-permute-start(bf16[512,512]{1,0:T(8,128)(2,1)} %collective-permute-done.18.refs_5_), channel_id=1, source_target_pairs={{0,16},{1,9},{2,18},{3,11},{4,20},{5,13},{6,22},{7,15},{8,24},{9,1... | collective-permute-start | bytes 1572872 | tf_op jit(solution)/shard_map/ppermute | solution.py:719
  117.6 17.9 %collective-permute-start.21 = (bf16[512,1024]{1,0:T(8,128)(2,1)S(1)}, bf16[512,1024]{1,0:T(8,128)(2,1)S(1)}, u32[]{:S(2)}, u32[]{:S(2)}) collective-permute-start(bf16[512,1024]{1,0:T(8,128)(2,1)S(1)} %get-tuple-element.142.refs_1_.refs_2_), channel_id=1, source_target_pairs={{0,1},{1,0},{2,3},{3,2},{4,5},{5,4},{6,7},{7,6},{8,9},{9,8},{10,11... | collective-permute-start | bytes 3145736 | tf_op jit(solution)/shard_map/ppermute | solution.py:719
  117.6 14.3 %collective-permute-start.27 = (bf16[512,512]{1,0:T(8,128)(2,1)S(1)}, bf16[512,512]{1,0:T(8,128)(2,1)S(1)}, u32[]{:S(2)}, u32[]{:S(2)}) collective-permute-start(bf16[512,512]{1,0:T(8,128)(2,1)S(1)} %collective-permute-done.26.refs_7_), channel_id=1, source_target_pairs={{0,16},{1,9},{2,18},{3,11},{4,20},{5,13},{6,22},{7,15},{8,24},{9,1... | collective-permute-start | bytes 1572872 | tf_op jit(solution)/shard_map/ppermute | solution.py:719
  119.2 23.0 %collective-permute-start.30 = (bf16[512,512]{1,0:T(8,128)(2,1)}, bf16[512,512]{1,0:T(8,128)(2,1)S(1)}, u32[]{:S(2)}, u32[]{:S(2)}) collective-permute-start(bf16[512,512]{1,0:T(8,128)(2,1)} %collective-permute-done.24.refs_3_), channel_id=1, source_target_pairs={{0,8},{1,17},{2,10},{3,19},{4,12},{5,21},{6,14},{7,23},{8,0},{9,25... | collective-permute-start | bytes 1572872 | tf_op jit(solution)/shard_map/ppermute | solution.py:719
  119.7 15.4 %collective-permute-start.23 = (bf16[4,16,1024]{2,1,0:T(8,128)(2,1)S(1)}, bf16[4,16,1024]{2,1,0:T(8,128)(2,1)S(1)}, u32[]{:S(2)}, u32[]{:S(2)}) collective-permute-start(bf16[4,16,1024]{2,1,0:T(8,128)(2,1)S(1)} %get-tuple-element.143), channel_id=1, source_target_pairs={{0,2},{1,3},{2,0},{3,1},{4,6},{5,7},{6,4},{7,5},{8,10},{9,11},{10,... | collective-permute-start | bytes 393224 | tf_op jit(solution)/shard_map/ppermute | solution.py:719
  123.0 12.5 %collective-permute-start.22 = (bf16[4,16,1024]{2,1,0:T(8,128)(2,1)S(1)}, bf16[4,16,1024]{2,1,0:T(8,128)(2,1)S(1)}, u32[]{:S(2)}, u32[]{:S(2)}) collective-permute-start(bf16[4,16,1024]{2,1,0:T(8,128)(2,1)S(1)} %get-tuple-element.141.refs_1_), channel_id=1, source_target_pairs={{0,6},{1,7},{2,4},{3,5},{4,2},{5,3},{6,0},{7,1},{8,14},{9,15},{10,... | collective-permute-start | bytes 393224 | tf_op jit(solution)/shard_map/ppermute | solution.py:719
  140.2 13.9 %collective-permute-start.28 = (bf16[512,512]{1,0:T(8,128)(2,1)}, bf16[512,512]{1,0:T(8,128)(2,1)S(1)}, u32[]{:S(2)}, u32[]{:S(2)}) collective-permute-start(bf16[512,512]{1,0:T(8,128)(2,1)} %collective-permute-done.24.refs_3_), channel_id=1, source_target_pairs={{0,16},{1,9},{2,18},{3,11},{4,20},{5,13},{6,22},{7,15},{8,24},{9,1... | collective-permute-start | bytes 1572872 | tf_op jit(solution)/shard_map/ppermute | solution.py:719
  142.2 13.3 %collective-permute-start.31 = (bf16[512,512]{1,0:T(8,128)(2,1)S(1)}, bf16[512,512]{1,0:T(8,128)(2,1)S(1)}, u32[]{:S(2)}, u32[]{:S(2)}) collective-permute-start(bf16[512,512]{1,0:T(8,128)(2,1)S(1)} %collective-permute-done.30.refs_6_), channel_id=1, source_target_pairs={{0,16},{1,9},{2,18},{3,11},{4,20},{5,13},{6,22},{7,15},{8,24},{9,1... | collective-permute-start | bytes 1572872 | tf_op jit(solution)/shard_map/ppermute | solution.py:719
  164.0 18.9 %collective-permute-start.36 = (bf16[4,256,512]{2,1,0:T(8,128)(2,1)S(1)}, bf16[4,256,512]{2,1,0:T(8,128)(2,1)S(1)}, u32[]{:S(2)}, u32[]{:S(2)}) collective-permute-start(bf16[4,256,512]{2,1,0:T(8,128)(2,1)S(1)} %get-tuple-element.171), channel_id=1, source_target_pairs={{0,8},{1,17},{2,10},{3,19},{4,12},{5,21},{6,14},{7,23},{8,0},{9,25... | collective-permute-start | bytes 3145736 | tf_op jit(solution)/shard_map/ppermute | solution.py:719
  165.7 17.2 %collective-permute-start.37 = (bf16[256,1024]{1,0:T(8,128)(2,1)S(1)}, bf16[256,1024]{1,0:T(8,128)(2,1)S(1)}, u32[]{:S(2)}, u32[]{:S(2)}) collective-permute-start(bf16[256,1024]{1,0:T(8,128)(2,1)S(1)} %get-tuple-element.172), channel_id=1, source_target_pairs={{0,2},{1,3},{2,4},{3,5},{4,6},{5,7},{6,0},{7,1},{8,10},{9,11},{10,... | collective-permute-start | bytes 1572872 | tf_op jit(solution)/shard_map/ppermute | solution.py:719
  179.7 39.6 %collective-permute-start.40 = (bf16[4,272,512]{2,1,0:T(8,128)(2,1)S(1)}, bf16[4,272,512]{2,1,0:T(8,128)(2,1)S(1)}, u32[]{:S(2)}, u32[]{:S(2)}) collective-permute-start(bf16[4,272,512]{2,1,0:T(8,128)(2,1)S(1)} %get-tuple-element.176), channel_id=1, source_target_pairs={{0,8},{1,17},{2,10},{3,19},{4,12},{5,21},{6,14},{7,23},{8,0},{9,25... | collective-permute-start | bytes 3342344 | tf_op jit(solution)/shard_map/ppermute | solution.py:719
  181.3 15.6 %collective-permute-start.35 = (bf16[256,1024]{1,0:T(8,128)(2,1)S(1)}, bf16[256,1024]{1,0:T(8,128)(2,1)S(1)}, u32[]{:S(2)}, u32[]{:S(2)}) collective-permute-start(bf16[256,1024]{1,0:T(8,128)(2,1)S(1)} %get-tuple-element.168), channel_id=1, source_target_pairs={{0,2},{1,3},{2,4},{3,5},{4,6},{5,7},{6,0},{7,1},{8,10},{9,11},{10,... | collective-permute-start | bytes 1572872 | tf_op jit(solution)/shard_map/ppermute | solution.py:719
  183.2 37.4 %collective-permute-start.39 = (bf16[4,256,512]{2,1,0:T(8,128)(2,1)S(1)}, bf16[4,256,512]{2,1,0:T(8,128)(2,1)S(1)}, u32[]{:S(2)}, u32[]{:S(2)}) collective-permute-start(bf16[4,256,512]{2,1,0:T(8,128)(2,1)S(1)} %shard_map.255.refs_2_), channel_id=1, source_target_pairs={{0,16},{1,9},{2,18},{3,11},{4,20},{5,13},{6,22},{7,15},{8,24},{9,1... | collective-permute-start | bytes 3145736 | tf_op jit(solution)/shard_map/ppermute | solution.py:719
  184.7 41.4 %collective-permute-start.44 = (bf16[4,256,512]{2,1,0:T(8,128)(2,1)S(1)}, bf16[4,256,512]{2,1,0:T(8,128)(2,1)S(1)}, u32[]{:S(2)}, u32[]{:S(2)}) collective-permute-start(bf16[4,256,512]{2,1,0:T(8,128)(2,1)S(1)} %get-tuple-element.183), channel_id=1, source_target_pairs={{0,8},{1,17},{2,10},{3,19},{4,12},{5,21},{6,14},{7,23},{8,0},{9,25... | collective-permute-start | bytes 3145736 | tf_op jit(solution)/shard_map/ppermute | solution.py:719
  197.1 16.7 %collective-permute-start.38 = (bf16[256,1024]{1,0:T(8,128)(2,1)S(1)}, bf16[256,1024]{1,0:T(8,128)(2,1)S(1)}, u32[]{:S(2)}, u32[]{:S(2)}) collective-permute-start(bf16[256,1024]{1,0:T(8,128)(2,1)S(1)} %shard_map.256.refs_2_), channel_id=1, source_target_pairs={{0,2},{1,3},{2,4},{3,5},{4,6},{5,7},{6,0},{7,1},{8,10},{9,11},{10,... | collective-permute-start | bytes 1572872 | tf_op jit(solution)/shard_map/ppermute | solution.py:719
  197.1 28.8 %collective-permute-start.45 = (bf16[256,1024]{1,0:T(8,128)(2,1)S(1)}, bf16[256,1024]{1,0:T(8,128)(2,1)S(1)}, u32[]{:S(2)}, u32[]{:S(2)}) collective-permute-start(bf16[256,1024]{1,0:T(8,128)(2,1)S(1)} %shard_map.254.refs_2_), channel_id=1, source_target_pairs={{0,2},{1,3},{2,4},{3,5},{4,6},{5,7},{6,0},{7,1},{8,10},{9,11},{10,... | collective-permute-start | bytes 1572872 | tf_op jit(solution)/shard_map/ppermute | solution.py:719
  213.8 56.6 %collective-permute-start.51 = (bf16[4,272,512]{2,1,0:T(8,128)(2,1)S(1)}, bf16[4,272,512]{2,1,0:T(8,128)(2,1)S(1)}, u32[]{:S(2)}, u32[]{:S(2)}) collective-permute-start(bf16[4,272,512]{2,1,0:T(8,128)(2,1)S(1)} %get-tuple-element.195), channel_id=1, source_target_pairs={{0,8},{1,17},{2,10},{3,19},{4,12},{5,21},{6,14},{7,23},{8,0},{9,25... | collective-permute-start | bytes 3342344 | tf_op jit(solution)/shard_map/ppermute | solution.py:719
  219.5 50.9 %collective-permute-start.52 = (bf16[4,272,512]{2,1,0:T(8,128)(2,1)S(1)}, bf16[4,272,512]{2,1,0:T(8,128)(2,1)S(1)}, u32[]{:S(2)}, u32[]{:S(2)}) collective-permute-start(bf16[4,272,512]{2,1,0:T(8,128)(2,1)S(1)} %shard_map.259.refs_1_), channel_id=1, source_target_pairs={{0,16},{1,9},{2,18},{3,11},{4,20},{5,13},{6,22},{7,15},{8,24},{9,1... | collective-permute-start | bytes 3342344 | tf_op jit(solution)/shard_map/ppermute | solution.py:719
  220.6 16.7 %collective-permute-start.49 = (bf16[256,1024]{1,0:T(8,128)(2,1)S(1)}, bf16[256,1024]{1,0:T(8,128)(2,1)S(1)}, u32[]{:S(2)}, u32[]{:S(2)}) collective-permute-start(bf16[256,1024]{1,0:T(8,128)(2,1)S(1)} %shard_map.257.refs_10_), channel_id=1, source_target_pairs={{0,2},{1,3},{2,4},{3,5},{4,6},{5,7},{6,0},{7,1},{8,10},{9,11},{10,... | collective-permute-start | bytes 1572872 | tf_op jit(solution)/shard_map/ppermute | solution.py:719
  226.0 22.5 %collective-permute-start.48 = (bf16[256,1024]{1,0:T(8,128)(2,1)S(1)}, bf16[256,1024]{1,0:T(8,128)(2,1)S(1)}, u32[]{:S(2)}, u32[]{:S(2)}) collective-permute-start(bf16[256,1024]{1,0:T(8,128)(2,1)S(1)} %shard_map.263.refs_3_), channel_id=1, source_target_pairs={{0,2},{1,3},{2,4},{3,5},{4,6},{5,7},{6,0},{7,1},{8,10},{9,11},{10,... | collective-permute-start | bytes 1572872 | tf_op jit(solution)/shard_map/ppermute | solution.py:719
  226.1 29.8 %collective-permute-start.47 = (bf16[256,1024]{1,0:T(8,128)(2,1)S(1)}, bf16[256,1024]{1,0:T(8,128)(2,1)S(1)}, u32[]{:S(2)}, u32[]{:S(2)}) collective-permute-start(bf16[256,1024]{1,0:T(8,128)(2,1)S(1)} %get-tuple-element.177.refs_1_), channel_id=1, source_target_pairs={{0,1},{1,0},{2,3},{3,2},{4,5},{5,4},{6,7},{7,6},{8,9},{9,8},{10,11... | collective-permute-start | bytes 1572872 | tf_op jit(solution)/shard_map/ppermute | solution.py:719
  237.3 18.0 %collective-permute-start.46 = (bf16[256,512]{1,0:T(8,128)(2,1)S(1)}, bf16[256,512]{1,0:T(8,128)(2,1)S(1)}, u32[]{:S(2)}, u32[]{:S(2)}) collective-permute-start(bf16[256,512]{1,0:T(8,128)(2,1)S(1)} %get-tuple-element.184), channel_id=1, source_target_pairs={{0,2},{1,3},{2,4},{3,5},{4,6},{5,7},{6,0},{7,1},{8,10},{9,11},{10,... | collective-permute-start | bytes 786440 | tf_op jit(solution)/shard_map/ppermute | solution.py:719
  254.0 32.8 %collective-permute-start.54 = (bf16[2,128,1024]{2,1,0:T(8,128)(2,1)S(1)}, bf16[2,128,1024]{2,1,0:T(8,128)(2,1)S(1)}, u32[]{:S(2)}, u32[]{:S(2)}) collective-permute-start(bf16[2,128,1024]{2,1,0:T(8,128)(2,1)S(1)} %get-tuple-element.191.refs_5_), channel_id=1, source_target_pairs={{0,8},{1,17},{2,10},{3,19},{4,12},{5,21},{6,14},{7,23},{8,0},{9,25... | collective-permute-start | bytes 1572872 | tf_op jit(solution)/shard_map/ppermute | solution.py:719
  255.3 14.3 %collective-permute-start.42 = (bf16[4,16,1024]{2,1,0:T(8,128)(2,1)S(1)}, bf16[4,16,1024]{2,1,0:T(8,128)(2,1)S(1)}, u32[]{:S(2)}, u32[]{:S(2)}) collective-permute-start(bf16[4,16,1024]{2,1,0:T(8,128)(2,1)S(1)} %get-tuple-element.180), channel_id=1, source_target_pairs={{0,4},{1,5},{2,6},{3,7},{4,0},{5,1},{6,2},{7,3},{8,12},{9,13},{10,... | collective-permute-start | bytes 393224 | tf_op jit(solution)/shard_map/ppermute | solution.py:719
  255.9 13.8 %collective-permute-start.43 = (bf16[4,16,1024]{2,1,0:T(8,128)(2,1)S(1)}, bf16[4,16,1024]{2,1,0:T(8,128)(2,1)S(1)}, u32[]{:S(2)}, u32[]{:S(2)}) collective-permute-start(bf16[4,16,1024]{2,1,0:T(8,128)(2,1)S(1)} %get-tuple-element.181.refs_2_), channel_id=1, source_target_pairs={{0,6},{1,7},{2,4},{3,5},{4,2},{5,3},{6,0},{7,1},{8,14},{9,15},{10,... | collective-permute-start | bytes 393224 | tf_op jit(solution)/shard_map/ppermute | solution.py:719
  269.6 17.0 %collective-permute-start.55 = (bf16[256,512]{1,0:T(8,128)(2,1)S(1)}, bf16[256,512]{1,0:T(8,128)(2,1)S(1)}, u32[]{:S(2)}, u32[]{:S(2)}) collective-permute-start(bf16[256,512]{1,0:T(8,128)(2,1)S(1)} %shard_map.267.refs_4_), channel_id=1, source_target_pairs={{0,2},{1,3},{2,4},{3,5},{4,6},{5,7},{6,0},{7,1},{8,10},{9,11},{10,... | collective-permute-start | bytes 786440 | tf_op jit(solution)/shard_map/ppermute | solution.py:719
  270.8 16.2 %collective-permute-start.53 = (bf16[272,512]{1,0:T(8,128)(2,1)S(1)}, bf16[272,512]{1,0:T(8,128)(2,1)S(1)}, u32[]{:S(2)}, u32[]{:S(2)}) collective-permute-start(bf16[272,512]{1,0:T(8,128)(2,1)S(1)} %get-tuple-element.196), channel_id=1, source_target_pairs={{0,2},{1,3},{2,4},{3,5},{4,6},{5,7},{6,0},{7,1},{8,10},{9,11},{10,... | collective-permute-start | bytes 835592 | tf_op jit(solution)/shard_map/ppermute | solution.py:719
  272.8 18.2 %collective-permute-start.50 = (bf16[8,16,1024]{2,1,0:T(8,128)(2,1)S(1)}, bf16[8,16,1024]{2,1,0:T(8,128)(2,1)S(1)}, u32[]{:S(2)}, u32[]{:S(2)}) collective-permute-start(bf16[8,16,1024]{2,1,0:T(8,128)(2,1)S(1)} %get-tuple-element.193.refs_3_), channel_id=1, source_target_pairs={{0,8},{1,17},{2,10},{3,19},{4,12},{5,21},{6,14},{7,23},{8,0},{9,25... | collective-permute-start | bytes 786440 | tf_op jit(solution)/shard_map/ppermute | solution.py:719
  298.2 23.9 %collective-permute-start.73 = (bf16[256,1024]{1,0:T(8,128)(2,1)S(1)}, bf16[256,1024]{1,0:T(8,128)(2,1)S(1)}, u32[]{:S(2)}, u32[]{:S(2)}) collective-permute-start(bf16[256,1024]{1,0:T(8,128)(2,1)S(1)} %shard_map.275.refs_2_.refs_0_), channel_id=1, source_target_pairs={{0,8},{1,17},{2,10},{3,19},{4,12},{5,21},{6,14},{7,23},{8,0},{9,25... | collective-permute-start | bytes 1572872 | tf_op jit(solution)/shard_map/ppermute | solution.py:719
  304.2 14.1 %collective-permute-start.62 = (bf16[8,16,1024]{2,1,0:T(8,128)(2,1)S(1)}, bf16[8,16,1024]{2,1,0:T(8,128)(2,1)S(1)}, u32[]{:S(2)}, u32[]{:S(2)}) collective-permute-start(bf16[8,16,1024]{2,1,0:T(8,128)(2,1)S(1)} %get-tuple-element.208.refs_2_), channel_id=1, source_target_pairs={{0,8},{1,17},{2,10},{3,19},{4,12},{5,21},{6,14},{7,23},{8,0},{9,25... | collective-permute-start | bytes 786440 | tf_op jit(solution)/shard_map/ppermute | solution.py:719
  306.0 24.1 %collective-permute-start.65 = (bf16[256,1024]{1,0:T(8,128)(2,1)S(1)}, bf16[256,1024]{1,0:T(8,128)(2,1)S(1)}, u32[]{:S(2)}, u32[]{:S(2)}) collective-permute-start(bf16[256,1024]{1,0:T(8,128)(2,1)S(1)} %shard_map.275.refs_2_.refs_0_), channel_id=1, source_target_pairs={{0,16},{1,9},{2,18},{3,11},{4,20},{5,13},{6,22},{7,15},{8,24},{9,1... | collective-permute-start | bytes 1572872 | tf_op jit(solution)/shard_map/ppermute | solution.py:719
  322.1 24.9 %collective-permute-start.74 = (bf16[256,1024]{1,0:T(8,128)(2,1)S(1)}, bf16[256,1024]{1,0:T(8,128)(2,1)S(1)}, u32[]{:S(2)}, u32[]{:S(2)}) collective-permute-start(bf16[256,1024]{1,0:T(8,128)(2,1)S(1)} %collective-permute-done.73.refs_1_), channel_id=1, source_target_pairs={{0,16},{1,9},{2,18},{3,11},{4,20},{5,13},{6,22},{7,15},{8,24},{9,1... | collective-permute-start | bytes 1572872 | tf_op jit(solution)/shard_map/ppermute | solution.py:719
  324.2 26.3 %collective-permute-start.71 = (bf16[144,1024]{1,0:T(8,128)(2,1)S(1)}, bf16[144,1024]{1,0:T(8,128)(2,1)S(1)}, u32[]{:S(2)}, u32[]{:S(2)}) collective-permute-start(bf16[144,1024]{1,0:T(8,128)(2,1)S(1)} %shard_map.281.refs_1_.refs_0_), channel_id=1, source_target_pairs={{0,16},{1,9},{2,18},{3,11},{4,20},{5,13},{6,22},{7,15},{8,24},{9,1... | collective-permute-start | bytes 884744 | tf_op jit(solution)/shard_map/ppermute | solution.py:719
  330.1 20.4 %collective-permute-start.72 = (bf16[144,1024]{1,0:T(8,128)(2,1)S(1)}, bf16[144,1024]{1,0:T(8,128)(2,1)S(1)}, u32[]{:S(2)}, u32[]{:S(2)}) collective-permute-start(bf16[144,1024]{1,0:T(8,128)(2,1)S(1)} %collective-permute-done.70.refs_1_), channel_id=1, source_target_pairs={{0,16},{1,9},{2,18},{3,11},{4,20},{5,13},{6,22},{7,15},{8,24},{9,1... | collective-permute-start | bytes 884744 | tf_op jit(solution)/shard_map/ppermute | solution.py:719
  (87 other events, 592.3 us)
